TPU v7x, 512 devices: a whole 4x8x8 slice. The times are simulated.
512 devices in a mesh: band: 16 (over y_hi, z), dom: 32 (over y_lo, x, core).
Axes of the slice: x: 4, y: 8 (y_hi: 2, y_lo: 4; y = y_hi * 4 + y_lo), z: 8, core: 2. Of those that a mesh axis runs over, the one named last changes fastest.
Arguments:
- orbitals: float32 [64, 192, 48, 128], P('band', 'dom'), may hold values from -6 to 6
- occupation: float32 [64], P('band'), may hold values from 0.005 to 0.03
- dielectric: float32 [192, 48, 128], P('dom'), may hold values from 1 to 10
- core_density: float32 [192, 48, 128], P('dom'), may hold values from 0.05 to 0.5
- start_field: float32 [192, 48, 128], P('dom'), may hold values from -6 to 6
Outputs:
- potential: float32 [192, 48, 128], P('dom')
- filtered: float32 [64, 192, 48, 128], P('band', 'dom')
All inputs are finite; a program needn't handle non-finite values.
Results may differ from a plain program's by a relative error of at most 0.00002.
Values sent between devices are 32-bit elements; how exact they have to be, the bound alone decides.
No kernel may reach another device: no remote copies, remote signals or barrier semaphores. Data moves between devices by JAX's collectives and lax.ppermute only.
A program may use at most 64 MiB of HBM per device.

v0:
```python
import jax
import jax.numpy as jnp
from jax import lax
from jax.sharding import PartitionSpec as P

ITERS = 4
DEGREE = 4


coeff_one = 1.5
coeff_two = -0.15
coeff_three = 1.0 / 90.0
coeff_zero = -49.0 / 18.0
center_value = 5.25
half_value = 4.75
slater = -0.9847450218426964


def padded_2(cells, sides, width):
    for axis, dim in sides:
        count = lax.axis_size(axis)
        ends = count - 1
        head = lax.slice_in_dim(cells, 0, width, axis=dim)
        tail = lax.slice_in_dim(cells, cells.shape[dim] - width, cells.shape[dim], axis=dim)
        cells = jnp.concatenate(
            [
                lax.ppermute(tail, axis, [(i, (i + 1) % count) for i in range(ends)]),
                cells,
                lax.ppermute(head, axis, [((i + 1) % count, i) for i in range(ends)]),
            ],
            axis=dim,
        )
    return cells


def laplace(padded):
    size_x = padded.shape[-3] - 6
    size_y = padded.shape[-2] - 6
    size_z = padded.shape[-1] - 6
    core = padded[..., 3 : 3 + size_x, 3 : 3 + size_y, 3 : 3 + size_z]
    total = 3.0 * coeff_zero * core
    for dist, weight in ((1, coeff_one), (2, coeff_two), (3, coeff_three)):
        along = padded[..., 3 + dist : 3 + dist + size_x, 3 : 3 + size_y, 3 : 3 + size_z]
        along = along + padded[..., 3 - dist : 3 - dist + size_x, 3 : 3 + size_y, 3 : 3 + size_z]
        along = along + padded[..., 3 : 3 + size_x, 3 + dist : 3 + dist + size_y, 3 : 3 + size_z]
        along = along + padded[..., 3 : 3 + size_x, 3 - dist : 3 - dist + size_y, 3 : 3 + size_z]
        along = along + padded[..., 3 : 3 + size_x, 3 : 3 + size_y, 3 + dist : 3 + dist + size_z]
        along = along + padded[..., 3 : 3 + size_x, 3 : 3 + size_y, 3 - dist : 3 - dist + size_z]
        total = total + weight * along
    return total


def face_weights(permit, padded):
    weights = (
        0.5 * (permit + padded[2:, 1:-1, 1:-1]),
        0.5 * (permit + padded[:-2, 1:-1, 1:-1]),
        0.5 * (permit + padded[1:-1, 2:, 1:-1]),
        0.5 * (permit + padded[1:-1, :-2, 1:-1]),
        0.5 * (permit + padded[1:-1, 1:-1, 2:]),
        0.5 * (permit + padded[1:-1, 1:-1, :-2]),
    )
    denominator = weights[0] + weights[1] + weights[2] + weights[3] + weights[4] + weights[5]
    return (weights, denominator)


def sweep(padded, weights, denominator, source):
    numerator = weights[0] * padded[2:, 1:-1, 1:-1] + weights[1] * padded[:-2, 1:-1, 1:-1]
    numerator = (
        numerator + weights[2] * padded[1:-1, 2:, 1:-1] + weights[3] * padded[1:-1, :-2, 1:-1]
    )
    numerator = (
        numerator + weights[4] * padded[1:-1, 1:-1, 2:] + weights[5] * padded[1:-1, 1:-1, :-2]
    )
    return (numerator + source) / denominator


def copies_rim(block):
    padded = padded_2(block, (("dom", 0),), 1)
    return jnp.pad(padded, ((0, 0), (1, 1), (1, 1)))


def apply_extended(padded_x, pot):
    padded = jnp.pad(padded_x, ((0, 0), (0, 0), (3, 3), (3, 3)))
    inner = padded_x[:, 3:-3]
    return -0.5 * laplace(padded) + pot[None] * inner


def local(orbitals, occupation, dielectric, core_density, start_field):
    partial_density = jnp.sum(occupation[:, None, None, None] * orbitals * orbitals, axis=0)
    density = lax.psum(partial_density, "band")
    permit_pad = padded_2(dielectric, (("dom", 0),), 1)
    permit_pad = jnp.pad(permit_pad, ((0, 0), (1, 1), (1, 1)))
    weights, denominator = face_weights(dielectric, permit_pad)
    source = 4.0 * density
    field = start_field
    for turn_index in range(ITERS):
        field = sweep(copies_rim(field), weights, denominator, source)
    potential = field + slater * jnp.cbrt(density + core_density)

    def hamil(block):
        padded = padded_2(block, (("dom", 1),), 3)
        return apply_extended(padded, potential)

    before = orbitals
    current = (hamil(orbitals) - center_value * orbitals) / half_value
    for turn_index in range(DEGREE - 1):
        nextone = 2.0 * (hamil(current) - center_value * current) / half_value - before
        before = current
        current = nextone
    return (potential, current)


def solution(mesh):
    return jax.shard_map(
        local,
        mesh=mesh,
        in_specs=(
            P("band", "dom", None, None),
            P("band"),
            P("dom", None, None),
            P("dom", None, None),
            P("dom", None, None),
        ),
        out_specs=(P("dom", None, None), P("band", "dom", None, None)),
        check_vma=False,
    )
```

profile of v0, /device:TPU:7, one launch (start us, length us, event | category | flops | bytes accessed | tf_op | source)
XLA Modules:
  0.0 298.7 jit_solution(7753704916314582418)
XLA Ops:
  7.2 1.9 fusion.148
  9.1 3.7 %collective-permute-start.11 = (f32[4,3,48,128]{3,2,1,0:T(8,128)S(1)}, f32[4,3,48,128]{3,2,1,0:T(8,128)S(1)}, u32[]{:S(2)}, u32[]{:S(2)}) collective-permute-start(f32[4,3,48,128]{3,2,1,0:T(8,128)S(1)} %get-tuple-element.20), channel_id=1, source_target_pairs={{0,1},{1,2},{2,3},{3,4},{4,5},{5,6},{6,7},{7,8},{8,9},{9,10},{10,1... | collective-permute-start | bytes 884744 | tf_op jit(solution)/shard_map/ppermute | solution.py:27
  13.5 1.9 collective-permute-start.3
  15.4 2.4 collective-permute-start.1
  18.6 5.3 %collective-permute-start.2 = (f32[1,48,128]{2,1,0:T(8,128)S(1)}, f32[1,48,128]{2,1,0:T(8,128)S(1)}, u32[]{:S(2)}, u32[]{:S(2)}) collective-permute-start(f32[1,48,128]{2,1,0:T(8,128)S(1)} %get-tuple-element.28), channel_id=1, source_target_pairs={{0,1},{1,2},{2,3},{3,4},{4,5},{5,6},{6,7},{7,8},{8,9},{9,10},{10,1... | collective-permute-start | bytes 73736 | tf_op jit(solution)/shard_map/ppermute | solution.py:27
  23.9 1.9 collective-permute-start
  26.6 1.9 constant_dynamic-update-slice_fusion.1
  28.5 2.6 collective-permute-done
  31.6 174.9 %all-reduce.11.cloned.1.call-done = f32[6,48,128]{2,1,0:T(8,128)} async-done(((f32[6,48,128]{2,1,0:T(8,128)}), f32[6,48,128]{2,1,0:T(8,128)}) %all-reduce.11.cloned.1.call-update) | async-done | bytes 147472 | tf_op jit(solution)/shard_map/psum | solution.py:90
  207.9 9.9 %collective-permute-start.5 = (f32[1,48,128]{2,1,0:T(8,128)S(1)}, f32[1,48,128]{2,1,0:T(8,128)S(1)}, u32[]{:S(2)}, u32[]{:S(2)}) collective-permute-start(f32[1,48,128]{2,1,0:T(8,128)S(1)} %get-tuple-element.26), channel_id=1, source_target_pairs={{0,1},{1,2},{2,3},{3,4},{4,5},{5,6},{6,7},{7,8},{8,9},{9,10},{10,1... | collective-permute-start | bytes 73736 | tf_op jit(solution)/shard_map/ppermute | solution.py:27
  217.8 1.9 collective-permute-start.4
  219.7 3.4 %collective-permute-start.10 = (f32[4,3,48,128]{3,2,1,0:T(8,128)}, f32[4,3,48,128]{3,2,1,0:T(8,128)S(1)}, u32[]{:S(2)}, u32[]{:S(2)}) collective-permute-start(f32[4,3,48,128]{3,2,1,0:T(8,128)} %get-tuple-element.21), channel_id=1, source_target_pairs={{1,0},{2,1},{3,2},{4,3},{5,4},{6,5},{7,6},{8,7},{9,8},{10,9},{11,1... | collective-permute-start | bytes 884744 | tf_op jit(solution)/shard_map/ppermute | solution.py:29
  223.2 1.9 collective-permute-done.4
  225.5 2.4 collective-permute-start.7
  227.9 2.0 collective-permute-start.6
  231.0 4.2 %collective-permute-done.6 = f32[1,48,128]{2,1,0:T(8,128)S(1)} collective-permute-done((f32[1,48,128]{2,1,0:T(8,128)S(1)}, f32[1,48,128]{2,1,0:T(8,128)S(1)}, u32[]{:S(2)}, u32[]{:S(2)}) %collective-permute-start.6) | collective-permute-done | bytes 24608 | tf_op jit(solution)/shard_map/ppermute | solution.py:29
  235.6 1.9 collective-permute-start.9
  237.6 2.4 collective-permute-start.8
  240.0 4.8 %collective-permute-done.8 = f32[1,48,128]{2,1,0:T(8,128)S(1)} collective-permute-done((f32[1,48,128]{2,1,0:T(8,128)S(1)}, f32[1,48,128]{2,1,0:T(8,128)S(1)}, u32[]{:S(2)}, u32[]{:S(2)}) %collective-permute-start.8) | collective-permute-done | bytes 24608 | tf_op jit(solution)/shard_map/ppermute | solution.py:29
  245.4 1.8 broadcast_multiply_fusion
  247.2 1.9 collective-permute-start.12
  249.1 5.8 %collective-permute-start.13 = (f32[4,3,48,128]{3,2,1,0:T(8,128)S(1)}, f32[4,3,48,128]{3,2,1,0:T(8,128)S(1)}, u32[]{:S(2)}, u32[]{:S(2)}) collective-permute-start(f32[4,3,48,128]{3,2,1,0:T(8,128)S(1)} %get-tuple-element.16), channel_id=1, source_target_pairs={{0,1},{1,2},{2,3},{3,4},{4,5},{5,6},{6,7},{7,8},{8,9},{9,10},{10,1... | collective-permute-start | bytes 884744 | tf_op jit(solution)/shard_map/ppermute | solution.py:27
  254.9 2.5 collective-permute-done.12
  259.4 1.9 fusion.65
  261.4 1.9 collective-permute-start.14
  263.3 6.5 %collective-permute-start.15 = (f32[4,3,48,128]{3,2,1,0:T(8,128)S(1)}, f32[4,3,48,128]{3,2,1,0:T(8,128)S(1)}, u32[]{:S(2)}, u32[]{:S(2)}) collective-permute-start(f32[4,3,48,128]{3,2,1,0:T(8,128)S(1)} %get-tuple-element.14), channel_id=1, source_target_pairs={{0,1},{1,2},{2,3},{3,4},{4,5},{5,6},{6,7},{7,8},{8,9},{9,10},{10,1... | collective-permute-start | bytes 884744 | tf_op jit(solution)/shard_map/ppermute | solution.py:27
  269.8 2.5 collective-permute-done.14
  274.3 1.9 fusion.41
  276.3 1.9 collective-permute-start.16
  278.2 6.5 %collective-permute-start.17 = (f32[4,3,48,128]{3,2,1,0:T(8,128)S(1)}, f32[4,3,48,128]{3,2,1,0:T(8,128)S(1)}, u32[]{:S(2)}, u32[]{:S(2)}) collective-permute-start(f32[4,3,48,128]{3,2,1,0:T(8,128)S(1)} %get-tuple-element.12), channel_id=1, source_target_pairs={{0,1},{1,2},{2,3},{3,4},{4,5},{5,6},{6,7},{7,8},{8,9},{9,10},{10,1... | collective-permute-start | bytes 884744 | tf_op jit(solution)/shard_map/ppermute | solution.py:27
  284.7 2.5 collective-permute-done.16
  289.2 2.6 fusion.17
  (52 shorter events, 12.8 us)
Async XLA Ops:
  7.2 24.2 %copy-start.6 = (f32[6,48,128]{2,1,0:T(8,128)S(1)}, f32[6,48,128]{2,1,0:T(8,128)}, u32[]{:S(2)}) copy-start(f32[6,48,128]{2,1,0:T(8,128)} %param.9) | copy-start | bytes 442372
  7.2 24.0 %copy-start.1 = (f32[6,48,128]{2,1,0:T(8,128)S(1)}, f32[6,48,128]{2,1,0:T(8,128)}, u32[]{:S(2)}) copy-start(f32[6,48,128]{2,1,0:T(8,128)} %param.7) | copy-start | bytes 442372
  7.2 199.3 %all-reduce.11.cloned.1.call-start = ((), (), s32[]{:S(2)}) async-start(), calls=%async_computation | async-start | bytes 294912 | tf_op jit(solution)/shard_map/psum | solution.py:90
  9.1 16.7 %collective-permute-start.11 = (f32[4,3,48,128]{3,2,1,0:T(8,128)S(1)}, f32[4,3,48,128]{3,2,1,0:T(8,128)S(1)}, u32[]{:S(2)}, u32[]{:S(2)}) collective-permute-start(f32[4,3,48,128]{3,2,1,0:T(8,128)S(1)} %get-tuple-element.20), channel_id=1, source_target_pairs={{0,1},{1,2},{2,3},{3,4},{4,5},{5,6},{6,7},{7,8},{8,9},{9,10},{10,1... | collective-permute-start | bytes 884744 | tf_op jit(solution)/shard_map/ppermute | solution.py:27
  13.5 17.8 %collective-permute-start.3 = (f32[1,48,128]{2,1,0:T(8,128)S(1)}, f32[1,48,128]{2,1,0:T(8,128)S(1)}, u32[]{:S(2)}, u32[]{:S(2)}) collective-permute-start(f32[1,48,128]{2,1,0:T(8,128)S(1)} %get-tuple-element.30), channel_id=1, source_target_pairs={{0,1},{1,2},{2,3},{3,4},{4,5},{5,6},{6,7},{7,8},{8,9},{9,10},{10,1... | collective-permute-start | bytes 73736 | tf_op jit(solution)/shard_map/ppermute | solution.py:27
  15.4 15.9 %collective-permute-start.1 = (f32[1,48,128]{2,1,0:T(8,128)S(1)}, f32[1,48,128]{2,1,0:T(8,128)S(1)}, u32[]{:S(2)}, u32[]{:S(2)}) collective-permute-start(f32[1,48,128]{2,1,0:T(8,128)S(1)} %get-tuple-element.31), channel_id=1, source_target_pairs={{1,0},{2,1},{3,2},{4,3},{5,4},{6,5},{7,6},{8,7},{9,8},{10,9},{11,1... | collective-permute-start | bytes 73736 | tf_op jit(solution)/shard_map/ppermute | solution.py:29
  18.6 9.9 %collective-permute-start.2 = (f32[1,48,128]{2,1,0:T(8,128)S(1)}, f32[1,48,128]{2,1,0:T(8,128)S(1)}, u32[]{:S(2)}, u32[]{:S(2)}) collective-permute-start(f32[1,48,128]{2,1,0:T(8,128)S(1)} %get-tuple-element.28), channel_id=1, source_target_pairs={{0,1},{1,2},{2,3},{3,4},{4,5},{5,6},{6,7},{7,8},{8,9},{9,10},{10,1... | collective-permute-start | bytes 73736 | tf_op jit(solution)/shard_map/ppermute | solution.py:27
  23.9 7.3 %collective-permute-start = (f32[1,48,128]{2,1,0:T(8,128)S(1)}, f32[1,48,128]{2,1,0:T(8,128)S(1)}, u32[]{:S(2)}, u32[]{:S(2)}) collective-permute-start(f32[1,48,128]{2,1,0:T(8,128)S(1)} %get-tuple-element.29), channel_id=1, source_target_pairs={{1,0},{2,1},{3,2},{4,3},{5,4},{6,5},{7,6},{8,7},{9,8},{10,9},{11,1... | collective-permute-start | bytes 73736 | tf_op jit(solution)/shard_map/ppermute | solution.py:29
  25.8 0.7 copy-start.4
  31.6 198.6 %copy-start = (f32[4,6,48,128]{3,2,1,0:T(8,128)S(1)}, f32[4,6,48,128]{3,2,1,0:T(8,128)}, u32[]{:S(2)}) copy-start(f32[4,6,48,128]{3,2,1,0:T(8,128)} %param.5) | copy-start | bytes 1769476
  206.5 18.8 %copy-start.2 = (f32[6,48,128]{2,1,0:T(8,128)S(1)}, f32[6,48,128]{2,1,0:T(8,128)}, u32[]{:S(2)}) copy-start(f32[6,48,128]{2,1,0:T(8,128)} %all-reduce.11.cloned.1.call-done) | copy-start | bytes 442372
  206.5 23.6 %copy-start.5 = (f32[4,3,48,128]{3,2,1,0:T(8,128)S(1)}, f32[4,3,48,128]{3,2,1,0:T(8,128)}, u32[]{:S(2)}) copy-start(f32[4,3,48,128]{3,2,1,0:T(8,128)} %copy-done.4) | copy-start | bytes 884740
  207.9 15.2 %collective-permute-start.5 = (f32[1,48,128]{2,1,0:T(8,128)S(1)}, f32[1,48,128]{2,1,0:T(8,128)S(1)}, u32[]{:S(2)}, u32[]{:S(2)}) collective-permute-start(f32[1,48,128]{2,1,0:T(8,128)S(1)} %get-tuple-element.26), channel_id=1, source_target_pairs={{0,1},{1,2},{2,3},{3,4},{4,5},{5,6},{6,7},{7,8},{8,9},{9,10},{10,1... | collective-permute-start | bytes 73736 | tf_op jit(solution)/shard_map/ppermute | solution.py:27
  217.8 7.3 %collective-permute-start.4 = (f32[1,48,128]{2,1,0:T(8,128)S(1)}, f32[1,48,128]{2,1,0:T(8,128)S(1)}, u32[]{:S(2)}, u32[]{:S(2)}) collective-permute-start(f32[1,48,128]{2,1,0:T(8,128)S(1)} %get-tuple-element.27), channel_id=1, source_target_pairs={{1,0},{2,1},{3,2},{4,3},{5,4},{6,5},{7,6},{8,7},{9,8},{10,9},{11,1... | collective-permute-start | bytes 73736 | tf_op jit(solution)/shard_map/ppermute | solution.py:29
  219.7 10.4 %collective-permute-start.10 = (f32[4,3,48,128]{3,2,1,0:T(8,128)}, f32[4,3,48,128]{3,2,1,0:T(8,128)S(1)}, u32[]{:S(2)}, u32[]{:S(2)}) collective-permute-start(f32[4,3,48,128]{3,2,1,0:T(8,128)} %get-tuple-element.21), channel_id=1, source_target_pairs={{1,0},{2,1},{3,2},{4,3},{5,4},{6,5},{7,6},{8,7},{9,8},{10,9},{11,1... | collective-permute-start | bytes 884744 | tf_op jit(solution)/shard_map/ppermute | solution.py:29
  225.5 5.4 %collective-permute-start.7 = (f32[1,48,128]{2,1,0:T(8,128)S(1)}, f32[1,48,128]{2,1,0:T(8,128)S(1)}, u32[]{:S(2)}, u32[]{:S(2)}) collective-permute-start(f32[1,48,128]{2,1,0:T(8,128)S(1)} %get-tuple-element.24), channel_id=1, source_target_pairs={{0,1},{1,2},{2,3},{3,4},{4,5},{5,6},{6,7},{7,8},{8,9},{9,10},{10,1... | collective-permute-start | bytes 73736 | tf_op jit(solution)/shard_map/ppermute | solution.py:27
  227.9 7.3 %collective-permute-start.6 = (f32[1,48,128]{2,1,0:T(8,128)S(1)}, f32[1,48,128]{2,1,0:T(8,128)S(1)}, u32[]{:S(2)}, u32[]{:S(2)}) collective-permute-start(f32[1,48,128]{2,1,0:T(8,128)S(1)} %get-tuple-element.25), channel_id=1, source_target_pairs={{1,0},{2,1},{3,2},{4,3},{5,4},{6,5},{7,6},{8,7},{9,8},{10,9},{11,1... | collective-permute-start | bytes 73736 | tf_op jit(solution)/shard_map/ppermute | solution.py:29
  230.9 14.1 %copy-start.7 = (f32[6,48,128]{2,1,0:T(8,128)S(1)}, f32[6,48,128]{2,1,0:T(8,128)}, u32[]{:S(2)}) copy-start(f32[6,48,128]{2,1,0:T(8,128)} %param.8) | copy-start | bytes 442372
  235.6 4.4 %collective-permute-start.9 = (f32[1,48,128]{2,1,0:T(8,128)S(1)}, f32[1,48,128]{2,1,0:T(8,128)S(1)}, u32[]{:S(2)}, u32[]{:S(2)}) collective-permute-start(f32[1,48,128]{2,1,0:T(8,128)S(1)} %get-tuple-element.22), channel_id=1, source_target_pairs={{0,1},{1,2},{2,3},{3,4},{4,5},{5,6},{6,7},{7,8},{8,9},{9,10},{10,1... | collective-permute-start | bytes 73736 | tf_op jit(solution)/shard_map/ppermute | solution.py:27
  237.6 7.3 %collective-permute-start.8 = (f32[1,48,128]{2,1,0:T(8,128)S(1)}, f32[1,48,128]{2,1,0:T(8,128)S(1)}, u32[]{:S(2)}, u32[]{:S(2)}) collective-permute-start(f32[1,48,128]{2,1,0:T(8,128)S(1)} %get-tuple-element.23), channel_id=1, source_target_pairs={{1,0},{2,1},{3,2},{4,3},{5,4},{6,5},{7,6},{8,7},{9,8},{10,9},{11,1... | collective-permute-start | bytes 73736 | tf_op jit(solution)/shard_map/ppermute | solution.py:29
  245.4 43.8 %copy-start.3 = (f32[6,48,128]{2,1,0:T(8,128)}, f32[6,48,128]{2,1,0:T(8,128)S(1)}, u32[]{:S(2)}) copy-start(f32[6,48,128]{2,1,0:T(8,128)S(1)} %get-tuple-element.3) | copy-start | bytes 442372
  247.2 10.2 %collective-permute-start.12 = (f32[4,3,48,128]{3,2,1,0:T(8,128)S(1)}, f32[4,3,48,128]{3,2,1,0:T(8,128)S(1)}, u32[]{:S(2)}, u32[]{:S(2)}) collective-permute-start(f32[4,3,48,128]{3,2,1,0:T(8,128)S(1)} %get-tuple-element.15), channel_id=1, source_target_pairs={{1,0},{2,1},{3,2},{4,3},{5,4},{6,5},{7,6},{8,7},{9,8},{10,9},{11,1... | collective-permute-start | bytes 884744 | tf_op jit(solution)/shard_map/ppermute | solution.py:29
  249.1 9.4 %collective-permute-start.13 = (f32[4,3,48,128]{3,2,1,0:T(8,128)S(1)}, f32[4,3,48,128]{3,2,1,0:T(8,128)S(1)}, u32[]{:S(2)}, u32[]{:S(2)}) collective-permute-start(f32[4,3,48,128]{3,2,1,0:T(8,128)S(1)} %get-tuple-element.16), channel_id=1, source_target_pairs={{0,1},{1,2},{2,3},{3,4},{4,5},{5,6},{6,7},{7,8},{8,9},{9,10},{10,1... | collective-permute-start | bytes 884744 | tf_op jit(solution)/shard_map/ppermute | solution.py:27
  261.4 10.9 %collective-permute-start.14 = (f32[4,3,48,128]{3,2,1,0:T(8,128)S(1)}, f32[4,3,48,128]{3,2,1,0:T(8,128)S(1)}, u32[]{:S(2)}, u32[]{:S(2)}) collective-permute-start(f32[4,3,48,128]{3,2,1,0:T(8,128)S(1)} %get-tuple-element.13), channel_id=1, source_target_pairs={{1,0},{2,1},{3,2},{4,3},{5,4},{6,5},{7,6},{8,7},{9,8},{10,9},{11,1... | collective-permute-start | bytes 884744 | tf_op jit(solution)/shard_map/ppermute | solution.py:29
  263.3 10.2 %collective-permute-start.15 = (f32[4,3,48,128]{3,2,1,0:T(8,128)S(1)}, f32[4,3,48,128]{3,2,1,0:T(8,128)S(1)}, u32[]{:S(2)}, u32[]{:S(2)}) collective-permute-start(f32[4,3,48,128]{3,2,1,0:T(8,128)S(1)} %get-tuple-element.14), channel_id=1, source_target_pairs={{0,1},{1,2},{2,3},{3,4},{4,5},{5,6},{6,7},{7,8},{8,9},{9,10},{10,1... | collective-permute-start | bytes 884744 | tf_op jit(solution)/shard_map/ppermute | solution.py:27
  276.3 10.9 %collective-permute-start.16 = (f32[4,3,48,128]{3,2,1,0:T(8,128)S(1)}, f32[4,3,48,128]{3,2,1,0:T(8,128)S(1)}, u32[]{:S(2)}, u32[]{:S(2)}) collective-permute-start(f32[4,3,48,128]{3,2,1,0:T(8,128)S(1)} %get-tuple-element.11), channel_id=1, source_target_pairs={{1,0},{2,1},{3,2},{4,3},{5,4},{6,5},{7,6},{8,7},{9,8},{10,9},{11,1... | collective-permute-start | bytes 884744 | tf_op jit(solution)/shard_map/ppermute | solution.py:29
  278.2 10.2 %collective-permute-start.17 = (f32[4,3,48,128]{3,2,1,0:T(8,128)S(1)}, f32[4,3,48,128]{3,2,1,0:T(8,128)S(1)}, u32[]{:S(2)}, u32[]{:S(2)}) collective-permute-start(f32[4,3,48,128]{3,2,1,0:T(8,128)S(1)} %get-tuple-element.12), channel_id=1, source_target_pairs={{0,1},{1,2},{2,3},{3,4},{4,5},{5,6},{6,7},{7,8},{8,9},{9,10},{10,1... | collective-permute-start | bytes 884744 | tf_op jit(solution)/shard_map/ppermute | solution.py:27
Sparse Core Ops, SparseCore 0:
  28.6 177.8 all-reduce.10
where the time goes:
time: 302 us; the launch traced here: 299 us
  waiting for transfers between devices  200 us (66%)
  starting transfers between devices  63.6 us (21%)
  other arithmetic  16.7 us (6%)
  between operations  14.5 us (5%)
  local copies, waits for them, and re-layouts  4.32 us (1%)
    psum x1, waiting for transfers between devices, local(): density = lax.psum(partial_density, 'band')  175 us
    ppermute x9, starting transfers between devices, padded_2(): lax.ppermute(tail, axis, [(i, (i + 1) % count) for i in range(ends)])  43.8 us
    ppermute x9, waiting for transfers between devices, padded_2(): lax.ppermute(head, axis, [((i + 1) % count, i) for i in range(ends)])  21.1 us
    ppermute x9, starting transfers between devices, padded_2(): lax.ppermute(head, axis, [((i + 1) % count, i) for i in range(ends)])  19.8 us
    sub x3, other arithmetic, local(): 2.0 * (hamil(current) - center_value * current) / half_value - before  6.52 us
  transfers between devices with their start and end apart: 19, of which 12 were waited for; matrix products, arithmetic and copies ran while one was open for 2% of the time, Pallas kernels for 0%

commit v1 on v0

v1 whole, which is shorter than its diff:
```python
import jax
import jax.numpy as jnp
from jax import lax
from jax.experimental import pallas as pl
from jax.experimental.pallas import tpu as pltpu
from jax.sharding import PartitionSpec as P

NB = 4
BX = 6
NY = 48
NZ = 128
ROWS = BX * NY
TOP = 8
PADY = NY + 2 * TOP

COEFFS = (1.5, -0.15, 1.0 / 90.0)
COEFF_ZERO = -49.0 / 18.0
CENTER = 5.25
HALF = 4.75
SLATER = -0.9847450218426964
SCALE = -0.5 / HALF

VMEM_LIMIT = 48 * 1024 * 1024
ANY = pl.BlockSpec(memory_space=pl.ANY)
VM = pl.BlockSpec(memory_space=pltpu.VMEM)
SM = pl.BlockSpec(memory_space=pltpu.SMEM)
MID = pl.ds(TOP, NY)


def call(kernel, outs, in_specs, out_specs, scratch, args, flops):
    return pl.pallas_call(
        kernel,
        out_shape=[jax.ShapeDtypeStruct(s, jnp.float32) for s in outs],
        in_specs=in_specs,
        out_specs=out_specs,
        scratch_shapes=scratch,
        compiler_params=pltpu.CompilerParams(vmem_limit_bytes=VMEM_LIMIT),
        cost_estimate=pl.CostEstimate(flops=flops, bytes_accessed=2_000_000, transcendentals=0),
    )(*args)


def pack_kernel(chunks, occ, orb, diel, core, field, parts, packed, u, dens, sems):
    size = ROWS // chunks
    load = pltpu.make_async_copy(orb, u, sems.at[0])
    load.start()
    out = [
        pltpu.make_async_copy(orb, packed.at[pl.ds(0, NB)], sems.at[1]),
        pltpu.make_async_copy(field, packed.at[NB], sems.at[2]),
        pltpu.make_async_copy(diel, packed.at[NB + 1], sems.at[3]),
        pltpu.make_async_copy(core, packed.at[NB + 2], sems.at[4]),
    ]
    for c in out:
        c.start()
    load.wait()

    def plane(p, _):
        total = occ[0] * u[0, p] * u[0, p]
        for o in range(1, NB):
            total = total + occ[o] * u[o, p] * u[o, p]
        dens[pl.ds(pl.multiple_of(p * NY, NY), NY), :] = total
        return 0

    lax.fori_loop(0, BX, plane, 0)
    for c in range(chunks):
        parts[c] = dens[pl.ds(c * size, size), :]
    for c in out:
        c.wait()


def pack(chunks, occ, orb, diel, core, field):
    def kernel(*refs):
        pack_kernel(chunks, *refs)

    return call(
        kernel,
        [(chunks, ROWS // chunks, NZ), (NB + 3, BX, NY, NZ)],
        [SM, ANY, ANY, ANY, ANY],
        [VM, ANY],
        [
            pltpu.VMEM((NB, BX, NY, NZ), jnp.float32),
            pltpu.VMEM((ROWS, NZ), jnp.float32),
            pltpu.SemaphoreType.DMA((5,)),
        ],
        (occ, orb, diel, core, field),
        500_000,
    )


def join_kernel(chunks, got, left, right, rho, to_right, to_left, sems):
    size = ROWS // chunks
    copies = []
    for at, (src, edge, dst) in enumerate(
        (
            (left, BX - 1, to_right),
            (right, 0, to_left),
        )
    ):
        for k in range(2):
            copies.append(
                pltpu.make_async_copy(
                    src.at[NB + k, edge],
                    dst.at[pl.ds(ROWS + k * NY, NY)],
                    sems.at[2 * at + k],
                )
            )
    for c in copies:
        c.start()
    for c in range(chunks):
        value = got[c]
        for dst in (rho, to_right, to_left):
            dst[pl.ds(c * size, size), :] = value
    for c in copies:
        c.wait()


def join(chunks, got, left, right):
    def kernel(*refs):
        join_kernel(chunks, *refs)

    return call(
        kernel,
        [(ROWS, NZ), (ROWS + 2 * NY, NZ), (ROWS + 2 * NY, NZ)],
        [VM, ANY, ANY],
        [VM, VM, VM],
        [pltpu.SemaphoreType.DMA((4,))],
        (got, left, right),
        100_000,
    )


def lane_shift(value, dist, lane):
    ahead = jnp.where(lane < NZ - dist, pltpu.roll(value, NZ - dist, 1), 0.0)
    behind = jnp.where(lane >= dist, pltpu.roll(value, dist, 1), 0.0)
    return ahead + behind


def stencil(src, o, p, lane, factor):
    mid = src[o, p, MID, :]
    total = None
    for dist, weight in zip((1, 2, 3), COEFFS):
        along = src[o, p + dist, MID, :] + src[o, p - dist, MID, :]
        along = along + (src[o, p, pl.ds(TOP + dist, NY), :] + src[o, p, pl.ds(TOP - dist, NY), :])
        along = along + lane_shift(mid, dist, lane)
        term = (factor * SCALE * weight) * along
        total = term if total is None else total + term
    return total, mid


def zero_rows(ref, lead):
    blank = jnp.zeros((TOP, NZ), jnp.float32)

    def one(i, _):
        at = []
        for size in reversed(lead):
            at.append(lax.rem(i, size))
            i = lax.div(i, size)
        at = tuple(reversed(at))
        ref[(*at, pl.ds(0, TOP), slice(None))] = blank
        ref[(*at, pl.ds(TOP + NY, TOP), slice(None))] = blank
        return 0

    count = 1
    for size in lead:
        count *= size
    lax.fori_loop(0, count, one, 0)


def first_kernel(
    edges, orb, diel, core, field, rho, left, right, rho_left, rho_right,
    potential, y1_out, y2_out, diag_out,
    u, y1, fa, fb, di, rh, co, wts, sems, big_sems, out_sems,
):
    E = 3 * BX + 2
    orb_copies = [
        pltpu.make_async_copy(left.at[pl.ds(0, NB)], u.at[:, pl.ds(0, BX), MID, :], big_sems.at[0]),
        pltpu.make_async_copy(orb, u.at[:, pl.ds(BX, BX), MID, :], big_sems.at[1]),
        pltpu.make_async_copy(right.at[pl.ds(0, NB)], u.at[:, pl.ds(2 * BX, BX), MID, :], big_sems.at[2]),
    ]
    moves = []
    for k, (dst, own) in enumerate(((fa, field), (di, diel))):
        moves += [
            (left.at[NB + k], dst.at[pl.ds(1, BX), MID, :]),
            (own, dst.at[pl.ds(1 + BX, BX), MID, :]),
            (right.at[NB + k], dst.at[pl.ds(1 + 2 * BX, BX), MID, :]),
            (rho_left.at[BX + k], dst.at[0, MID, :]),
            (rho_right.at[BX + k], dst.at[E - 1, MID, :]),
        ]
    moves += [
        (rho_left.at[pl.ds(0, BX)], rh.at[pl.ds(0, BX)]),
        (rho, rh.at[pl.ds(BX, BX)]),
        (rho_right.at[pl.ds(0, BX)], rh.at[pl.ds(2 * BX, BX)]),
        (left.at[NB + 2, pl.ds(BX - 3, 3)], co.at[pl.ds(0, 3)]),
        (core, co.at[pl.ds(3, BX)]),
        (right.at[NB + 2, pl.ds(0, 3)], co.at[pl.ds(3 + BX, 3)]),
    ]
    copies = [pltpu.make_async_copy(s, d, sems.at[i]) for i, (s, d) in enumerate(moves)]
    for c in copies + orb_copies:
        c.start()
    has_left = edges[0] > 0
    has_right = edges[1] > 0
    zero_rows(fa, (E,))
    zero_rows(fb, (E,))
    zero_rows(di, (E,))
    zero_rows(u, (NB, 3 * BX))
    zero_rows(y1, (NB, 2 * BX))
    lane = lax.broadcasted_iota(jnp.int32, (NY, NZ), 1)
    for c in copies:
        c.wait()

    def inside(e):
        return ((e >= 1 + BX) | has_left) & ((e < 1 + 2 * BX) | has_right)

    def weigh(e, _):
        d = di[e, MID, :]
        xp = 0.5 * (d + di[e + 1, MID, :])
        xm = 0.5 * (d + di[e - 1, MID, :])
        yp = 0.5 * (d + di[e, pl.ds(TOP + 1, NY), :])
        ym = 0.5 * (d + di[e, pl.ds(TOP - 1, NY), :])
        last = lane == NZ - 1
        begin = lane == 0
        zp = 0.5 * (d + jnp.where(last, 0.0, pltpu.roll(d, NZ - 1, 1)))
        zm = 0.5 * (d + jnp.where(begin, 0.0, pltpu.roll(d, 1, 1)))
        den = xp + xm + yp + ym + zp + zm
        inverse = jnp.where(inside(e), 1.0 / den, 0.0)
        wts[0, e] = xp * inverse
        wts[1, e] = xm * inverse
        wts[2, e] = yp * inverse
        wts[3, e] = ym * inverse
        wts[4, e] = jnp.where(last, 0.0, zp * inverse)
        wts[5, e] = jnp.where(begin, 0.0, zm * inverse)
        wts[6, e] = 4.0 * rh[e - 1] * inverse
        return 0

    lax.fori_loop(1, E - 1, weigh, 0)

    def swept(src, e):
        mid = src[e, MID, :]
        total = wts[0, e] * src[e + 1, MID, :] + wts[1, e] * src[e - 1, MID, :]
        total = total + (wts[2, e] * src[e, pl.ds(TOP + 1, NY), :] + wts[3, e] * src[e, pl.ds(TOP - 1, NY), :])
        total = total + (wts[4, e] * pltpu.roll(mid, NZ - 1, 1) + wts[5, e] * pltpu.roll(mid, 1, 1))
        return total + wts[6, e]

    def sweep(src, dst, margin):
        def body(e, _):
            dst[e, MID, :] = swept(src, e)
            return 0

        lax.fori_loop(margin, E - margin, body, 0)

    sweep(fa, fb, 1)
    sweep(fb, fa, 2)
    sweep(fa, fb, 3)

    def last_sweep(j, _):
        e = j + 4
        x = rh[e - 1] + co[j]
        x = jnp.where(inside(e), x, 1.0)
        root = jnp.exp(jnp.log(x) * (1.0 / 3.0))
        root = root - (root - x / (root * root)) * (1.0 / 3.0)
        value = swept(fb, e) + SLATER * root
        fa[e, MID, :] = value
        diag_out[j] = (value - CENTER) * (1.0 / HALF) + 3.0 * COEFF_ZERO * SCALE
        return 0

    lax.fori_loop(0, 2 * BX, last_sweep, 0)
    for p in range(BX):
        potential[p] = fa[p + 1 + BX, MID, :]
    for c in orb_copies:
        c.wait()

    def step_one(i, _):
        o = lax.div(i, 2 * BX)
        j = lax.rem(i, 2 * BX)
        rest, mid = stencil(u, o, j + 3, lane, 1.0)
        here = ((j >= 3) | has_left) & ((j < 3 + BX) | has_right)
        y1[o, j, MID, :] = jnp.where(here, diag_out[j] * mid + rest, 0.0)
        return 0

    lax.fori_loop(0, NB * 2 * BX, step_one, 0)
    save = pltpu.make_async_copy(y1.at[:, :, MID, :], y1_out, out_sems.at[0])
    save.start()

    def step_two(i, _):
        o = lax.div(i, BX)
        j = lax.rem(i, BX)
        rest, mid = stencil(y1, o, j + 3, lane, 2.0)
        y2_out[o, j] = 2.0 * diag_out[j + 3] * mid + rest - u[o, j + BX, MID, :]
        return 0

    lax.fori_loop(0, NB * BX, step_two, 0)
    save.wait()


def first(edges, orb, diel, core, field, rho, left, right, rho_left, rho_right):
    E = 3 * BX + 2
    f = jnp.float32
    return call(
        first_kernel,
        [(BX, NY, NZ), (NB, 2 * BX, NY, NZ), (NB, BX, NY, NZ), (2 * BX, NY, NZ)],
        [SM] + [ANY] * 9,
        [VM, ANY, VM, VM],
        [
            pltpu.VMEM((NB, 3 * BX, PADY, NZ), f),
            pltpu.VMEM((NB, 2 * BX, PADY, NZ), f),
            pltpu.VMEM((E, PADY, NZ), f),
            pltpu.VMEM((E, PADY, NZ), f),
            pltpu.VMEM((E, PADY, NZ), f),
            pltpu.VMEM((3 * BX, NY, NZ), f),
            pltpu.VMEM((2 * BX, NY, NZ), f),
            pltpu.VMEM((7, E, NY, NZ), f),
            pltpu.SemaphoreType.DMA((16,)),
            pltpu.SemaphoreType.DMA((3,)),
            pltpu.SemaphoreType.DMA((1,)),
        ],
        (edges, orb, diel, core, field, rho, left, right, rho_left, rho_right),
        20_000_000,
    )


def second_kernel(edges, y1, y2, left, right, diag, out, u, y3, y1_in, sems):
    copies = [
        pltpu.make_async_copy(left, u.at[:, pl.ds(0, BX), MID, :], sems.at[0]),
        pltpu.make_async_copy(y2, u.at[:, pl.ds(BX, BX), MID, :], sems.at[1]),
        pltpu.make_async_copy(right, u.at[:, pl.ds(2 * BX, BX), MID, :], sems.at[2]),
        pltpu.make_async_copy(y1, y1_in, sems.at[3]),
    ]
    for c in copies:
        c.start()
    has_left = edges[0] > 0
    has_right = edges[1] > 0
    zero_rows(u, (NB, 3 * BX))
    zero_rows(y3, (NB, 2 * BX))
    lane = lax.broadcasted_iota(jnp.int32, (NY, NZ), 1)
    for c in copies:
        c.wait()

    def step_three(i, _):
        o = lax.div(i, 2 * BX)
        j = lax.rem(i, 2 * BX)
        rest, mid = stencil(u, o, j + 3, lane, 2.0)
        here = ((j >= 3) | has_left) & ((j < 3 + BX) | has_right)
        y3[o, j, MID, :] = jnp.where(here, 2.0 * diag[j] * mid + rest - y1_in[o, j], 0.0)
        return 0

    lax.fori_loop(0, NB * 2 * BX, step_three, 0)

    def step_four(i, _):
        o = lax.div(i, BX)
        j = lax.rem(i, BX)
        rest, mid = stencil(y3, o, j + 3, lane, 2.0)
        out[o, j] = 2.0 * diag[j + 3] * mid + rest - u[o, j + BX, MID, :]
        return 0

    lax.fori_loop(0, NB * BX, step_four, 0)


def second(edges, y1, y2, left, right, diag):
    f = jnp.float32
    return call(
        second_kernel,
        [(NB, BX, NY, NZ)],
        [SM, ANY, ANY, ANY, ANY, VM],
        [VM],
        [
            pltpu.VMEM((NB, 3 * BX, PADY, NZ), f),
            pltpu.VMEM((NB, 2 * BX, PADY, NZ), f),
            pltpu.VMEM((NB, 2 * BX, NY, NZ), f),
            pltpu.SemaphoreType.DMA((4,)),
        ],
        (edges, y1, y2, left, right, diag),
        15_000_000,
    )[0]


def from_sides(to_right, to_left):
    n = lax.axis_size("dom")
    left = lax.ppermute(to_right, "dom", [(i, i + 1) for i in range(n - 1)])
    right = lax.ppermute(to_left, "dom", [(i + 1, i) for i in range(n - 1)])
    return left, right


def local(orbitals, occupation, dielectric, core_density, start_field):
    bands = lax.axis_size("band")
    dom = lax.axis_index("dom")
    far = bands // 2
    groups = [list(range(far)), list(range(far, bands))]
    edges = jnp.stack([(dom > 0).astype(jnp.int32), (dom < lax.axis_size("dom") - 1).astype(jnp.int32)])

    parts, packed = pack(far, occupation, orbitals, dielectric, core_density, start_field)
    parts = lax.all_to_all(parts, "band", 0, 0, axis_index_groups=groups)
    mine = jnp.sum(parts, axis=0)
    other = lax.ppermute(mine, "band", [(i, (i + far) % bands) for i in range(bands)])
    left, right = from_sides(packed, packed)
    mine = mine + other
    got = lax.all_to_all(
        jnp.broadcast_to(mine[None], (far, *mine.shape)), "band", 0, 0, axis_index_groups=groups
    )
    rho, to_right, to_left = join(far, got, left, right)
    rho_left, rho_right = from_sides(to_right, to_left)
    cells = (-1, NY, NZ)
    potential, y1, y2, diag = first(
        edges, orbitals, dielectric, core_density, start_field, rho.reshape(cells), left, right,
        rho_left.reshape(cells), rho_right.reshape(cells),
    )
    y2_left, y2_right = from_sides(y2, y2)
    return potential, second(edges, y1, y2, y2_left, y2_right, diag)


def solution(mesh):
    return jax.shard_map(
        local,
        mesh=mesh,
        in_specs=(
            P("band", "dom", None, None),
            P("band"),
            P("dom", None, None),
            P("dom", None, None),
            P("dom", None, None),
        ),
        out_specs=(P("dom", None, None), P("band", "dom", None, None)),
        check_vma=False,
    )
```

time: 302 us -> 120 us (0.40)
  the two profiles are of different devices: /device:TPU:7 before, /device:TPU:48 now
where the time goes in v1:
time: 120 us
  Pallas kernels  34.6 us (29%)
  blocking collectives  31.4 us (26%)
  starting transfers between devices  25.2 us (21%)
  waiting for transfers between devices  21.5 us (18%)
  local copies, waits for them, and re-layouts  6.03 us (5%)
    pallas_call x4, Pallas kernels, call(): pl.pallas_call(kernel, out_shape=[jax.ShapeDtypeStruct(s, jnp.float32) fo...  34.6 us
    all_to_all x1, blocking collectives, local(): parts = lax.all_to_all(parts, 'band', 0, 0, axis_index_groups=groups)  19.5 us
    ppermute x3, starting transfers between devices, from_sides(): right = lax.ppermute(to_left, 'dom', [(i + 1, i) for i in range(n - 1)])  16.5 us
    all_to_all x1, blocking collectives, local(): lax.all_to_all(jnp.broadcast_to(mine[None], (far, *mine.shape)), 'band',...  11.8 us
    ppermute x3, waiting for transfers between devices, from_sides(): left = lax.ppermute(to_right, 'dom', [(i, i + 1) for i in range(n - 1)])  7.47 us
    ppermute x3, waiting for transfers between devices, from_sides(): right = lax.ppermute(to_left, 'dom', [(i + 1, i) for i in range(n - 1)])  7.31 us
    ppermute x1, waiting for transfers between devices, local(): lax.ppermute(mine, 'band', [(i, (i + far) % bands) for i in range(bands)])  6.68 us
    unnamed x22, local copies, waits for them, and re-layouts  6.02 us
  transfers between devices with their start and end apart: 7, of which 5 were waited for; matrix products, arithmetic and copies ran while one was open for 0% of the time, Pallas kernels for 0%

profile of v1, /device:TPU:48, one launch (start us, length us, event | category | flops | bytes accessed | tf_op | source)
XLA Modules:
  0.0 119.5 jit_solution(15483708297401435815)
XLA Ops:
  0.6 0.0 copy-start
  0.6 1.1 copy-done
  1.7 0.9 copy-done.2
  2.6 0.9 copy-done.4
  3.5 0.9 copy-done.6
  4.4 0.7 copy-done.10
  5.1 1.7 %shard_map.68 = (f32[8,36,128]{2,1,0:T(8,128)S(1)}, f32[7,6,48,128]{3,2,1,0:T(8,128)}) custom-call(f32[4]{0:T(128)S(1)} %copy-done.10, f32[4,6,48,128]{3,2,1,0:T(8,128)S(1)} %copy-done, f32[6,48,128]{2,1,0:T(8,128)S(1)} %copy-done.2, f32[6,48,128]{2,1,0:T(8,128)S(1)} %copy-done.4, f32[6,48,128]{2,1,0:T(8,128)S(1)} %copy-done.6), custom_call_target="tpu_custom_call" | custom-call | flops 500000 | bytes 2000000 | tf_op jit(solution)/shard_map/pallas_call | solution.py:31
  6.8 4.9 %collective-permute-start.2 = (f32[7,6,48,128]{3,2,1,0:T(8,128)}, f32[7,6,48,128]{3,2,1,0:T(8,128)S(1)}, u32[]{:S(2)}, u32[]{:S(2)}) collective-permute-start(f32[7,6,48,128]{3,2,1,0:T(8,128)} %get-tuple-element.12), channel_id=1, source_target_pairs={{1,0},{2,1},{3,2},{4,3},{5,4},{6,5},{7,6},{8,7},{9,8},{10,9},{11,1... | collective-permute-start | bytes 3096584 | tf_op jit(solution)/shard_map/ppermute | solution.py:378
  11.7 1.9 %collective-permute-start.1 = (f32[7,6,48,128]{3,2,1,0:T(8,128)}, f32[7,6,48,128]{3,2,1,0:T(8,128)S(1)}, u32[]{:S(2)}, u32[]{:S(2)}) collective-permute-start(f32[7,6,48,128]{3,2,1,0:T(8,128)} %get-tuple-element.12), channel_id=1, source_target_pairs={{0,1},{1,2},{2,3},{3,4},{4,5},{5,6},{6,7},{7,8},{8,9},{9,10},{10,1... | collective-permute-start | bytes 3096584 | tf_op jit(solution)/shard_map/ppermute | solution.py:377
  13.6 19.5 %all_to_all.10 = f32[8,36,128]{2,1,0:T(8,128)S(1)} all-to-all(f32[8,36,128]{2,1,0:T(8,128)S(1)} %get-tuple-element.11), channel_id=1, replica_groups={{0,32,64,96,128,160,192,224},{256,288,320,352,384,416,448,480},{1,33,65..., dimensions={0} | all-to-all | bytes 294912 | tf_op jit(solution)/shard_map/all_to_all | solution.py:390
  33.2 2.9 %collective-permute-start = (f32[36,128]{1,0:T(8,128)S(1)}, f32[36,128]{1,0:T(8,128)S(1)}, u32[]{:S(2)}, u32[]{:S(2)}) collective-permute-start(f32[36,128]{1,0:T(8,128)S(1)} %reduce_sum.9), channel_id=1, source_target_pairs={{0,256},{32,288},{64,320},{96,352},{128,384},{160,416},{192,448},{... | collective-permute-start | bytes 55304 | tf_op jit(solution)/shard_map/ppermute | solution.py:392
  36.1 6.7 %collective-permute-done = f32[36,128]{1,0:T(8,128)S(1)} collective-permute-done((f32[36,128]{1,0:T(8,128)S(1)}, f32[36,128]{1,0:T(8,128)S(1)}, u32[]{:S(2)}, u32[]{:S(2)}) %collective-permute-start) | collective-permute-done | bytes 18464 | tf_op jit(solution)/shard_map/ppermute | solution.py:392
  42.8 11.8 %all_to_all.11.refs_0_ = f32[8,36,128]{2,1,0:T(8,128)S(1)} all-to-all(f32[8,36,128]{2,1,0:T(8,128)S(1)} %broadcast_in_dim.2), channel_id=1, replica_groups={{0,32,64,96,128,160,192,224},{256,288,320,352,384,416,448,480},{1,33,65..., dimensions={0} | all-to-all | bytes 294912 | tf_op jit(solution)/shard_map/all_to_all | solution.py:395
  54.7 0.0 collective-permute-done.2.refs_2_.right
  54.7 0.0 collective-permute-done.1.refs_1_.left
  54.7 1.0 shard_map.69
  55.6 0.0 copy-start.8
  55.7 0.7 copy-done.8
  56.3 1.9 %collective-permute-start.3 = (f32[384,128]{1,0:T(8,128)}, f32[384,128]{1,0:T(8,128)S(1)}, u32[]{:S(2)}, u32[]{:S(2)}) collective-permute-start(f32[384,128]{1,0:T(8,128)} %get-tuple-element.14), channel_id=1, source_target_pairs={{0,1},{1,2},{2,3},{3,4},{4,5},{5,6},{6,7},{7,8},{8,9},{9,10},{10,1... | collective-permute-start | bytes 589832 | tf_op jit(solution)/shard_map/ppermute | solution.py:377
  58.2 5.8 %collective-permute-start.4 = (f32[384,128]{1,0:T(8,128)}, f32[384,128]{1,0:T(8,128)S(1)}, u32[]{:S(2)}, u32[]{:S(2)}) collective-permute-start(f32[384,128]{1,0:T(8,128)} %get-tuple-element.15), channel_id=1, source_target_pairs={{1,0},{2,1},{3,2},{4,3},{5,4},{6,5},{7,6},{8,7},{9,8},{10,9},{11,1... | collective-permute-start | bytes 589832 | tf_op jit(solution)/shard_map/ppermute | solution.py:378
  64.0 0.1 add_convert_fusion.edges
  64.1 1.5 %collective-permute-done.3 = f32[384,128]{1,0:T(8,128)S(1)} collective-permute-done((f32[384,128]{1,0:T(8,128)}, f32[384,128]{1,0:T(8,128)S(1)}, u32[]{:S(2)}, u32[]{:S(2)}) %collective-permute-start.3) | collective-permute-done | bytes 196640 | tf_op jit(solution)/shard_map/ppermute | solution.py:377
  65.6 1.9 %collective-permute-done.4 = f32[384,128]{1,0:T(8,128)S(1)} collective-permute-done((f32[384,128]{1,0:T(8,128)}, f32[384,128]{1,0:T(8,128)S(1)}, u32[]{:S(2)}, u32[]{:S(2)}) %collective-permute-start.4) | collective-permute-done | bytes 196640 | tf_op jit(solution)/shard_map/ppermute | solution.py:378
  67.5 0.0 copy-done.1
  67.5 0.0 copy-start.9
  67.5 0.9 copy-done.9
  68.4 20.3 %shard_map.70 = (f32[6,48,128]{2,1,0:T(8,128)}, f32[4,12,48,128]{3,2,1,0:T(8,128)S(1)}, f32[4,6,48,128]{3,2,1,0:T(8,128)S(1)}, f32[12,48,128]{2,1,0:T(8,128)S(1)}) custom-call(s32[2]{0:T(128)S(1)} %add_convert_fusion.edges, f32[4,6,48,128]{3,2,1,0:T(8,128)S(1)} %copy-done.1, f32[6,48,128]{2,1,0:T(8,128)S(1)} %copy-done.3, f32[6,48,128]{2,1,0:T(8,128)S(1)} %copy-done.5, ...), custom_call_target="tpu_custom_call" | custom-call | flops 20000000 | bytes 2000000 | tf_op jit(solution)/shard_map/pallas_call | solution.py:31
  88.7 5.8 %collective-permute-start.6 = (f32[4,6,48,128]{3,2,1,0:T(8,128)S(1)}, f32[4,6,48,128]{3,2,1,0:T(8,128)S(1)}, u32[]{:S(2)}, u32[]{:S(2)}) collective-permute-start(f32[4,6,48,128]{3,2,1,0:T(8,128)S(1)} %get-tuple-element.18.y2), channel_id=1, source_target_pairs={{1,0},{2,1},{3,2},{4,3},{5,4},{6,5},{7,6},{8,7},{9,8},{10,9},{11,1... | collective-permute-start | bytes 1769480 | tf_op jit(solution)/shard_map/ppermute | solution.py:378
  94.6 1.9 %collective-permute-start.5 = (f32[4,6,48,128]{3,2,1,0:T(8,128)S(1)}, f32[4,6,48,128]{3,2,1,0:T(8,128)S(1)}, u32[]{:S(2)}, u32[]{:S(2)}) collective-permute-start(f32[4,6,48,128]{3,2,1,0:T(8,128)S(1)} %get-tuple-element.18.y2), channel_id=1, source_target_pairs={{0,1},{1,2},{2,3},{3,4},{4,5},{5,6},{6,7},{7,8},{8,9},{9,10},{10,1... | collective-permute-start | bytes 1769480 | tf_op jit(solution)/shard_map/ppermute | solution.py:377
  96.5 5.5 %collective-permute-done.6.right = f32[4,6,48,128]{3,2,1,0:T(8,128)S(1)} collective-permute-done((f32[4,6,48,128]{3,2,1,0:T(8,128)S(1)}, f32[4,6,48,128]{3,2,1,0:T(8,128)S(1)}, u32[]{:S(2)}, u32[]{:S(2)}) %collective-permute-start.6) | collective-permute-done | bytes 589856 | tf_op jit(solution)/shard_map/ppermute | solution.py:378
  101.9 5.9 %collective-permute-done.5.left = f32[4,6,48,128]{3,2,1,0:T(8,128)S(1)} collective-permute-done((f32[4,6,48,128]{3,2,1,0:T(8,128)S(1)}, f32[4,6,48,128]{3,2,1,0:T(8,128)S(1)}, u32[]{:S(2)}, u32[]{:S(2)}) %collective-permute-start.5) | collective-permute-done | bytes 589856 | tf_op jit(solution)/shard_map/ppermute | solution.py:377
  107.9 11.7 %shard_map.71 = f32[4,6,48,128]{3,2,1,0:T(8,128)} custom-call(s32[2]{0:T(128)S(1)} %add_convert_fusion.edges, f32[4,12,48,128]{3,2,1,0:T(8,128)S(1)} %get-tuple-element.17.y1, f32[4,6,48,128]{3,2,1,0:T(8,128)S(1)} %get-tuple-element.18.y2, f32[4,6,48,128]{3,2,1,0:T(8,128)S(1)} %collective-permute-done.5.left, ...), custom_call_target="tpu_custom_call" | custom-call | flops 15000000 | bytes 2000000 | tf_op jit(solution)/shard_map/pallas_call | solution.py:31
  (14 shorter events, 0.1 us)
Async XLA Ops:
  0.6 1.1 copy-start
  1.7 0.9 copy-start.2
  2.6 0.9 copy-start.4
  3.5 0.9 copy-start.6
  4.4 0.7 copy-start.10
  6.8 47.9 %collective-permute-start.2 = (f32[7,6,48,128]{3,2,1,0:T(8,128)}, f32[7,6,48,128]{3,2,1,0:T(8,128)S(1)}, u32[]{:S(2)}, u32[]{:S(2)}) collective-permute-start(f32[7,6,48,128]{3,2,1,0:T(8,128)} %get-tuple-element.12), channel_id=1, source_target_pairs={{1,0},{2,1},{3,2},{4,3},{5,4},{6,5},{7,6},{8,7},{9,8},{10,9},{11,1... | collective-permute-start | bytes 3096584 | tf_op jit(solution)/shard_map/ppermute | solution.py:378
  11.7 43.0 %collective-permute-start.1 = (f32[7,6,48,128]{3,2,1,0:T(8,128)}, f32[7,6,48,128]{3,2,1,0:T(8,128)S(1)}, u32[]{:S(2)}, u32[]{:S(2)}) collective-permute-start(f32[7,6,48,128]{3,2,1,0:T(8,128)} %get-tuple-element.12), channel_id=1, source_target_pairs={{0,1},{1,2},{2,3},{3,4},{4,5},{5,6},{6,7},{7,8},{8,9},{9,10},{10,1... | collective-permute-start | bytes 3096584 | tf_op jit(solution)/shard_map/ppermute | solution.py:377
  33.2 9.6 %collective-permute-start = (f32[36,128]{1,0:T(8,128)S(1)}, f32[36,128]{1,0:T(8,128)S(1)}, u32[]{:S(2)}, u32[]{:S(2)}) collective-permute-start(f32[36,128]{1,0:T(8,128)S(1)} %reduce_sum.9), channel_id=1, source_target_pairs={{0,256},{32,288},{64,320},{96,352},{128,384},{160,416},{192,448},{... | collective-permute-start | bytes 55304 | tf_op jit(solution)/shard_map/ppermute | solution.py:392
  54.6 12.8 %copy-start.1 = (f32[4,6,48,128]{3,2,1,0:T(8,128)S(1)}, f32[4,6,48,128]{3,2,1,0:T(8,128)}, u32[]{:S(2)}) copy-start(f32[4,6,48,128]{3,2,1,0:T(8,128)} %orb.1) | copy-start | bytes 1769476
  54.6 12.8 %copy-start.3 = (f32[6,48,128]{2,1,0:T(8,128)S(1)}, f32[6,48,128]{2,1,0:T(8,128)}, u32[]{:S(2)}) copy-start(f32[6,48,128]{2,1,0:T(8,128)} %diel.1) | copy-start | bytes 442372
  54.6 12.8 %copy-start.5 = (f32[6,48,128]{2,1,0:T(8,128)S(1)}, f32[6,48,128]{2,1,0:T(8,128)}, u32[]{:S(2)}) copy-start(f32[6,48,128]{2,1,0:T(8,128)} %core.1) | copy-start | bytes 442372
  54.6 12.8 %copy-start.7 = (f32[6,48,128]{2,1,0:T(8,128)S(1)}, f32[6,48,128]{2,1,0:T(8,128)}, u32[]{:S(2)}) copy-start(f32[6,48,128]{2,1,0:T(8,128)} %field.1) | copy-start | bytes 442372
  55.6 0.7 copy-start.8
  56.3 9.3 %collective-permute-start.3 = (f32[384,128]{1,0:T(8,128)}, f32[384,128]{1,0:T(8,128)S(1)}, u32[]{:S(2)}, u32[]{:S(2)}) collective-permute-start(f32[384,128]{1,0:T(8,128)} %get-tuple-element.14), channel_id=1, source_target_pairs={{0,1},{1,2},{2,3},{3,4},{4,5},{5,6},{6,7},{7,8},{8,9},{9,10},{10,1... | collective-permute-start | bytes 589832 | tf_op jit(solution)/shard_map/ppermute | solution.py:377
  58.2 9.2 %collective-permute-start.4 = (f32[384,128]{1,0:T(8,128)}, f32[384,128]{1,0:T(8,128)S(1)}, u32[]{:S(2)}, u32[]{:S(2)}) collective-permute-start(f32[384,128]{1,0:T(8,128)} %get-tuple-element.15), channel_id=1, source_target_pairs={{1,0},{2,1},{3,2},{4,3},{5,4},{6,5},{7,6},{8,7},{9,8},{10,9},{11,1... | collective-permute-start | bytes 589832 | tf_op jit(solution)/shard_map/ppermute | solution.py:378
  67.5 0.9 copy-start.9
  88.7 13.2 %collective-permute-start.6 = (f32[4,6,48,128]{3,2,1,0:T(8,128)S(1)}, f32[4,6,48,128]{3,2,1,0:T(8,128)S(1)}, u32[]{:S(2)}, u32[]{:S(2)}) collective-permute-start(f32[4,6,48,128]{3,2,1,0:T(8,128)S(1)} %get-tuple-element.18.y2), channel_id=1, source_target_pairs={{1,0},{2,1},{3,2},{4,3},{5,4},{6,5},{7,6},{8,7},{9,8},{10,9},{11,1... | collective-permute-start | bytes 1769480 | tf_op jit(solution)/shard_map/ppermute | solution.py:378
  94.6 13.3 %collective-permute-start.5 = (f32[4,6,48,128]{3,2,1,0:T(8,128)S(1)}, f32[4,6,48,128]{3,2,1,0:T(8,128)S(1)}, u32[]{:S(2)}, u32[]{:S(2)}) collective-permute-start(f32[4,6,48,128]{3,2,1,0:T(8,128)S(1)} %get-tuple-element.18.y2), channel_id=1, source_target_pairs={{0,1},{1,2},{2,3},{3,4},{4,5},{5,6},{6,7},{7,8},{8,9},{9,10},{10,1... | collective-permute-start | bytes 1769480 | tf_op jit(solution)/shard_map/ppermute | solution.py:377

commit v2 on v0

v2 whole, which is shorter than its diff:
```python
import jax
import jax.numpy as jnp
from jax import lax
from jax.experimental import pallas as pl
from jax.experimental.pallas import tpu as pltpu
from jax.sharding import PartitionSpec as P

NB = 4
BX = 6
NY = 48
NZ = 128
ROWS = BX * NY
STRIPS = 8
NV = NY // STRIPS

COEFFS = (1.5, -0.15, 1.0 / 90.0)
COEFF_ZERO = -49.0 / 18.0
CENTER = 5.25
HALF = 4.75
SLATER = -0.9847450218426964
SCALE = -0.5 / HALF

VMEM_LIMIT = 12 * 1024 * 1024
VMEM_ALL = 63 * 1024 * 1024
ANY = pl.BlockSpec(memory_space=pl.ANY)
HBM = pl.BlockSpec(memory_space=pltpu.HBM)
BESIDE_FAR = 20_000_000
BESIDE_NEAR = 80_000_000
VM = pl.BlockSpec(memory_space=pltpu.VMEM)
SM = pl.BlockSpec(memory_space=pltpu.SMEM)


def call(kernel, outs, in_specs, out_specs, scratch, args, moved=2_000_000, vmem=VMEM_LIMIT):
    return pl.pallas_call(
        kernel,
        out_shape=[jax.ShapeDtypeStruct(s, jnp.float32) for s in outs],
        in_specs=in_specs,
        out_specs=out_specs,
        scratch_shapes=scratch,
        compiler_params=pltpu.CompilerParams(vmem_limit_bytes=vmem),
        cost_estimate=pl.CostEstimate(flops=moved * 1000, bytes_accessed=moved, transcendentals=0),
    )(*args)


def density_kernel(chunks, occ_in, orb, parts, occ, u, dens, sems):
    size = ROWS // chunks
    loads = [pltpu.make_async_copy(occ_in, occ, sems.at[0]), pltpu.make_async_copy(orb, u, sems.at[1])]
    for c in loads:
        c.start()
    for c in loads:
        c.wait()

    def plane(p, _):
        total = occ[0] * u[0, p] * u[0, p]
        for o in range(1, NB):
            total = total + occ[o] * u[o, p] * u[o, p]
        dens[pl.ds(pl.multiple_of(p * NY, NY), NY), :] = total
        return 0

    lax.fori_loop(0, BX, plane, 0, unroll=2)
    for c in range(chunks):
        parts[c] = dens[pl.ds(c * size, size), :]


def density(chunks, occ, orb):
    def kernel(*refs):
        density_kernel(chunks, *refs)

    return call(
        kernel,
        [(chunks, ROWS // chunks, NZ)],
        [HBM, HBM],
        [VM],
        [
            pltpu.SMEM((NB,), jnp.float32),
            pltpu.VMEM((NB, BX, NY, NZ), jnp.float32),
            pltpu.VMEM((ROWS, NZ), jnp.float32),
            pltpu.SemaphoreType.DMA((2,)),
        ],
        (occ, orb),
        vmem=VMEM_ALL,
    )[0]


def pack_kernel(orb, field, diel, core, packed, u, sems):
    loads = [
        pltpu.make_async_copy(orb, u.at[pl.ds(0, NB)], sems.at[0]),
        pltpu.make_async_copy(field, u.at[NB], sems.at[1]),
        pltpu.make_async_copy(diel, u.at[NB + 1], sems.at[2]),
        pltpu.make_async_copy(core, u.at[NB + 2], sems.at[3]),
    ]
    for c in loads:
        c.start()
    for c in loads:
        c.wait()
    save = pltpu.make_async_copy(u, packed, sems.at[4])
    save.start()
    save.wait()


def pack(orb, field, diel, core):
    return call(
        pack_kernel,
        [(NB + 3, BX, NY, NZ)],
        [HBM] * 4,
        [HBM],
        [pltpu.VMEM((NB + 3, BX, NY, NZ), jnp.float32), pltpu.SemaphoreType.DMA((5,))],
        (orb, field, diel, core),
        moved=BESIDE_FAR,
        vmem=VMEM_ALL,
    )[0]


def spread_kernel(mine, other, out):
    value = mine[...] + other[...]
    for c in range(out.shape[0]):
        out[c] = value


def spread(chunks, mine, other):
    return call(
        spread_kernel,
        [(chunks, *mine.shape)],
        [VM, VM],
        [VM],
        [],
        (mine, other),
        moved=BESIDE_NEAR,
    )[0]


def join_kernel(chunks, got, left, right, to_right, to_left, sems):
    size = ROWS // chunks
    copies = []
    for at, (src, edge, dst) in enumerate(
        (
            (left, BX - 1, to_right),
            (right, 0, to_left),
        )
    ):
        for k in range(2):
            copies.append(
                pltpu.make_async_copy(
                    src.at[NB + k, edge],
                    dst.at[pl.ds(ROWS + k * NY, NY)],
                    sems.at[2 * at + k],
                )
            )
    for c in copies:
        c.start()
    for c in range(chunks):
        value = got[c]
        for dst in (to_right, to_left):
            dst[pl.ds(c * size, size), :] = value
    for c in copies:
        c.wait()


def join(chunks, got, left, right):
    def kernel(*refs):
        join_kernel(chunks, *refs)

    return call(
        kernel,
        [(ROWS + 2 * NY, NZ), (ROWS + 2 * NY, NZ)],
        [VM, ANY, ANY],
        [VM, VM],
        [pltpu.SemaphoreType.DMA((4,))],
        (got, left, right),
    )


def strips(ref, *at):
    return [ref[(*at, pl.ds(j, STRIPS, stride=NV), slice(None))] for j in range(NV)]


def put_strips(ref, values, *at):
    for j, value in enumerate(values):
        ref[(*at, pl.ds(j, STRIPS, stride=NV), slice(None))] = value


def plain(ref, *at):
    return [ref[(*at, j)] for j in range(NV)]


def put_plain(ref, values, *at):
    for j, value in enumerate(values):
        ref[(*at, j)] = value


class Masks:
    def __init__(self):
        self.lane = lax.broadcasted_iota(jnp.int32, (STRIPS, NZ), 1)
        self.row = lax.broadcasted_iota(jnp.int32, (STRIPS, NZ), 0)


def with_sides(mid, count, m):
    before = [jnp.where(m.row >= 1, pltpu.roll(mid[NV - count + k], 1, 0), 0.0) for k in range(count)]
    after = [jnp.where(m.row < STRIPS - 1, pltpu.roll(mid[k], STRIPS - 1, 0), 0.0) for k in range(count)]
    return before + mid + after


def band_matrix():
    row = lax.broadcasted_iota(jnp.int32, (2 * NZ, NZ), 0)
    apart = jnp.abs(jnp.where(row >= NZ, row - NZ, row) - lax.broadcasted_iota(jnp.int32, (2 * NZ, NZ), 1))
    value = jnp.zeros((2 * NZ, NZ), jnp.float32)
    for dist, weight in zip((1, 2, 3), COEFFS):
        value = jnp.where(apart == dist, float(round(180.0 * weight)), value)
    return value.astype(jnp.bfloat16)


def along_z(x, matrix):
    high = x.astype(jnp.bfloat16)
    low = (x - high.astype(jnp.float32)).astype(jnp.bfloat16)
    return jnp.dot(jnp.concatenate([high, low], axis=1), matrix, preferred_element_type=jnp.float32)


def stencil(get, zs, m, factor):
    mid = get(0)
    wide = with_sides(mid, 3, m)
    totals = [(factor * SCALE / 180.0) * z for z in zs]
    for dist, weight in zip((1, 2, 3), COEFFS):
        up, down = get(dist), get(-dist)
        for j in range(NV):
            along = (up[j] + down[j]) + (wide[3 + j + dist] + wide[3 + j - dist])
            totals[j] = totals[j] + (factor * SCALE * weight) * along
    return totals, mid


def face_sums(d, xp, xm, keep, m):
    wide = with_sides(d, 1, m)
    not_last = m.lane < NZ - 1
    not_begin = m.lane >= 1
    out = []
    for j in range(NV):
        ahead = jnp.where(not_last, pltpu.roll(d[j], NZ - 1, 1), 0.0)
        behind = jnp.where(not_begin, pltpu.roll(d[j], 1, 1), 0.0)
        sums = [d[j] + v for v in (xp[j], xm[j], wide[j + 2], wide[j], ahead, behind)]
        den = ((sums[0] + sums[1]) + (sums[2] + sums[3])) + (sums[4] + sums[5])
        inverse = jnp.where(keep, 1.0 / den, 0.0)
        sums[4] = jnp.where(not_last, sums[4], 0.0)
        sums[5] = jnp.where(not_begin, sums[5], 0.0)
        out.append([s * inverse for s in sums] + [8.0 * inverse])
    return out


def weigh_kernel(edges, diel, field, left, right, wts, fs, ds):
    m = Masks()
    for k, (lo, own, hi) in enumerate(((left.at[NB], field, right.at[NB]), (left.at[NB + 1], diel, right.at[NB + 1]))):
        dst = (fs, ds)[k]

        def move(p, _):
            put_plain(dst, strips(lo, p), p)
            put_plain(dst, strips(own, p), p + BX)
            put_plain(dst, strips(hi, p), p + 2 * BX)
            return 0

        lax.fori_loop(0, BX, move, 0)
    has_left = edges[0] > 0
    has_right = edges[1] > 0

    def weigh(i, _):
        keep = ((i >= BX - 1) | has_left) & ((i < 2 * BX - 1) | has_right)
        got = face_sums(plain(ds, i + 1), plain(ds, i + 2), plain(ds, i), keep, m)
        for j in range(NV):
            for k in range(7):
                wts[k, i, j] = got[j][k]
        return 0

    lax.fori_loop(0, 3 * BX - 2, weigh, 0, unroll=2)


def weigh(edges, diel, field, left, right):
    vec = (NV, STRIPS, NZ)
    return call(
        weigh_kernel,
        [(7, 3 * BX - 2, *vec), (3 * BX, *vec)],
        [SM] + [VM] * 4,
        [VM, VM],
        [pltpu.VMEM((3 * BX, *vec), jnp.float32)],
        (edges, diel, field, left, right),
    )


def first_kernel(
    edges, orb, core, left, right, mine, rho_left, rho_right, wts, fs,
    potential, y1, y2, diag,
    fa, fb, src, xc, zp,
):
    has_left = edges[0] > 0
    has_right = edges[1] > 0
    m = Masks()
    matrix = band_matrix()

    for o in range(NB):
        for ref, lo, count, at in ((left, BX - 3, 3, 0), (orb, 0, BX, 3), (right, 0, 3, 3 + BX)):
            x = ref[o, pl.ds(lo, count)].reshape(count * NY, NZ)
            zp[o, pl.ds(at, count)] = along_z(x, matrix).reshape(count, NY, NZ)

    def sources(ref, lo, hi, base):
        def body(p, _):
            i = p + base
            for j, v in enumerate(strips(ref, p)):
                src[i, j] = wts[6, i, j] * v
            return 0

        lax.fori_loop(lo, hi, body, 0)

    sources(rho_left, 1, BX, -1)
    sources(mine, 0, BX, BX - 1)
    sources(rho_right, 0, BX - 1, 2 * BX - 1)

    def exchange(ref, extra, lo, count, base):
        def body(p, _):
            for j, (a, b) in enumerate(zip(strips(ref, p + lo), strips(extra, p + lo))):
                x = a + b
                x = jnp.where(x > 0.0, x, 1.0)
                root = jnp.exp(jnp.log(x) * (1.0 / 3.0))
                root = root - (root - x / (root * root)) * (1.0 / 3.0)
                xc[p + base, j] = SLATER * root
            return 0

        lax.fori_loop(0, count, body, 0)

    exchange(rho_left, left.at[NB + 2], BX - 3, 3, 0)
    exchange(mine, core, 0, BX, 3)
    exchange(rho_right, right.at[NB + 2], 0, 3, 3 + BX)

    def swept(mid, up, down, w, s):
        wide = with_sides(mid, 1, m)
        out = []
        for j in range(NV):
            total = w(0, j) * up[j] + w(1, j) * down[j]
            total = total + (w(2, j) * wide[j + 2] + w(3, j) * wide[j])
            total = total + (w(4, j) * pltpu.roll(mid[j], NZ - 1, 1) + w(5, j) * pltpu.roll(mid[j], 1, 1))
            out.append(total + s(j))
        return out

    for near, far, rho, sign in ((left, rho_left, rho_left, 1), (right, rho_right, rho_right, -1)):
        p = 0 if sign > 0 else BX - 1
        e = p if sign > 0 else 3 * BX - 1
        inner, outer = strips(near, NB + 1, p + sign), strips(far, BX + 1)
        xp, xm = (inner, outer) if sign > 0 else (outer, inner)
        got = face_sums(strips(near, NB + 1, p), xp, xm, has_left if sign > 0 else has_right, m)
        f_in, f_out = plain(fs, e + sign), strips(far, BX)
        up, down = (f_in, f_out) if sign > 0 else (f_out, f_in)
        dens = strips(rho, p)
        new = swept(plain(fs, e), up, down, lambda k, j: got[j][k], lambda j: got[j][6] * dens[j])
        put_plain(fb, new, e)

    def sweep(ref, dst, margin):
        def body(e, _):
            new = swept(
                plain(ref, e), plain(ref, e + 1), plain(ref, e - 1),
                lambda k, j: wts[k, e - 1, j], lambda j: src[e - 1, j],
            )
            put_plain(dst, new, e)
            return 0

        lax.fori_loop(margin, 3 * BX - margin, body, 0, unroll=4)

    sweep(fs, fb, 1)
    sweep(fb, fa, 1)
    sweep(fa, fb, 2)

    def last_sweep(j, _):
        e = j + 3
        new = swept(
            plain(fb, e), plain(fb, e + 1), plain(fb, e - 1),
            lambda k, i: wts[k, e - 1, i], lambda i: src[e - 1, i] + xc[j, i],
        )
        put_plain(fa, new, e)
        put_plain(diag, [(v - CENTER) * (1.0 / HALF) + 3.0 * COEFF_ZERO * SCALE for v in new], j)
        return 0

    lax.fori_loop(0, 2 * BX, last_sweep, 0, unroll=2)

    def give(p, _):
        put_strips(potential, plain(fa, p + BX), p)
        return 0

    lax.fori_loop(0, BX, give, 0, unroll=2)

    def step_one(o, _):
        def get(p):
            if p < BX:
                return strips(left, o, p)
            return strips(orb, o, p - BX) if p < 2 * BX else strips(right, o, p - 2 * BX)

        for j in range(2 * BX):
            rest, mid = stencil(lambda dist: get(j + 3 + dist), strips(zp, o, j), m, 1.0)
            new = [a * b + c for a, b, c in zip(plain(diag, j), mid, rest)]
            if j < 3:
                new = [jnp.where(has_left, v, 0.0) for v in new]
            if j >= 3 + BX:
                new = [jnp.where(has_right, v, 0.0) for v in new]
            put_plain(y1, new, o, j)
        return 0

    lax.fori_loop(0, NB, step_one, 0)
    for o in range(NB):
        x = y1[o, pl.ds(3, BX)].reshape(BX * NY, NZ)
        zp[o, pl.ds(0, BX)] = along_z(x, matrix).reshape(BX, NY, NZ)

    def step_two(j, _):
        q = plain(diag, j + 3)
        for o in range(NB):
            zs = [zp[o, j, pl.ds(i * STRIPS, STRIPS), :] for i in range(NV)]
            rest, mid = stencil(lambda dist: plain(y1, o, j + 3 + dist), zs, m, 2.0)
            old = strips(orb, o, j)
            put_plain(y2, [2.0 * a * b + (c - d) for a, b, c, d in zip(q, mid, rest, old)], o, j)
        return 0

    lax.fori_loop(0, BX, step_two, 0)


def first(edges, orb, core, left, right, mine, rho_left, rho_right, wts, fs):
    f = jnp.float32
    vec = (NV, STRIPS, NZ)
    return call(
        first_kernel,
        [(BX, NY, NZ), (NB, 2 * BX, *vec), (NB, BX, *vec), (2 * BX, *vec)],
        [SM] + [VM] * 9,
        [VM, VM, VM, VM],
        [
            pltpu.VMEM((3 * BX, *vec), f),
            pltpu.VMEM((3 * BX, *vec), f),
            pltpu.VMEM((3 * BX - 2, *vec), f),
            pltpu.VMEM((2 * BX, *vec), f),
            pltpu.VMEM((NB, 2 * BX, NY, NZ), f),
        ],
        (edges, orb, core, left, right, mine, rho_left, rho_right, wts, fs),
    )


def second_kernel(edges, y1, y2, left, right, diag, out, y3, zp, done, sems):
    has_left = edges[0] > 0
    has_right = edges[1] > 0
    m = Masks()
    matrix = band_matrix()
    for o in range(NB):
        for ref, lo, count, at in ((left, BX - 3, 3, 0), (y2, 0, BX, 3), (right, 0, 3, 3 + BX)):
            x = ref[o, pl.ds(lo, count)].reshape(count * NY, NZ)
            zp[o, pl.ds(at, count)] = along_z(x, matrix).reshape(count, NV, STRIPS, NZ)

    def step_three(o, _):
        def get(p):
            if p < BX:
                return plain(left, o, p)
            return plain(y2, o, p - BX) if p < 2 * BX else plain(right, o, p - 2 * BX)

        for j in range(2 * BX):
            rest, mid = stencil(lambda dist: get(j + 3 + dist), plain(zp, o, j), m, 2.0)
            old = plain(y1, o, j)
            new = [2.0 * a * b + (c - d) for a, b, c, d in zip(plain(diag, j), mid, rest, old)]
            if j < 3:
                new = [jnp.where(has_left, v, 0.0) for v in new]
            if j >= 3 + BX:
                new = [jnp.where(has_right, v, 0.0) for v in new]
            put_plain(y3, new, o, j)
        return 0

    lax.fori_loop(0, NB, step_three, 0)
    for o in range(NB):
        x = y3[o, pl.ds(3, BX)].reshape(BX * NY, NZ)
        zp[o, pl.ds(0, BX)] = along_z(x, matrix).reshape(BX, NV, STRIPS, NZ)

    def step_four(o, _):
        for j in range(BX):
            rest, mid = stencil(lambda dist: plain(y3, o, j + 3 + dist), plain(zp, o, j), m, 2.0)
            old = plain(y2, o, j)
            new = [2.0 * a * b + (c - d) for a, b, c, d in zip(plain(diag, j + 3), mid, rest, old)]
            put_strips(done, new, o, j)
        pltpu.make_async_copy(done.at[o], out.at[o], sems.at[o]).start()
        return 0

    lax.fori_loop(0, NB, step_four, 0)
    for o in range(NB):
        pltpu.make_async_copy(done.at[o], out.at[o], sems.at[o]).wait()


def second(edges, y1, y2, left, right, diag):
    f = jnp.float32
    vec = (NV, STRIPS, NZ)
    return call(
        second_kernel,
        [(NB, BX, NY, NZ)],
        [SM] + [VM] * 5,
        [ANY],
        [
            pltpu.VMEM((NB, 2 * BX, *vec), f),
            pltpu.VMEM((NB, 2 * BX, *vec), f),
            pltpu.VMEM((NB, BX, NY, NZ), f),
            pltpu.SemaphoreType.DMA((NB,)),
        ],
        (edges, y1, y2, left, right, diag),
    )[0]


def from_sides(to_right, to_left):
    n = lax.axis_size("dom")
    left = lax.ppermute(to_right, "dom", [(i, i + 1) for i in range(n - 1)])
    right = lax.ppermute(to_left, "dom", [(i + 1, i) for i in range(n - 1)])
    return left, right


def local(orbitals, occupation, dielectric, core_density, start_field):
    bands = lax.axis_size("band")
    dom = lax.axis_index("dom")
    far = bands // 2
    groups = [list(range(far)), list(range(far, bands))]
    edges = jnp.stack([(dom > 0).astype(jnp.int32), (dom < lax.axis_size("dom") - 1).astype(jnp.int32)])

    parts = density(far, occupation, orbitals)
    parts = lax.all_to_all(parts, "band", 0, 0, axis_index_groups=groups)
    mine = jnp.sum(parts, axis=0)
    other = lax.ppermute(mine, "band", [(i, (i + far) % bands) for i in range(bands)])
    held, mine = lax.optimization_barrier(((orbitals, start_field, dielectric, core_density), mine))
    packed = pack(*held)
    left, right = from_sides(packed, packed)
    got = lax.all_to_all(spread(far, mine, other), "band", 0, 0, axis_index_groups=groups)
    to_right, to_left = join(far, got, left, right)
    rho_left, rho_right = from_sides(to_right, to_left)
    (left, right), to_right = lax.optimization_barrier(((left, right), to_right))
    wts, fs = weigh(edges, dielectric, start_field, left, right)
    cells = (-1, NY, NZ)
    potential, y1, y2, diag = first(
        edges, orbitals, core_density, left, right,
        to_right.reshape(cells), rho_left.reshape(cells), rho_right.reshape(cells), wts, fs,
    )
    y2_left, y2_right = from_sides(y2, y2)
    return potential, second(edges, y1, y2, y2_left, y2_right, diag)


def solution(mesh):
    return jax.shard_map(
        local,
        mesh=mesh,
        in_specs=(
            P("band", "dom", None, None),
            P("band"),
            P("dom", None, None),
            P("dom", None, None),
            P("dom", None, None),
        ),
        out_specs=(P("dom", None, None), P("band", "dom", None, None)),
        check_vma=False,
    )
```

time: 302 us -> 90.9 us (0.30)
  the two profiles are of different devices: /device:TPU:7 before, /device:TPU:8 now
where the time goes in v2:
time: 90.9 us; the launch traced here: 90.4 us
  waiting for transfers between devices  28.7 us (32%)
  starting transfers between devices  24.8 us (27%)
  blocking collectives  20.1 us (22%)
  Pallas kernels  16 us (18%)
    all_to_all x1, blocking collectives, local(): parts = lax.all_to_all(parts, 'band', 0, 0, axis_index_groups=groups)  20.1 us
    pallas_call x7, Pallas kernels, call(): pl.pallas_call(kernel, out_shape=[jax.ShapeDtypeStruct(s, jnp.float32) fo...  16 us
    ppermute x3, waiting for transfers between devices, from_sides(): left = lax.ppermute(to_right, 'dom', [(i, i + 1) for i in range(n - 1)])  12.8 us
    all_to_all x1, waiting for transfers between devices, local(): lax.all_to_all(spread(far, mine, other), 'band', 0, 0, axis_index_groups=...  10.9 us
    ppermute x3, starting transfers between devices, from_sides(): right = lax.ppermute(to_left, 'dom', [(i + 1, i) for i in range(n - 1)])  8.35 us
    ppermute x1, starting transfers between devices, local(): lax.ppermute(mine, 'band', [(i, (i + far) % bands) for i in range(bands)])  6.83 us
    ppermute x3, starting transfers between devices, from_sides(): left = lax.ppermute(to_right, 'dom', [(i, i + 1) for i in range(n - 1)])  6.25 us
    ppermute x3, waiting for transfers between devices, from_sides(): right = lax.ppermute(to_left, 'dom', [(i + 1, i) for i in range(n - 1)])  4.97 us
  transfers between devices with their start and end apart: 8, of which 5 were waited for; matrix products, arithmetic and copies ran while one was open for 0% of the time, Pallas kernels for 5%

profile of v2, /device:TPU:8, one launch (start us, length us, event | category | flops | bytes accessed | tf_op | source)
XLA Modules:
  0.0 90.4 jit_solution(11008740680655335815)
XLA Ops:
  0.6 1.8 %shard_map.68 = f32[8,36,128]{2,1,0:T(8,128)} custom-call(f32[4]{0:T(128)} %refs_0_.1, f32[4,6,48,128]{3,2,1,0:T(8,128)} %orb.2), custom_call_target="tpu_custom_call" | custom-call | flops 2000000000 | bytes 2000000 | tf_op jit(solution)/shard_map/pallas_call | solution.py:34
  2.5 20.1 %all_to_all.10 = f32[8,36,128]{2,1,0:T(8,128)S(1)} all-to-all(f32[8,36,128]{2,1,0:T(8,128)} %shard_map.68), channel_id=1, replica_groups={{0,32,64,96,128,160,192,224},{256,288,320,352,384,416,448,480},{1,33,65..., dimensions={0} | all-to-all | bytes 294912 | tf_op jit(solution)/shard_map/all_to_all | solution.py:515
  22.6 6.8 %collective-permute-start.2 = (f32[36,128]{1,0:T(8,128)S(1)}, f32[36,128]{1,0:T(8,128)S(1)}, u32[]{:S(2)}, u32[]{:S(2)}) collective-permute-start(f32[36,128]{1,0:T(8,128)S(1)} %reduce_sum.9.mine), channel_id=1, source_target_pairs={{0,256},{32,288},{64,320},{96,352},{128,384},{160,416},{192,448},{... | collective-permute-start | bytes 55304 | tf_op jit(solution)/shard_map/ppermute | solution.py:517
  29.4 2.2 %shard_map.69 = f32[7,6,48,128]{3,2,1,0:T(8,128)} custom-call(f32[4,6,48,128]{3,2,1,0:T(8,128)} %orb.2, f32[6,48,128]{2,1,0:T(8,128)} %field.2, f32[6,48,128]{2,1,0:T(8,128)} %diel.2, f32[6,48,128]{2,1,0:T(8,128)} %core.2), custom_call_target="tpu_custom_call" | custom-call | flops 20000000000 | bytes 20000000 | tf_op jit(solution)/shard_map/pallas_call | solution.py:34
  31.6 2.7 %collective-permute-start.1 = (f32[7,6,48,128]{3,2,1,0:T(8,128)}, f32[7,6,48,128]{3,2,1,0:T(8,128)S(1)}, u32[]{:S(2)}, u32[]{:S(2)}) collective-permute-start(f32[7,6,48,128]{3,2,1,0:T(8,128)} %shard_map.69), channel_id=1, source_target_pairs={{1,0},{2,1},{3,2},{4,3},{5,4},{6,5},{7,6},{8,7},{9,8},{10,9},{11,1... | collective-permute-start | bytes 3096584 | tf_op jit(solution)/shard_map/ppermute | solution.py:503
  34.3 1.9 %collective-permute-start = (f32[7,6,48,128]{3,2,1,0:T(8,128)}, f32[7,6,48,128]{3,2,1,0:T(8,128)S(1)}, u32[]{:S(2)}, u32[]{:S(2)}) collective-permute-start(f32[7,6,48,128]{3,2,1,0:T(8,128)} %shard_map.69), channel_id=1, source_target_pairs={{0,1},{1,2},{2,3},{3,4},{4,5},{5,6},{6,7},{7,8},{8,9},{9,10},{10,1... | collective-permute-start | bytes 3096584 | tf_op jit(solution)/shard_map/ppermute | solution.py:502
  36.3 0.0 collective-permute-done.2.other
  36.3 0.7 shard_map.70
  37.0 3.4 %all-to-all-start.1 = ((f32[8,36,128]{2,1,0:T(8,128)}), f32[8,36,128]{2,1,0:T(8,128)S(1)}, u32[]{:S(2)}, u32[]{:S(2)}) async-start(f32[8,36,128]{2,1,0:T(8,128)} %shard_map.70), calls=%async_computation.1 | async-start | bytes 327680 | tf_op jit(solution)/shard_map/all_to_all | solution.py:521
  40.4 0.0 copy-start.1
  40.4 0.0 copy-start.2
  40.4 10.9 %all-to-all-done.1.refs_0_ = f32[8,36,128]{2,1,0:T(8,128)S(1)} async-done(((f32[8,36,128]{2,1,0:T(8,128)}), f32[8,36,128]{2,1,0:T(8,128)S(1)}, u32[]{:S(2)}, u32[]{:S(2)}) %all-to-all-start.1) | async-done | bytes 147488 | tf_op jit(solution)/shard_map/all_to_all | solution.py:521
  51.3 0.0 collective-permute-done.1.refs_2_.right
  51.3 1.3 %collective-permute-done.refs_1_.left = f32[7,6,48,128]{3,2,1,0:T(8,128)S(1)} collective-permute-done((f32[7,6,48,128]{3,2,1,0:T(8,128)}, f32[7,6,48,128]{3,2,1,0:T(8,128)S(1)}, u32[]{:S(2)}, u32[]{:S(2)}) %collective-permute-start) | collective-permute-done | bytes 1032224 | tf_op jit(solution)/shard_map/ppermute | solution.py:502
  52.6 0.2 shard_map.71
  52.8 3.7 %collective-permute-start.4 = (f32[384,128]{1,0:T(8,128)S(1)}, f32[384,128]{1,0:T(8,128)S(1)}, u32[]{:S(2)}, u32[]{:S(2)}) collective-permute-start(f32[384,128]{1,0:T(8,128)S(1)} %get-tuple-element.27), channel_id=1, source_target_pairs={{1,0},{2,1},{3,2},{4,3},{5,4},{6,5},{7,6},{8,7},{9,8},{10,9},{11,1... | collective-permute-start | bytes 589832 | tf_op jit(solution)/shard_map/ppermute | solution.py:503
  56.5 1.9 %collective-permute-start.3 = (f32[384,128]{1,0:T(8,128)S(1)}, f32[384,128]{1,0:T(8,128)S(1)}, u32[]{:S(2)}, u32[]{:S(2)}) collective-permute-start(f32[384,128]{1,0:T(8,128)S(1)} %get-tuple-element.26), channel_id=1, source_target_pairs={{0,1},{1,2},{2,3},{3,4},{4,5},{5,6},{6,7},{7,8},{8,9},{9,10},{10,1... | collective-permute-start | bytes 589832 | tf_op jit(solution)/shard_map/ppermute | solution.py:502
  58.4 0.1 add_convert_fusion.edges
  58.5 0.0 copy-done.1
  58.5 0.0 copy-done.2
  58.5 0.0 copy-start
  58.5 1.5 %shard_map.72 = (f32[7,16,6,8,128]{4,3,2,1,0:T(8,128)S(1)}, f32[18,6,8,128]{3,2,1,0:T(8,128)S(1)}) custom-call(s32[2]{0:T(128)S(1)} %add_convert_fusion.edges, f32[6,48,128]{2,1,0:T(8,128)S(1)} %copy-done.2, f32[6,48,128]{2,1,0:T(8,128)S(1)} %copy-done.1, f32[7,6,48,128]{3,2,1,0:T(8,128)S(1)} %collective-permute-done.refs_1_.left, ...), custom_call_target="tpu_custom_call" | custom-call | flops 2000000000 | bytes 2000000 | tf_op jit(solution)/shard_map/pallas_call | solution.py:34
  60.1 0.0 collective-permute-done.4
  60.1 5.5 %collective-permute-done.3 = f32[384,128]{1,0:T(8,128)S(1)} collective-permute-done((f32[384,128]{1,0:T(8,128)S(1)}, f32[384,128]{1,0:T(8,128)S(1)}, u32[]{:S(2)}, u32[]{:S(2)}) %collective-permute-start.3) | collective-permute-done | bytes 196640 | tf_op jit(solution)/shard_map/ppermute | solution.py:502
  65.6 0.0 copy-done
  65.6 0.0 copy-done.3
  65.6 6.1 %shard_map.73 = (f32[6,48,128]{2,1,0:T(8,128)}, f32[4,12,6,8,128]{4,3,2,1,0:T(8,128)S(1)}, f32[4,6,6,8,128]{4,3,2,1,0:T(8,128)S(1)}, f32[12,6,8,128]{3,2,1,0:T(8,128)S(1)}) custom-call(s32[2]{0:T(128)S(1)} %add_convert_fusion.edges, f32[4,6,48,128]{3,2,1,0:T(8,128)S(1)} %copy-done, f32[6,48,128]{2,1,0:T(8,128)S(1)} %copy-done.3, ...), custom_call_target="tpu_custom_call" | custom-call | flops 2000000000 | bytes 2000000 | tf_op jit(solution)/shard_map/pallas_call | solution.py:34
  71.7 1.9 %collective-permute-start.6 = (f32[4,6,6,8,128]{4,3,2,1,0:T(8,128)S(1)}, f32[4,6,6,8,128]{4,3,2,1,0:T(8,128)S(1)}, u32[]{:S(2)}, u32[]{:S(2)}) collective-permute-start(f32[4,6,6,8,128]{4,3,2,1,0:T(8,128)S(1)} %get-tuple-element.32.y2), channel_id=1, source_target_pairs={{1,0},{2,1},{3,2},{4,3},{5,4},{6,5},{7,6},{8,7},{9,8},{10,9},{11,1... | collective-permute-start | bytes 1769480 | tf_op jit(solution)/shard_map/ppermute | solution.py:503
  73.6 2.4 %collective-permute-start.5 = (f32[4,6,6,8,128]{4,3,2,1,0:T(8,128)S(1)}, f32[4,6,6,8,128]{4,3,2,1,0:T(8,128)S(1)}, u32[]{:S(2)}, u32[]{:S(2)}) collective-permute-start(f32[4,6,6,8,128]{4,3,2,1,0:T(8,128)S(1)} %get-tuple-element.32.y2), channel_id=1, source_target_pairs={{0,1},{1,2},{2,3},{3,4},{4,5},{5,6},{6,7},{7,8},{8,9},{9,10},{10,1... | collective-permute-start | bytes 1769480 | tf_op jit(solution)/shard_map/ppermute | solution.py:502
  76.1 5.0 %collective-permute-done.6.right = f32[4,6,6,8,128]{4,3,2,1,0:T(8,128)S(1)} collective-permute-done((f32[4,6,6,8,128]{4,3,2,1,0:T(8,128)S(1)}, f32[4,6,6,8,128]{4,3,2,1,0:T(8,128)S(1)}, u32[]{:S(2)}, u32[]{:S(2)}) %collective-permute-start.6) | collective-permute-done | bytes 589856 | tf_op jit(solution)/shard_map/ppermute | solution.py:503
  81.0 5.9 %collective-permute-done.5.left = f32[4,6,6,8,128]{4,3,2,1,0:T(8,128)S(1)} collective-permute-done((f32[4,6,6,8,128]{4,3,2,1,0:T(8,128)S(1)}, f32[4,6,6,8,128]{4,3,2,1,0:T(8,128)S(1)}, u32[]{:S(2)}, u32[]{:S(2)}) %collective-permute-start.5) | collective-permute-done | bytes 589856 | tf_op jit(solution)/shard_map/ppermute | solution.py:502
  87.0 3.5 %shard_map.74 = f32[4,6,48,128]{3,2,1,0:T(8,128)} custom-call(s32[2]{0:T(128)S(1)} %add_convert_fusion.edges, f32[4,12,6,8,128]{4,3,2,1,0:T(8,128)S(1)} %get-tuple-element.31.y1, f32[4,6,6,8,128]{4,3,2,1,0:T(8,128)S(1)} %get-tuple-element.32.y2, f32[4,6,6,8,128]{4,3,2,1,0:T(8,128)S(1)} %collective-permute-done.5.left, ...), custom_call_target="tpu_custom_call" | custom-call | flops 2000000000 | bytes 2000000 | tf_op jit(solution)/shard_map/pallas_call | solution.py:34
  (2 shorter events, 0.0 us)
Async XLA Ops:
  22.6 13.7 %collective-permute-start.2 = (f32[36,128]{1,0:T(8,128)S(1)}, f32[36,128]{1,0:T(8,128)S(1)}, u32[]{:S(2)}, u32[]{:S(2)}) collective-permute-start(f32[36,128]{1,0:T(8,128)S(1)} %reduce_sum.9.mine), channel_id=1, source_target_pairs={{0,256},{32,288},{64,320},{96,352},{128,384},{160,416},{192,448},{... | collective-permute-start | bytes 55304 | tf_op jit(solution)/shard_map/ppermute | solution.py:517
  31.6 19.7 %collective-permute-start.1 = (f32[7,6,48,128]{3,2,1,0:T(8,128)}, f32[7,6,48,128]{3,2,1,0:T(8,128)S(1)}, u32[]{:S(2)}, u32[]{:S(2)}) collective-permute-start(f32[7,6,48,128]{3,2,1,0:T(8,128)} %shard_map.69), channel_id=1, source_target_pairs={{1,0},{2,1},{3,2},{4,3},{5,4},{6,5},{7,6},{8,7},{9,8},{10,9},{11,1... | collective-permute-start | bytes 3096584 | tf_op jit(solution)/shard_map/ppermute | solution.py:503
  34.3 18.3 %collective-permute-start = (f32[7,6,48,128]{3,2,1,0:T(8,128)}, f32[7,6,48,128]{3,2,1,0:T(8,128)S(1)}, u32[]{:S(2)}, u32[]{:S(2)}) collective-permute-start(f32[7,6,48,128]{3,2,1,0:T(8,128)} %shard_map.69), channel_id=1, source_target_pairs={{0,1},{1,2},{2,3},{3,4},{4,5},{5,6},{6,7},{7,8},{8,9},{9,10},{10,1... | collective-permute-start | bytes 3096584 | tf_op jit(solution)/shard_map/ppermute | solution.py:502
  37.0 14.3 %all-to-all-start.1 = ((f32[8,36,128]{2,1,0:T(8,128)}), f32[8,36,128]{2,1,0:T(8,128)S(1)}, u32[]{:S(2)}, u32[]{:S(2)}) async-start(f32[8,36,128]{2,1,0:T(8,128)} %shard_map.70), calls=%async_computation.1 | async-start | bytes 327680 | tf_op jit(solution)/shard_map/all_to_all | solution.py:521
  40.4 18.2 %copy-start.1 = (f32[6,48,128]{2,1,0:T(8,128)S(1)}, f32[6,48,128]{2,1,0:T(8,128)}, u32[]{:S(2)}) copy-start(f32[6,48,128]{2,1,0:T(8,128)} %field.2) | copy-start | bytes 442372
  40.4 18.2 %copy-start.2 = (f32[6,48,128]{2,1,0:T(8,128)S(1)}, f32[6,48,128]{2,1,0:T(8,128)}, u32[]{:S(2)}) copy-start(f32[6,48,128]{2,1,0:T(8,128)} %diel.2) | copy-start | bytes 442372
  52.8 7.3 %collective-permute-start.4 = (f32[384,128]{1,0:T(8,128)S(1)}, f32[384,128]{1,0:T(8,128)S(1)}, u32[]{:S(2)}, u32[]{:S(2)}) collective-permute-start(f32[384,128]{1,0:T(8,128)S(1)} %get-tuple-element.27), channel_id=1, source_target_pairs={{1,0},{2,1},{3,2},{4,3},{5,4},{6,5},{7,6},{8,7},{9,8},{10,9},{11,1... | collective-permute-start | bytes 589832 | tf_op jit(solution)/shard_map/ppermute | solution.py:503
  56.5 9.1 %collective-permute-start.3 = (f32[384,128]{1,0:T(8,128)S(1)}, f32[384,128]{1,0:T(8,128)S(1)}, u32[]{:S(2)}, u32[]{:S(2)}) collective-permute-start(f32[384,128]{1,0:T(8,128)S(1)} %get-tuple-element.26), channel_id=1, source_target_pairs={{0,1},{1,2},{2,3},{3,4},{4,5},{5,6},{6,7},{7,8},{8,9},{9,10},{10,1... | collective-permute-start | bytes 589832 | tf_op jit(solution)/shard_map/ppermute | solution.py:502
  58.5 7.1 %copy-start = (f32[4,6,48,128]{3,2,1,0:T(8,128)S(1)}, f32[4,6,48,128]{3,2,1,0:T(8,128)}, u32[]{:S(2)}) copy-start(f32[4,6,48,128]{3,2,1,0:T(8,128)} %orb.2) | copy-start | bytes 1769476
  58.5 7.1 %copy-start.3 = (f32[6,48,128]{2,1,0:T(8,128)S(1)}, f32[6,48,128]{2,1,0:T(8,128)}, u32[]{:S(2)}) copy-start(f32[6,48,128]{2,1,0:T(8,128)} %core.2) | copy-start | bytes 442372
  71.7 9.3 %collective-permute-start.6 = (f32[4,6,6,8,128]{4,3,2,1,0:T(8,128)S(1)}, f32[4,6,6,8,128]{4,3,2,1,0:T(8,128)S(1)}, u32[]{:S(2)}, u32[]{:S(2)}) collective-permute-start(f32[4,6,6,8,128]{4,3,2,1,0:T(8,128)S(1)} %get-tuple-element.32.y2), channel_id=1, source_target_pairs={{1,0},{2,1},{3,2},{4,3},{5,4},{6,5},{7,6},{8,7},{9,8},{10,9},{11,1... | collective-permute-start | bytes 1769480 | tf_op jit(solution)/shard_map/ppermute | solution.py:503
  73.6 13.3 %collective-permute-start.5 = (f32[4,6,6,8,128]{4,3,2,1,0:T(8,128)S(1)}, f32[4,6,6,8,128]{4,3,2,1,0:T(8,128)S(1)}, u32[]{:S(2)}, u32[]{:S(2)}) collective-permute-start(f32[4,6,6,8,128]{4,3,2,1,0:T(8,128)S(1)} %get-tuple-element.32.y2), channel_id=1, source_target_pairs={{0,1},{1,2},{2,3},{3,4},{4,5},{5,6},{6,7},{7,8},{8,9},{9,10},{10,1... | collective-permute-start | bytes 1769480 | tf_op jit(solution)/shard_map/ppermute | solution.py:502

commit v3 on v2

--- a/solution.py
+++ b/solution.py
@@ -129,19 +129,15 @@
     )[0]
 
 
-def join_kernel(chunks, got, left, right, to_right, to_left, sems):
+def join_kernel(chunks, sides, got, far, near, to_near, to_far, sems):
     size = ROWS // chunks
+    turn = sides[1]
     copies = []
-    for at, (src, edge, dst) in enumerate(
-        (
-            (left, BX - 1, to_right),
-            (right, 0, to_left),
-        )
-    ):
+    for at, (src, edge, dst) in enumerate(((far, BX - 1, to_near), (near, 0, to_far))):
         for k in range(2):
             copies.append(
                 pltpu.make_async_copy(
-                    src.at[NB + k, edge],
+                    src.at[NB + k, turned(turn, edge)],
                     dst.at[pl.ds(ROWS + k * NY, NY)],
                     sems.at[2 * at + k],
                 )
@@ -150,24 +146,28 @@
         c.start()
     for c in range(chunks):
         value = got[c]
-        for dst in (to_right, to_left):
+        for dst in (to_near, to_far):
             dst[pl.ds(c * size, size), :] = value
     for c in copies:
         c.wait()
 
 
-def join(chunks, got, left, right):
+def join(chunks, sides, got, near, far):
     def kernel(*refs):
         join_kernel(chunks, *refs)
 
     return call(
         kernel,
         [(ROWS + 2 * NY, NZ), (ROWS + 2 * NY, NZ)],
-        [VM, ANY, ANY],
+        [SM, VM, ANY, ANY],
         [VM, VM],
         [pltpu.SemaphoreType.DMA((4,))],
-        (got, left, right),
+        (sides, got, far, near),
     )
+
+
+def turned(turn, p):
+    return jnp.where(turn > 0, BX - 1 - p, p)
 
 
 def strips(ref, *at):
@@ -237,30 +237,30 @@
         behind = jnp.where(not_begin, pltpu.roll(d[j], 1, 1), 0.0)
         sums = [d[j] + v for v in (xp[j], xm[j], wide[j + 2], wide[j], ahead, behind)]
         den = ((sums[0] + sums[1]) + (sums[2] + sums[3])) + (sums[4] + sums[5])
-        inverse = jnp.where(keep, 1.0 / den, 0.0)
+        inverse = 1.0 / den if keep is None else jnp.where(keep, 1.0 / den, 0.0)
         sums[4] = jnp.where(not_last, sums[4], 0.0)
         sums[5] = jnp.where(not_begin, sums[5], 0.0)
         out.append([s * inverse for s in sums] + [8.0 * inverse])
     return out
 
 
-def weigh_kernel(edges, diel, field, left, right, wts, fs, ds):
+def weigh_kernel(sides, diel, field, far, near, wts, fs, ds):
     m = Masks()
-    for k, (lo, own, hi) in enumerate(((left.at[NB], field, right.at[NB]), (left.at[NB + 1], diel, right.at[NB + 1]))):
+    turn = sides[1]
+    for k, (lo, own, hi) in enumerate(((far.at[NB], field, near.at[NB]), (far.at[NB + 1], diel, near.at[NB + 1]))):
         dst = (fs, ds)[k]
 
         def move(p, _):
-            put_plain(dst, strips(lo, p), p)
-            put_plain(dst, strips(own, p), p + BX)
-            put_plain(dst, strips(hi, p), p + 2 * BX)
+            put_plain(dst, strips(lo, turned(turn, p)), p)
+            put_plain(dst, strips(own, turned(turn, p)), p + BX)
+            put_plain(dst, strips(hi, turned(turn, p)), p + 2 * BX)
             return 0
 
         lax.fori_loop(0, BX, move, 0)
-    has_left = edges[0] > 0
-    has_right = edges[1] > 0
+    has_far = sides[0] > 0
 
     def weigh(i, _):
-        keep = ((i >= BX - 1) | has_left) & ((i < 2 * BX - 1) | has_right)
+        keep = (i >= BX - 1) | has_far
         got = face_sums(plain(ds, i + 1), plain(ds, i + 2), plain(ds, i), keep, m)
         for j in range(NV):
             for k in range(7):
@@ -270,7 +270,7 @@
     lax.fori_loop(0, 3 * BX - 2, weigh, 0, unroll=2)
 
 
-def weigh(edges, diel, field, left, right):
+def weigh(sides, diel, field, far, near):
     vec = (NV, STRIPS, NZ)
     return call(
         weigh_kernel,
@@ -278,41 +278,43 @@
         [SM] + [VM] * 4,
         [VM, VM],
         [pltpu.VMEM((3 * BX, *vec), jnp.float32)],
-        (edges, diel, field, left, right),
+        (sides, diel, field, far, near),
     )
 
 
 def first_kernel(
-    edges, orb, core, left, right, mine, rho_left, rho_right, wts, fs,
+    sides, orb, core, far, near, mine, rho_far, rho_near, wts, fs,
     potential, y1, y2, diag,
     fa, fb, src, xc, zp,
 ):
-    has_left = edges[0] > 0
-    has_right = edges[1] > 0
+    has_far = sides[0] > 0
+    turn = sides[1]
+    at = [turned(turn, p) for p in range(BX)]
     m = Masks()
     matrix = band_matrix()
 
     for o in range(NB):
-        for ref, lo, count, at in ((left, BX - 3, 3, 0), (orb, 0, BX, 3), (right, 0, 3, 3 + BX)):
-            x = ref[o, pl.ds(lo, count)].reshape(count * NY, NZ)
-            zp[o, pl.ds(at, count)] = along_z(x, matrix).reshape(count, NY, NZ)
+        for ref, planes, base in ((far, (3, 4, 5), 0), (orb, range(BX), 3), (near, (0, 1, 2), 3 + BX)):
+            x = jnp.concatenate([ref[o, at[p]] for p in planes], axis=0)
+            zp[o, pl.ds(base, len(planes))] = along_z(x, matrix).reshape(len(planes), NY, NZ)
 
     def sources(ref, lo, hi, base):
         def body(p, _):
             i = p + base
-            for j, v in enumerate(strips(ref, p)):
+            for j, v in enumerate(strips(ref, turned(turn, p))):
                 src[i, j] = wts[6, i, j] * v
             return 0
 
         lax.fori_loop(lo, hi, body, 0)
 
-    sources(rho_left, 1, BX, -1)
+    sources(rho_far, 1, BX, -1)
     sources(mine, 0, BX, BX - 1)
-    sources(rho_right, 0, BX - 1, 2 * BX - 1)
+    sources(rho_near, 0, BX - 1, 2 * BX - 1)
 
     def exchange(ref, extra, lo, count, base):
         def body(p, _):
-            for j, (a, b) in enumerate(zip(strips(ref, p + lo), strips(extra, p + lo))):
+            plane = turned(turn, p + lo)
+            for j, (a, b) in enumerate(zip(strips(ref, plane), strips(extra, plane))):
                 x = a + b
                 x = jnp.where(x > 0.0, x, 1.0)
                 root = jnp.exp(jnp.log(x) * (1.0 / 3.0))
@@ -322,9 +324,9 @@
 
         lax.fori_loop(0, count, body, 0)
 
-    exchange(rho_left, left.at[NB + 2], BX - 3, 3, 0)
+    exchange(rho_far, far.at[NB + 2], BX - 3, 3, 0)
     exchange(mine, core, 0, BX, 3)
-    exchange(rho_right, right.at[NB + 2], 0, 3, 3 + BX)
+    exchange(rho_near, near.at[NB + 2], 0, 3, 3 + BX)
 
     def swept(mid, up, down, w, s):
         wide = with_sides(mid, 1, m)
@@ -336,15 +338,15 @@
             out.append(total + s(j))
         return out
 
-    for near, far, rho, sign in ((left, rho_left, rho_left, 1), (right, rho_right, rho_right, -1)):
+    for brick, rho, sign in ((far, rho_far, 1), (near, rho_near, -1)):
         p = 0 if sign > 0 else BX - 1
         e = p if sign > 0 else 3 * BX - 1
-        inner, outer = strips(near, NB + 1, p + sign), strips(far, BX + 1)
+        inner, outer = strips(brick, NB + 1, at[p + sign]), strips(rho, BX + 1)
         xp, xm = (inner, outer) if sign > 0 else (outer, inner)
-        got = face_sums(strips(near, NB + 1, p), xp, xm, has_left if sign > 0 else has_right, m)
-        f_in, f_out = plain(fs, e + sign), strips(far, BX)
+        got = face_sums(strips(brick, NB + 1, at[p]), xp, xm, has_far if sign > 0 else None, m)
+        f_in, f_out = plain(fs, e + sign), strips(rho, BX)
         up, down = (f_in, f_out) if sign > 0 else (f_out, f_in)
-        dens = strips(rho, p)
+        dens = strips(rho, at[p])
         new = swept(plain(fs, e), up, down, lambda k, j: got[j][k], lambda j: got[j][6] * dens[j])
         put_plain(fb, new, e)
 
@@ -376,24 +378,20 @@
     lax.fori_loop(0, 2 * BX, last_sweep, 0, unroll=2)
 
     def give(p, _):
-        put_strips(potential, plain(fa, p + BX), p)
+        put_strips(potential, plain(fa, p + BX), turned(turn, p))
         return 0
 
     lax.fori_loop(0, BX, give, 0, unroll=2)
 
     def step_one(o, _):
         def get(p):
-            if p < BX:
-                return strips(left, o, p)
-            return strips(orb, o, p - BX) if p < 2 * BX else strips(right, o, p - 2 * BX)
+            return strips((far, orb, near)[p // BX], o, at[p % BX])
 
         for j in range(2 * BX):
             rest, mid = stencil(lambda dist: get(j + 3 + dist), strips(zp, o, j), m, 1.0)
             new = [a * b + c for a, b, c in zip(plain(diag, j), mid, rest)]
             if j < 3:
-                new = [jnp.where(has_left, v, 0.0) for v in new]
-            if j >= 3 + BX:
-                new = [jnp.where(has_right, v, 0.0) for v in new]
+                new = [jnp.where(has_far, v, 0.0) for v in new]
             put_plain(y1, new, o, j)
         return 0
 
@@ -407,14 +405,15 @@
         for o in range(NB):
             zs = [zp[o, j, pl.ds(i * STRIPS, STRIPS), :] for i in range(NV)]
             rest, mid = stencil(lambda dist: plain(y1, o, j + 3 + dist), zs, m, 2.0)
-            old = strips(orb, o, j)
-            put_plain(y2, [2.0 * a * b + (c - d) for a, b, c, d in zip(q, mid, rest, old)], o, j)
+            here = turned(turn, j)
+            old = strips(orb, o, here)
+            put_plain(y2, [2.0 * a * b + (c - d) for a, b, c, d in zip(q, mid, rest, old)], o, here)
         return 0
 
     lax.fori_loop(0, BX, step_two, 0)
 
 
-def first(edges, orb, core, left, right, mine, rho_left, rho_right, wts, fs):
+def first(sides, orb, core, far, near, mine, rho_far, rho_near, wts, fs):
     f = jnp.float32
     vec = (NV, STRIPS, NZ)
     return call(
@@ -429,34 +428,31 @@
             pltpu.VMEM((2 * BX, *vec), f),
             pltpu.VMEM((NB, 2 * BX, NY, NZ), f),
         ],
-        (edges, orb, core, left, right, mine, rho_left, rho_right, wts, fs),
+        (sides, orb, core, far, near, mine, rho_far, rho_near, wts, fs),
     )
 
 
-def second_kernel(edges, y1, y2, left, right, diag, out, y3, zp, done, sems):
-    has_left = edges[0] > 0
-    has_right = edges[1] > 0
+def second_kernel(sides, y1, y2, near, far, diag, out, y3, zp, done, sems):
+    has_far = sides[0] > 0
+    turn = sides[1]
+    at = [turned(turn, p) for p in range(BX)]
     m = Masks()
     matrix = band_matrix()
     for o in range(NB):
-        for ref, lo, count, at in ((left, BX - 3, 3, 0), (y2, 0, BX, 3), (right, 0, 3, 3 + BX)):
-            x = ref[o, pl.ds(lo, count)].reshape(count * NY, NZ)
-            zp[o, pl.ds(at, count)] = along_z(x, matrix).reshape(count, NV, STRIPS, NZ)
+        for ref, planes, base in ((far, (3, 4, 5), 0), (y2, range(BX), 3), (near, (0, 1, 2), 3 + BX)):
+            x = jnp.concatenate([ref[o, at[p]].reshape(NY, NZ) for p in planes], axis=0)
+            zp[o, pl.ds(base, len(planes))] = along_z(x, matrix).reshape(len(planes), NV, STRIPS, NZ)
 
     def step_three(o, _):
         def get(p):
-            if p < BX:
-                return plain(left, o, p)
-            return plain(y2, o, p - BX) if p < 2 * BX else plain(right, o, p - 2 * BX)
+            return plain((far, y2, near)[p // BX], o, at[p % BX])
 
         for j in range(2 * BX):
             rest, mid = stencil(lambda dist: get(j + 3 + dist), plain(zp, o, j), m, 2.0)
             old = plain(y1, o, j)
             new = [2.0 * a * b + (c - d) for a, b, c, d in zip(plain(diag, j), mid, rest, old)]
             if j < 3:
-                new = [jnp.where(has_left, v, 0.0) for v in new]
-            if j >= 3 + BX:
-                new = [jnp.where(has_right, v, 0.0) for v in new]
+                new = [jnp.where(has_far, v, 0.0) for v in new]
             put_plain(y3, new, o, j)
         return 0
 
@@ -468,9 +464,9 @@
     def step_four(o, _):
         for j in range(BX):
             rest, mid = stencil(lambda dist: plain(y3, o, j + 3 + dist), plain(zp, o, j), m, 2.0)
-            old = plain(y2, o, j)
+            old = plain(y2, o, at[j])
             new = [2.0 * a * b + (c - d) for a, b, c, d in zip(plain(diag, j + 3), mid, rest, old)]
-            put_strips(done, new, o, j)
+            put_strips(done, new, o, at[j])
         pltpu.make_async_copy(done.at[o], out.at[o], sems.at[o]).start()
         return 0
 
@@ -479,7 +475,7 @@
         pltpu.make_async_copy(done.at[o], out.at[o], sems.at[o]).wait()
 
 
-def second(edges, y1, y2, left, right, diag):
+def second(sides, y1, y2, far, near, diag):
     f = jnp.float32
     vec = (NV, STRIPS, NZ)
     return call(
@@ -493,43 +489,46 @@
             pltpu.VMEM((NB, BX, NY, NZ), f),
             pltpu.SemaphoreType.DMA((NB,)),
         ],
-        (edges, y1, y2, left, right, diag),
+        (sides, y1, y2, near, far, diag),
     )[0]
 
 
-def from_sides(to_right, to_left):
+def swapped(to_far, to_near):
     n = lax.axis_size("dom")
-    left = lax.ppermute(to_right, "dom", [(i, i + 1) for i in range(n - 1)])
-    right = lax.ppermute(to_left, "dom", [(i + 1, i) for i in range(n - 1)])
-    return left, right
+    pairs = [(i, i + 1) for i in range(n - 1)]
+    far = [p for i, j in pairs if i % 2 for p in ((i, j), (j, i))]
+    near = [p for i, j in pairs if i % 2 == 0 for p in ((i, j), (j, i))]
+    return lax.ppermute(to_far, "dom", far), lax.ppermute(to_near, "dom", near)
 
 
 def local(orbitals, occupation, dielectric, core_density, start_field):
     bands = lax.axis_size("band")
     dom = lax.axis_index("dom")
-    far = bands // 2
-    groups = [list(range(far)), list(range(far, bands))]
-    edges = jnp.stack([(dom > 0).astype(jnp.int32), (dom < lax.axis_size("dom") - 1).astype(jnp.int32)])
-
-    parts = density(far, occupation, orbitals)
+    half = bands // 2
+    groups = [list(range(half)), list(range(half, bands))]
+    turn = dom % 2
+    has_far = jnp.where(turn > 0, dom < lax.axis_size("dom") - 1, dom > 0)
+    sides = jnp.stack([has_far.astype(jnp.int32), turn.astype(jnp.int32)])
+
+    parts = density(half, occupation, orbitals)
     parts = lax.all_to_all(parts, "band", 0, 0, axis_index_groups=groups)
     mine = jnp.sum(parts, axis=0)
-    other = lax.ppermute(mine, "band", [(i, (i + far) % bands) for i in range(bands)])
+    other = lax.ppermute(mine, "band", [(i, (i + half) % bands) for i in range(bands)])
     held, mine = lax.optimization_barrier(((orbitals, start_field, dielectric, core_density), mine))
     packed = pack(*held)
-    left, right = from_sides(packed, packed)
-    got = lax.all_to_all(spread(far, mine, other), "band", 0, 0, axis_index_groups=groups)
-    to_right, to_left = join(far, got, left, right)
-    rho_left, rho_right = from_sides(to_right, to_left)
-    (left, right), to_right = lax.optimization_barrier(((left, right), to_right))
-    wts, fs = weigh(edges, dielectric, start_field, left, right)
+    far, near = swapped(packed, packed)
+    got = lax.all_to_all(spread(half, mine, other), "band", 0, 0, axis_index_groups=groups)
+    to_near, to_far = join(half, sides, got, near, far)
+    rho_far, rho_near = swapped(to_far, to_near)
+    (far, near), to_near = lax.optimization_barrier(((far, near), to_near))
+    wts, fs = weigh(sides, dielectric, start_field, far, near)
     cells = (-1, NY, NZ)
     potential, y1, y2, diag = first(
-        edges, orbitals, core_density, left, right,
-        to_right.reshape(cells), rho_left.reshape(cells), rho_right.reshape(cells), wts, fs,
+        sides, orbitals, core_density, far, near,
+        to_near.reshape(cells), rho_far.reshape(cells), rho_near.reshape(cells), wts, fs,
     )
-    y2_left, y2_right = from_sides(y2, y2)
-    return potential, second(edges, y1, y2, y2_left, y2_right, diag)
+    y2_far, y2_near = swapped(y2, y2)
+    return potential, second(sides, y1, y2, y2_far, y2_near, diag)
 
 
 def solution(mesh):

time: 90.9 us -> 86.8 us (0.955)
  the two profiles are of different devices: /device:TPU:8 before, /device:TPU:7 now
where the time goes in v3:
time: 86.8 us; the launch traced here: 86.2 us
  starting transfers between devices  27.4 us (32%)
  waiting for transfers between devices  23.1 us (27%)
  blocking collectives  18.2 us (21%)
  Pallas kernels  16.7 us (19%)
    all_to_all x1, blocking collectives, local(): parts = lax.all_to_all(parts, 'band', 0, 0, axis_index_groups=groups)  18.2 us
    pallas_call x7, Pallas kernels, call(): pl.pallas_call(kernel, out_shape=[jax.ShapeDtypeStruct(s, jnp.float32) fo...  16.7 us
    ppermute x3, waiting for transfers between devices, swapped(): lax.ppermute(to_far, 'dom', far)  15 us
    ppermute x3, starting transfers between devices, swapped(): lax.ppermute(to_near, 'dom', near)  8.74 us
    all_to_all x1, waiting for transfers between devices, local(): lax.all_to_all(spread(half, mine, other), 'band', 0, 0, axis_index_groups...  8.11 us
    ppermute x3, starting transfers between devices, swapped(): lax.ppermute(to_far, 'dom', far)  7.8 us
    ppermute x1, starting transfers between devices, local(): lax.ppermute(mine, 'band', [(i, (i + half) % bands) for i in range(bands)])  7.45 us
    all_to_all x1, starting transfers between devices, local(): lax.all_to_all(spread(half, mine, other), 'band', 0, 0, axis_index_groups...  3.38 us
  transfers between devices with their start and end apart: 8, of which 4 were waited for; matrix products, arithmetic and copies ran while one was open for 0% of the time, Pallas kernels for 5%

profile of v3, /device:TPU:7, one launch (start us, length us, event | category | flops | bytes accessed | tf_op | source)
XLA Modules:
  0.0 86.2 jit_solution(12773125838718660306)
XLA Ops:
  0.6 1.8 %shard_map.68 = f32[8,36,128]{2,1,0:T(8,128)} custom-call(f32[4]{0:T(128)} %refs_0_.1, f32[4,6,48,128]{3,2,1,0:T(8,128)} %orb.2), custom_call_target="tpu_custom_call" | custom-call | flops 2000000000 | bytes 2000000 | tf_op jit(solution)/shard_map/pallas_call | solution.py:34
  2.5 18.2 %all_to_all.10 = f32[8,36,128]{2,1,0:T(8,128)S(1)} all-to-all(f32[8,36,128]{2,1,0:T(8,128)} %shard_map.68), channel_id=1, replica_groups={{0,32,64,96,128,160,192,224},{256,288,320,352,384,416,448,480},{1,33,65..., dimensions={0} | all-to-all | bytes 294912 | tf_op jit(solution)/shard_map/all_to_all | solution.py:514
  20.7 7.5 %collective-permute-start.2 = (f32[36,128]{1,0:T(8,128)S(1)}, f32[36,128]{1,0:T(8,128)S(1)}, u32[]{:S(2)}, u32[]{:S(2)}) collective-permute-start(f32[36,128]{1,0:T(8,128)S(1)} %reduce_sum.9.mine), channel_id=1, source_target_pairs={{0,256},{32,288},{64,320},{96,352},{128,384},{160,416},{192,448},{... | collective-permute-start | bytes 55304 | tf_op jit(solution)/shard_map/ppermute | solution.py:516
  28.1 2.2 %shard_map.69 = f32[7,6,48,128]{3,2,1,0:T(8,128)} custom-call(f32[4,6,48,128]{3,2,1,0:T(8,128)} %orb.2, f32[6,48,128]{2,1,0:T(8,128)} %field.2, f32[6,48,128]{2,1,0:T(8,128)} %diel.2, f32[6,48,128]{2,1,0:T(8,128)} %core.2), custom_call_target="tpu_custom_call" | custom-call | flops 20000000000 | bytes 20000000 | tf_op jit(solution)/shard_map/pallas_call | solution.py:34
  30.3 4.8 %collective-permute-start.1 = (f32[7,6,48,128]{3,2,1,0:T(8,128)}, f32[7,6,48,128]{3,2,1,0:T(8,128)S(1)}, u32[]{:S(2)}, u32[]{:S(2)}) collective-permute-start(f32[7,6,48,128]{3,2,1,0:T(8,128)} %shard_map.69), channel_id=1, source_target_pairs={{0,1},{1,0},{2,3},{3,2},{4,5},{5,4},{6,7},{7,6},{8,9},{9,8},{10,11... | collective-permute-start | bytes 3096584 | tf_op jit(solution)/shard_map/ppermute | solution.py:501
  35.1 2.1 %collective-permute-start = (f32[7,6,48,128]{3,2,1,0:T(8,128)}, f32[7,6,48,128]{3,2,1,0:T(8,128)S(1)}, u32[]{:S(2)}, u32[]{:S(2)}) collective-permute-start(f32[7,6,48,128]{3,2,1,0:T(8,128)} %shard_map.69), channel_id=1, source_target_pairs={{1,2},{2,1},{3,4},{4,3},{5,6},{6,5},{7,8},{8,7},{9,10},{10,9},{11,... | collective-permute-start | bytes 3096584 | tf_op jit(solution)/shard_map/ppermute | solution.py:501
  37.2 0.0 collective-permute-done.2.other
  37.2 0.7 shard_map.70
  37.9 3.4 %all-to-all-start.1 = ((f32[8,36,128]{2,1,0:T(8,128)}), f32[8,36,128]{2,1,0:T(8,128)S(1)}, u32[]{:S(2)}, u32[]{:S(2)}) async-start(f32[8,36,128]{2,1,0:T(8,128)} %shard_map.70), calls=%async_computation.1 | async-start | bytes 327680 | tf_op jit(solution)/shard_map/all_to_all | solution.py:520
  41.3 0.1 pad_add_fusion.refs_0_.sides
  41.4 0.0 copy-start.1
  41.4 8.1 %all-to-all-done.1.refs_1_ = f32[8,36,128]{2,1,0:T(8,128)S(1)} async-done(((f32[8,36,128]{2,1,0:T(8,128)}), f32[8,36,128]{2,1,0:T(8,128)S(1)}, u32[]{:S(2)}, u32[]{:S(2)}) %all-to-all-start.1) | async-done | bytes 147488 | tf_op jit(solution)/shard_map/all_to_all | solution.py:520
  49.5 0.0 collective-permute-done.1.refs_3_.near
  49.5 3.8 %collective-permute-done.refs_2_.far = f32[7,6,48,128]{3,2,1,0:T(8,128)S(1)} collective-permute-done((f32[7,6,48,128]{3,2,1,0:T(8,128)}, f32[7,6,48,128]{3,2,1,0:T(8,128)S(1)}, u32[]{:S(2)}, u32[]{:S(2)}) %collective-permute-start) | collective-permute-done | bytes 1032224 | tf_op jit(solution)/shard_map/ppermute | solution.py:501
  53.4 0.7 shard_map.71
  54.1 2.8 %collective-permute-start.3 = (f32[384,128]{1,0:T(8,128)S(1)}, f32[384,128]{1,0:T(8,128)S(1)}, u32[]{:S(2)}, u32[]{:S(2)}) collective-permute-start(f32[384,128]{1,0:T(8,128)S(1)} %get-tuple-element.27), channel_id=1, source_target_pairs={{1,2},{2,1},{3,4},{4,3},{5,6},{6,5},{7,8},{8,7},{9,10},{10,9},{11,... | collective-permute-start | bytes 589832 | tf_op jit(solution)/shard_map/ppermute | solution.py:501
  57.0 0.0 copy-start
  57.0 0.0 copy-start.3
  57.0 2.1 %collective-permute-start.4 = (f32[384,128]{1,0:T(8,128)S(1)}, f32[384,128]{1,0:T(8,128)S(1)}, u32[]{:S(2)}, u32[]{:S(2)}) collective-permute-start(f32[384,128]{1,0:T(8,128)S(1)} %get-tuple-element.26), channel_id=1, source_target_pairs={{0,1},{1,0},{2,3},{3,2},{4,5},{5,4},{6,7},{7,6},{8,9},{9,8},{10,11... | collective-permute-start | bytes 589832 | tf_op jit(solution)/shard_map/ppermute | solution.py:501
  59.1 0.0 copy-done.1
  59.1 0.0 copy-done.2
  59.1 1.5 %shard_map.72 = (f32[7,16,6,8,128]{4,3,2,1,0:T(8,128)S(1)}, f32[18,6,8,128]{3,2,1,0:T(8,128)S(1)}) custom-call(s32[2]{0:T(128)S(1)} %pad_add_fusion.refs_0_.sides, f32[6,48,128]{2,1,0:T(8,128)S(1)} %copy-done.2, f32[6,48,128]{2,1,0:T(8,128)S(1)} %copy-done.1, f32[7,6,48,128]{3,2,1,0:T(8,128)S(1)} %collective-permute-done.refs_2_.far, ...), custom_call_target="tpu_custom_call" | custom-call | flops 2000000000 | bytes 2000000 | tf_op jit(solution)/shard_map/pallas_call | solution.py:34
  60.6 2.6 %collective-permute-done.3 = f32[384,128]{1,0:T(8,128)S(1)} collective-permute-done((f32[384,128]{1,0:T(8,128)S(1)}, f32[384,128]{1,0:T(8,128)S(1)}, u32[]{:S(2)}, u32[]{:S(2)}) %collective-permute-start.3) | collective-permute-done | bytes 196640 | tf_op jit(solution)/shard_map/ppermute | solution.py:501
  63.2 0.0 collective-permute-done.4
  63.2 0.0 copy-done
  63.2 0.0 copy-done.3
  63.2 6.2 %shard_map.73 = (f32[6,48,128]{2,1,0:T(8,128)}, f32[4,12,6,8,128]{4,3,2,1,0:T(8,128)S(1)}, f32[4,6,6,8,128]{4,3,2,1,0:T(8,128)S(1)}, f32[12,6,8,128]{3,2,1,0:T(8,128)S(1)}) custom-call(s32[2]{0:T(128)S(1)} %pad_add_fusion.refs_0_.sides, f32[4,6,48,128]{3,2,1,0:T(8,128)S(1)} %copy-done, f32[6,48,128]{2,1,0:T(8,128)S(1)} %copy-done.3, ...), custom_call_target="tpu_custom_call" | custom-call | flops 2000000000 | bytes 2000000 | tf_op jit(solution)/shard_map/pallas_call | solution.py:34
  69.4 2.8 %collective-permute-start.6 = (f32[4,6,6,8,128]{4,3,2,1,0:T(8,128)S(1)}, f32[4,6,6,8,128]{4,3,2,1,0:T(8,128)S(1)}, u32[]{:S(2)}, u32[]{:S(2)}) collective-permute-start(f32[4,6,6,8,128]{4,3,2,1,0:T(8,128)S(1)} %get-tuple-element.32.y2), channel_id=1, source_target_pairs={{1,2},{2,1},{3,4},{4,3},{5,6},{6,5},{7,8},{8,7},{9,10},{10,9},{11,... | collective-permute-start | bytes 1769480 | tf_op jit(solution)/shard_map/ppermute | solution.py:501
  72.3 1.9 %collective-permute-start.5 = (f32[4,6,6,8,128]{4,3,2,1,0:T(8,128)S(1)}, f32[4,6,6,8,128]{4,3,2,1,0:T(8,128)S(1)}, u32[]{:S(2)}, u32[]{:S(2)}) collective-permute-start(f32[4,6,6,8,128]{4,3,2,1,0:T(8,128)S(1)} %get-tuple-element.32.y2), channel_id=1, source_target_pairs={{0,1},{1,0},{2,3},{3,2},{4,5},{5,4},{6,7},{7,6},{8,9},{9,8},{10,11... | collective-permute-start | bytes 1769480 | tf_op jit(solution)/shard_map/ppermute | solution.py:501
  74.2 8.5 %collective-permute-done.6.far = f32[4,6,6,8,128]{4,3,2,1,0:T(8,128)S(1)} collective-permute-done((f32[4,6,6,8,128]{4,3,2,1,0:T(8,128)S(1)}, f32[4,6,6,8,128]{4,3,2,1,0:T(8,128)S(1)}, u32[]{:S(2)}, u32[]{:S(2)}) %collective-permute-start.6) | collective-permute-done | bytes 589856 | tf_op jit(solution)/shard_map/ppermute | solution.py:501
  82.7 0.0 collective-permute-done.5.near
  82.7 3.5 %shard_map.74 = f32[4,6,48,128]{3,2,1,0:T(8,128)} custom-call(s32[2]{0:T(128)S(1)} %pad_add_fusion.refs_0_.sides, f32[4,12,6,8,128]{4,3,2,1,0:T(8,128)S(1)} %get-tuple-element.31.y1, f32[4,6,6,8,128]{4,3,2,1,0:T(8,128)S(1)} %get-tuple-element.32.y2, f32[4,6,6,8,128]{4,3,2,1,0:T(8,128)S(1)} %collective-permute-done.5.near, ...), custom_call_target="tpu_custom_call" | custom-call | flops 2000000000 | bytes 2000000 | tf_op jit(solution)/shard_map/pallas_call | solution.py:34
  (2 shorter events, 0.0 us)
Async XLA Ops:
  20.7 16.6 %collective-permute-start.2 = (f32[36,128]{1,0:T(8,128)S(1)}, f32[36,128]{1,0:T(8,128)S(1)}, u32[]{:S(2)}, u32[]{:S(2)}) collective-permute-start(f32[36,128]{1,0:T(8,128)S(1)} %reduce_sum.9.mine), channel_id=1, source_target_pairs={{0,256},{32,288},{64,320},{96,352},{128,384},{160,416},{192,448},{... | collective-permute-start | bytes 55304 | tf_op jit(solution)/shard_map/ppermute | solution.py:516
  30.3 19.2 %collective-permute-start.1 = (f32[7,6,48,128]{3,2,1,0:T(8,128)}, f32[7,6,48,128]{3,2,1,0:T(8,128)S(1)}, u32[]{:S(2)}, u32[]{:S(2)}) collective-permute-start(f32[7,6,48,128]{3,2,1,0:T(8,128)} %shard_map.69), channel_id=1, source_target_pairs={{0,1},{1,0},{2,3},{3,2},{4,5},{5,4},{6,7},{7,6},{8,9},{9,8},{10,11... | collective-permute-start | bytes 3096584 | tf_op jit(solution)/shard_map/ppermute | solution.py:501
  35.1 18.3 %collective-permute-start = (f32[7,6,48,128]{3,2,1,0:T(8,128)}, f32[7,6,48,128]{3,2,1,0:T(8,128)S(1)}, u32[]{:S(2)}, u32[]{:S(2)}) collective-permute-start(f32[7,6,48,128]{3,2,1,0:T(8,128)} %shard_map.69), channel_id=1, source_target_pairs={{1,2},{2,1},{3,4},{4,3},{5,6},{6,5},{7,8},{8,7},{9,10},{10,9},{11,... | collective-permute-start | bytes 3096584 | tf_op jit(solution)/shard_map/ppermute | solution.py:501
  37.9 11.6 %all-to-all-start.1 = ((f32[8,36,128]{2,1,0:T(8,128)}), f32[8,36,128]{2,1,0:T(8,128)S(1)}, u32[]{:S(2)}, u32[]{:S(2)}) async-start(f32[8,36,128]{2,1,0:T(8,128)} %shard_map.70), calls=%async_computation.1 | async-start | bytes 327680 | tf_op jit(solution)/shard_map/all_to_all | solution.py:520
  41.4 17.6 %copy-start.1 = (f32[6,48,128]{2,1,0:T(8,128)S(1)}, f32[6,48,128]{2,1,0:T(8,128)}, u32[]{:S(2)}) copy-start(f32[6,48,128]{2,1,0:T(8,128)} %field.2) | copy-start | bytes 442372
  41.4 17.7 %copy-start.2 = (f32[6,48,128]{2,1,0:T(8,128)S(1)}, f32[6,48,128]{2,1,0:T(8,128)}, u32[]{:S(2)}) copy-start(f32[6,48,128]{2,1,0:T(8,128)} %diel.2) | copy-start | bytes 442372
  54.1 9.1 %collective-permute-start.3 = (f32[384,128]{1,0:T(8,128)S(1)}, f32[384,128]{1,0:T(8,128)S(1)}, u32[]{:S(2)}, u32[]{:S(2)}) collective-permute-start(f32[384,128]{1,0:T(8,128)S(1)} %get-tuple-element.27), channel_id=1, source_target_pairs={{1,2},{2,1},{3,4},{4,3},{5,6},{6,5},{7,8},{8,7},{9,10},{10,9},{11,... | collective-permute-start | bytes 589832 | tf_op jit(solution)/shard_map/ppermute | solution.py:501
  57.0 6.3 %copy-start = (f32[4,6,48,128]{3,2,1,0:T(8,128)S(1)}, f32[4,6,48,128]{3,2,1,0:T(8,128)}, u32[]{:S(2)}) copy-start(f32[4,6,48,128]{3,2,1,0:T(8,128)} %orb.2) | copy-start | bytes 1769476
  57.0 6.2 %copy-start.3 = (f32[6,48,128]{2,1,0:T(8,128)S(1)}, f32[6,48,128]{2,1,0:T(8,128)}, u32[]{:S(2)}) copy-start(f32[6,48,128]{2,1,0:T(8,128)} %core.2) | copy-start | bytes 442372
  57.0 6.2 %collective-permute-start.4 = (f32[384,128]{1,0:T(8,128)S(1)}, f32[384,128]{1,0:T(8,128)S(1)}, u32[]{:S(2)}, u32[]{:S(2)}) collective-permute-start(f32[384,128]{1,0:T(8,128)S(1)} %get-tuple-element.26), channel_id=1, source_target_pairs={{0,1},{1,0},{2,3},{3,2},{4,5},{5,4},{6,7},{7,6},{8,9},{9,8},{10,11... | collective-permute-start | bytes 589832 | tf_op jit(solution)/shard_map/ppermute | solution.py:501
  69.4 13.3 %collective-permute-start.6 = (f32[4,6,6,8,128]{4,3,2,1,0:T(8,128)S(1)}, f32[4,6,6,8,128]{4,3,2,1,0:T(8,128)S(1)}, u32[]{:S(2)}, u32[]{:S(2)}) collective-permute-start(f32[4,6,6,8,128]{4,3,2,1,0:T(8,128)S(1)} %get-tuple-element.32.y2), channel_id=1, source_target_pairs={{1,2},{2,1},{3,4},{4,3},{5,6},{6,5},{7,8},{8,7},{9,10},{10,9},{11,... | collective-permute-start | bytes 1769480 | tf_op jit(solution)/shard_map/ppermute | solution.py:501
  72.3 10.5 %collective-permute-start.5 = (f32[4,6,6,8,128]{4,3,2,1,0:T(8,128)S(1)}, f32[4,6,6,8,128]{4,3,2,1,0:T(8,128)S(1)}, u32[]{:S(2)}, u32[]{:S(2)}) collective-permute-start(f32[4,6,6,8,128]{4,3,2,1,0:T(8,128)S(1)} %get-tuple-element.32.y2), channel_id=1, source_target_pairs={{0,1},{1,0},{2,3},{3,2},{4,5},{5,4},{6,7},{7,6},{8,9},{9,8},{10,11... | collective-permute-start | bytes 1769480 | tf_op jit(solution)/shard_map/ppermute | solution.py:501

commit v4 on v3

--- a/solution.py
+++ b/solution.py
@@ -12,6 +12,7 @@
 ROWS = BX * NY
 STRIPS = 8
 NV = NY // STRIPS
+VEC = (NV, STRIPS, NZ)
 
 COEFFS = (1.5, -0.15, 1.0 / 90.0)
 COEFF_ZERO = -49.0 / 18.0
@@ -30,13 +31,14 @@
 SM = pl.BlockSpec(memory_space=pltpu.SMEM)
 
 
-def call(kernel, outs, in_specs, out_specs, scratch, args, moved=2_000_000, vmem=VMEM_LIMIT):
+def call(kernel, outs, in_specs, out_specs, scratch, args, moved=2_000_000, vmem=VMEM_LIMIT, aliases=None):
     return pl.pallas_call(
         kernel,
         out_shape=[jax.ShapeDtypeStruct(s, jnp.float32) for s in outs],
         in_specs=in_specs,
         out_specs=out_specs,
         scratch_shapes=scratch,
+        input_output_aliases=aliases or {},
         compiler_params=pltpu.CompilerParams(vmem_limit_bytes=vmem),
         cost_estimate=pl.CostEstimate(flops=moved * 1000, bytes_accessed=moved, transcendentals=0),
     )(*args)
@@ -129,27 +131,16 @@
     )[0]
 
 
-def join_kernel(chunks, sides, got, far, near, to_near, to_far, sems):
+def join_kernel(chunks, sides, got, far, near, to_near, to_far):
     size = ROWS // chunks
     turn = sides[1]
-    copies = []
-    for at, (src, edge, dst) in enumerate(((far, BX - 1, to_near), (near, 0, to_far))):
+    for src, edge, dst in ((far, BX - 1, to_near), (near, 0, to_far)):
         for k in range(2):
-            copies.append(
-                pltpu.make_async_copy(
-                    src.at[NB + k, turned(turn, edge)],
-                    dst.at[pl.ds(ROWS + k * NY, NY)],
-                    sems.at[2 * at + k],
-                )
-            )
-    for c in copies:
-        c.start()
+            dst[pl.ds(ROWS + k * NY, NY), :] = src[NB + k, turned(turn, edge)]
     for c in range(chunks):
         value = got[c]
         for dst in (to_near, to_far):
             dst[pl.ds(c * size, size), :] = value
-    for c in copies:
-        c.wait()
 
 
 def join(chunks, sides, got, near, far):
@@ -159,9 +150,9 @@
     return call(
         kernel,
         [(ROWS + 2 * NY, NZ), (ROWS + 2 * NY, NZ)],
-        [SM, VM, ANY, ANY],
+        [SM, VM, VM, VM],
         [VM, VM],
-        [pltpu.SemaphoreType.DMA((4,))],
+        [],
         (sides, got, far, near),
     )
 
@@ -220,9 +211,11 @@
     wide = with_sides(mid, 3, m)
     totals = [(factor * SCALE / 180.0) * z for z in zs]
     for dist, weight in zip((1, 2, 3), COEFFS):
-        up, down = get(dist), get(-dist)
+        planes = [p for p in (get(dist), get(-dist)) if p is not None]
         for j in range(NV):
-            along = (up[j] + down[j]) + (wide[3 + j + dist] + wide[3 + j - dist])
+            along = wide[3 + j + dist] + wide[3 + j - dist]
+            for p in planes:
+                along = along + p[j]
             totals[j] = totals[j] + (factor * SCALE * weight) * along
     return totals, mid
 
@@ -244,9 +237,23 @@
     return out
 
 
-def weigh_kernel(sides, diel, field, far, near, wts, fs, ds):
+def extended(bricks, o, at):
+    def get(p):
+        return strips(bricks[p // BX], o, at[p % BX])
+
+    return get
+
+
+def prepare_kernel(sides, orb, diel, field, far, near, wts, fs, rest, ds, zp):
     m = Masks()
+    matrix = band_matrix()
+    has_far = sides[0] > 0
     turn = sides[1]
+    at = [turned(turn, p) for p in range(BX)]
+    for o in range(NB):
+        for ref, planes, base in ((far, (3, 4, 5), 0), (orb, range(BX), 3), (near, (0, 1, 2), 3 + BX)):
+            x = jnp.concatenate([ref[o, at[p]] for p in planes], axis=0)
+            zp[o, pl.ds(base, len(planes))] = along_z(x, matrix).reshape(len(planes), NY, NZ)
     for k, (lo, own, hi) in enumerate(((far.at[NB], field, near.at[NB]), (far.at[NB + 1], diel, near.at[NB + 1]))):
         dst = (fs, ds)[k]
 
@@ -257,7 +264,6 @@
             return 0
 
         lax.fori_loop(0, BX, move, 0)
-    has_far = sides[0] > 0
 
     def weigh(i, _):
         keep = (i >= BX - 1) | has_far
@@ -269,34 +275,68 @@
 
     lax.fori_loop(0, 3 * BX - 2, weigh, 0, unroll=2)
 
-
-def weigh(sides, diel, field, far, near):
-    vec = (NV, STRIPS, NZ)
-    return call(
-        weigh_kernel,
-        [(7, 3 * BX - 2, *vec), (3 * BX, *vec)],
-        [SM] + [VM] * 4,
-        [VM, VM],
-        [pltpu.VMEM((3 * BX, *vec), jnp.float32)],
-        (sides, diel, field, far, near),
+    def laplace(o, _):
+        get = extended((far, orb, near), o, at)
+        for j in range(2 * BX):
+            total, _ = stencil(lambda dist: get(j + 3 + dist), strips(zp, o, j), m, 1.0)
+            put_plain(rest, total, o, j)
+        return 0
+
+    lax.fori_loop(0, NB, laplace, 0)
+
+
+def prepare(sides, orb, diel, field, far, near):
+    return call(
+        prepare_kernel,
+        [(7, 3 * BX - 2, *VEC), (3 * BX, *VEC), (NB, 2 * BX, *VEC)],
+        [SM] + [VM] * 5,
+        [VM] * 3,
+        [pltpu.VMEM((3 * BX, *VEC), jnp.float32), pltpu.VMEM((NB, 2 * BX, NY, NZ), jnp.float32)],
+        (sides, orb, diel, field, far, near),
     )
 
 
+def two_steps(sides, orb, far, near, diag, rest, y1, y2, zp, m):
+    has_far = sides[0] > 0
+    turn = sides[1]
+    at = [turned(turn, p) for p in range(BX)]
+    matrix = band_matrix()
+
+    def step_one(i, _):
+        get = extended((far, orb, near), i, at)
+        for j in range(2 * BX):
+            new = [a * b + c for a, b, c in zip(plain(diag, j), get(j + 3), plain(rest, i, j))]
+            if j < 3:
+                new = [jnp.where(has_far, v, 0.0) for v in new]
+            put_plain(y1, new, i, j)
+        return 0
+
+    lax.fori_loop(0, NB, step_one, 0)
+    for i in range(NB):
+        x = y1[i, pl.ds(3, BX)].reshape(BX * NY, NZ)
+        zp[i] = along_z(x, matrix).reshape(BX, *VEC)
+
+    def step_two(j, _):
+        q = plain(diag, j + 3)
+        here = turned(turn, j)
+        for i in range(NB):
+            part, mid = stencil(lambda dist: plain(y1, i, j + 3 + dist), plain(zp, i, j), m, 2.0)
+            old = strips(orb, i, here)
+            put_plain(y2, [2.0 * a * b + (c - d) for a, b, c, d in zip(q, mid, part, old)], i, here)
+        return 0
+
+    lax.fori_loop(0, BX, step_two, 0)
+
+
 def first_kernel(
-    sides, orb, core, far, near, mine, rho_far, rho_near, wts, fs,
-    potential, y1, y2, diag,
+    sides, orb, core, far, near, mine, rho_far, rho_near, wts, fs, rest,
+    potential, diag, y1, y2,
     fa, fb, src, xc, zp,
 ):
     has_far = sides[0] > 0
     turn = sides[1]
     at = [turned(turn, p) for p in range(BX)]
     m = Masks()
-    matrix = band_matrix()
-
-    for o in range(NB):
-        for ref, planes, base in ((far, (3, 4, 5), 0), (orb, range(BX), 3), (near, (0, 1, 2), 3 + BX)):
-            x = jnp.concatenate([ref[o, at[p]] for p in planes], axis=0)
-            zp[o, pl.ds(base, len(planes))] = along_z(x, matrix).reshape(len(planes), NY, NZ)
 
     def sources(ref, lo, hi, base):
         def body(p, _):
@@ -375,97 +415,108 @@
         put_plain(diag, [(v - CENTER) * (1.0 / HALF) + 3.0 * COEFF_ZERO * SCALE for v in new], j)
         return 0
 
-    lax.fori_loop(0, 2 * BX, last_sweep, 0, unroll=2)
+    lax.fori_loop(0, 2 * BX, last_sweep, 0, unroll=4)
 
     def give(p, _):
         put_strips(potential, plain(fa, p + BX), turned(turn, p))
         return 0
 
     lax.fori_loop(0, BX, give, 0, unroll=2)
-
-    def step_one(o, _):
-        def get(p):
-            return strips((far, orb, near)[p // BX], o, at[p % BX])
-
-        for j in range(2 * BX):
-            rest, mid = stencil(lambda dist: get(j + 3 + dist), strips(zp, o, j), m, 1.0)
-            new = [a * b + c for a, b, c in zip(plain(diag, j), mid, rest)]
-            if j < 3:
-                new = [jnp.where(has_far, v, 0.0) for v in new]
-            put_plain(y1, new, o, j)
-        return 0
-
-    lax.fori_loop(0, NB, step_one, 0)
+    two_steps(sides, orb, far, near, diag, rest, y1, y2, zp, m)
+
+
+def first(sides, orb, core, far, near, mine, rho_far, rho_near, wts, fs, rest):
+    f = jnp.float32
+    return call(
+        first_kernel,
+        [(BX, NY, NZ), (2 * BX, *VEC), (NB, 2 * BX, *VEC), (NB, BX, *VEC)],
+        [SM] + [VM] * 10,
+        [VM] * 4,
+        [
+            pltpu.VMEM((3 * BX, *VEC), f),
+            pltpu.VMEM((3 * BX, *VEC), f),
+            pltpu.VMEM((3 * BX - 2, *VEC), f),
+            pltpu.VMEM((2 * BX, *VEC), f),
+            pltpu.VMEM((NB, BX, *VEC), f),
+        ],
+        (sides, orb, core, far, near, mine, rho_far, rho_near, wts, fs, rest),
+    )
+
+
+def own_kernel(y1, y2, diag, turn_in, partial, zp):
+    turn = turn_in[1]
+    at = [turned(turn, p) for p in range(BX)]
+    m = Masks()
+    matrix = band_matrix()
     for o in range(NB):
-        x = y1[o, pl.ds(3, BX)].reshape(BX * NY, NZ)
-        zp[o, pl.ds(0, BX)] = along_z(x, matrix).reshape(BX, NY, NZ)
-
-    def step_two(j, _):
-        q = plain(diag, j + 3)
-        for o in range(NB):
-            zs = [zp[o, j, pl.ds(i * STRIPS, STRIPS), :] for i in range(NV)]
-            rest, mid = stencil(lambda dist: plain(y1, o, j + 3 + dist), zs, m, 2.0)
-            here = turned(turn, j)
-            old = strips(orb, o, here)
-            put_plain(y2, [2.0 * a * b + (c - d) for a, b, c, d in zip(q, mid, rest, old)], o, here)
-        return 0
-
-    lax.fori_loop(0, BX, step_two, 0)
-
-
-def first(sides, orb, core, far, near, mine, rho_far, rho_near, wts, fs):
-    f = jnp.float32
-    vec = (NV, STRIPS, NZ)
-    return call(
-        first_kernel,
-        [(BX, NY, NZ), (NB, 2 * BX, *vec), (NB, BX, *vec), (2 * BX, *vec)],
-        [SM] + [VM] * 9,
-        [VM, VM, VM, VM],
-        [
-            pltpu.VMEM((3 * BX, *vec), f),
-            pltpu.VMEM((3 * BX, *vec), f),
-            pltpu.VMEM((3 * BX - 2, *vec), f),
-            pltpu.VMEM((2 * BX, *vec), f),
-            pltpu.VMEM((NB, 2 * BX, NY, NZ), f),
-        ],
-        (sides, orb, core, far, near, mine, rho_far, rho_near, wts, fs),
-    )
-
-
-def second_kernel(sides, y1, y2, near, far, diag, out, y3, zp, done, sems):
+        x = jnp.concatenate([y2[o, at[p]].reshape(NY, NZ) for p in range(BX)], axis=0)
+        zp[o] = along_z(x, matrix).reshape(BX, *VEC)
+
+    def step_three(o, _):
+        for j in range(BX):
+            part, mid = stencil(
+                lambda dist: plain(y2, o, at[j + dist]) if 0 <= j + dist < BX else None, plain(zp, o, j), m, 2.0
+            )
+            old = plain(y1, o, j + 3)
+            new = [2.0 * a * b + (c - d) for a, b, c, d in zip(plain(diag, j + 3), mid, part, old)]
+            put_plain(partial, new, o, j)
+        return 0
+
+    lax.fori_loop(0, NB, step_three, 0)
+
+
+def own(sides, y1, y2, diag):
+    return call(
+        own_kernel,
+        [(NB, BX, *VEC)],
+        [VM] * 3 + [SM],
+        [VM],
+        [pltpu.VMEM((NB, BX, *VEC), jnp.float32)],
+        (y1, y2, diag, sides),
+    )[0]
+
+
+def last_kernel(sides, y1, y2, near, far, diag, partial, out, y3, zp, done, sems):
     has_far = sides[0] > 0
     turn = sides[1]
     at = [turned(turn, p) for p in range(BX)]
     m = Masks()
     matrix = band_matrix()
     for o in range(NB):
-        for ref, planes, base in ((far, (3, 4, 5), 0), (y2, range(BX), 3), (near, (0, 1, 2), 3 + BX)):
+        for ref, planes, base in ((far, (3, 4, 5), 0), (near, (0, 1, 2), 3)):
             x = jnp.concatenate([ref[o, at[p]].reshape(NY, NZ) for p in planes], axis=0)
-            zp[o, pl.ds(base, len(planes))] = along_z(x, matrix).reshape(len(planes), NV, STRIPS, NZ)
+            zp[o, pl.ds(base, 3)] = along_z(x, matrix).reshape(3, *VEC)
 
     def step_three(o, _):
         def get(p):
             return plain((far, y2, near)[p // BX], o, at[p % BX])
 
-        for j in range(2 * BX):
-            rest, mid = stencil(lambda dist: get(j + 3 + dist), plain(zp, o, j), m, 2.0)
+        for j in (0, 1, 2, BX + 3, BX + 4, BX + 5):
+            part, mid = stencil(lambda dist: get(j + 3 + dist), plain(zp, o, j if j < 3 else j - BX), m, 2.0)
             old = plain(y1, o, j)
-            new = [2.0 * a * b + (c - d) for a, b, c, d in zip(plain(diag, j), mid, rest, old)]
+            new = [2.0 * a * b + (c - d) for a, b, c, d in zip(plain(diag, j), mid, part, old)]
             if j < 3:
                 new = [jnp.where(has_far, v, 0.0) for v in new]
             put_plain(y3, new, o, j)
+        for j in range(BX):
+            new = plain(partial, o, j)
+            for dist, weight in zip((1, 2, 3), COEFFS):
+                for p in (j - dist, j + dist):
+                    if not 0 <= p < BX:
+                        new = [a + (2.0 * SCALE * weight) * b for a, b in zip(new, get(p + BX))]
+            put_plain(y3, new, o, j + 3)
         return 0
 
     lax.fori_loop(0, NB, step_three, 0)
     for o in range(NB):
         x = y3[o, pl.ds(3, BX)].reshape(BX * NY, NZ)
-        zp[o, pl.ds(0, BX)] = along_z(x, matrix).reshape(BX, NV, STRIPS, NZ)
+        zp[o] = along_z(x, matrix).reshape(BX, *VEC)
 
     def step_four(o, _):
         for j in range(BX):
-            rest, mid = stencil(lambda dist: plain(y3, o, j + 3 + dist), plain(zp, o, j), m, 2.0)
+            part, mid = stencil(lambda dist: plain(y3, o, j + 3 + dist), plain(zp, o, j), m, 2.0)
             old = plain(y2, o, at[j])
-            new = [2.0 * a * b + (c - d) for a, b, c, d in zip(plain(diag, j + 3), mid, rest, old)]
+            new = [2.0 * a * b + (c - d) for a, b, c, d in zip(plain(diag, j + 3), mid, part, old)]
             put_strips(done, new, o, at[j])
         pltpu.make_async_copy(done.at[o], out.at[o], sems.at[o]).start()
         return 0
@@ -475,30 +526,31 @@
         pltpu.make_async_copy(done.at[o], out.at[o], sems.at[o]).wait()
 
 
-def second(sides, y1, y2, far, near, diag):
+def last(sides, y1, y2, near, far, diag, partial):
     f = jnp.float32
-    vec = (NV, STRIPS, NZ)
-    return call(
-        second_kernel,
+    return call(
+        last_kernel,
         [(NB, BX, NY, NZ)],
-        [SM] + [VM] * 5,
-        [ANY],
+        [SM] + [VM] * 6,
+        [HBM],
         [
-            pltpu.VMEM((NB, 2 * BX, *vec), f),
-            pltpu.VMEM((NB, 2 * BX, *vec), f),
+            pltpu.VMEM((NB, 2 * BX, *VEC), f),
+            pltpu.VMEM((NB, BX, *VEC), f),
             pltpu.VMEM((NB, BX, NY, NZ), f),
             pltpu.SemaphoreType.DMA((NB,)),
         ],
-        (sides, y1, y2, near, far, diag),
+        (sides, y1, y2, near, far, diag, partial),
     )[0]
 
 
-def swapped(to_far, to_near):
+def swap_far(x):
     n = lax.axis_size("dom")
-    pairs = [(i, i + 1) for i in range(n - 1)]
-    far = [p for i, j in pairs if i % 2 for p in ((i, j), (j, i))]
-    near = [p for i, j in pairs if i % 2 == 0 for p in ((i, j), (j, i))]
-    return lax.ppermute(to_far, "dom", far), lax.ppermute(to_near, "dom", near)
+    return lax.ppermute(x, "dom", [p for i in range(1, n - 1, 2) for p in ((i, i + 1), (i + 1, i))])
+
+
+def swap_near(x):
+    n = lax.axis_size("dom")
+    return lax.ppermute(x, "dom", [p for i in range(0, n - 1, 2) for p in ((i, i + 1), (i + 1, i))])
 
 
 def local(orbitals, occupation, dielectric, core_density, start_field):
@@ -511,24 +563,26 @@
     sides = jnp.stack([has_far.astype(jnp.int32), turn.astype(jnp.int32)])
 
     parts = density(half, occupation, orbitals)
+    held, parts = lax.optimization_barrier(((orbitals, start_field, dielectric, core_density), parts))
+    packed = pack(*held)
     parts = lax.all_to_all(parts, "band", 0, 0, axis_index_groups=groups)
     mine = jnp.sum(parts, axis=0)
+    mine, packed = lax.optimization_barrier((mine, packed))
     other = lax.ppermute(mine, "band", [(i, (i + half) % bands) for i in range(bands)])
-    held, mine = lax.optimization_barrier(((orbitals, start_field, dielectric, core_density), mine))
-    packed = pack(*held)
-    far, near = swapped(packed, packed)
+    far, near = swap_far(packed), swap_near(packed)
     got = lax.all_to_all(spread(half, mine, other), "band", 0, 0, axis_index_groups=groups)
-    to_near, to_far = join(half, sides, got, near, far)
-    rho_far, rho_near = swapped(to_far, to_near)
+    to_near, to_far = join(half, sides, got, far, near)
+    rho_far, rho_near = swap_far(to_far), swap_near(to_near)
     (far, near), to_near = lax.optimization_barrier(((far, near), to_near))
-    wts, fs = weigh(sides, dielectric, start_field, far, near)
+    wts, fs, rest = prepare(sides, orbitals, dielectric, start_field, far, near)
     cells = (-1, NY, NZ)
-    potential, y1, y2, diag = first(
+    potential, diag, y1, y2 = first(
         sides, orbitals, core_density, far, near,
-        to_near.reshape(cells), rho_far.reshape(cells), rho_near.reshape(cells), wts, fs,
+        to_near.reshape(cells), rho_far.reshape(cells), rho_near.reshape(cells), wts, fs, rest,
     )
-    y2_far, y2_near = swapped(y2, y2)
-    return potential, second(sides, y1, y2, y2_far, y2_near, diag)
+    y2_far, y2_near = swap_far(y2), swap_near(y2)
+    partial = own(sides, y1, y2, diag)
+    return potential, last(sides, y1, y2, y2_near, y2_far, diag, partial)
 
 
 def solution(mesh):

time: 86.8 us -> 82.5 us (0.950)
  blocking collectives: 18.2 us -> 0 us
  starting transfers between devices: 27.4 us -> 38 us
  waiting for transfers between devices: 23.1 us -> 25.9 us
    all_to_all x1 -> x0, blocking collectives: 18.2 us -> none  [local(): parts = lax.all_to_all(parts, 'band', 0, 0, axis_index_groups=groups)]
    all_to_all x0 -> x1, starting transfers between devices: none -> 10 us  [local(): parts = lax.all_to_all(parts, 'band', 0, 0, axis_index_groups=groups)]
    all_to_all x0 -> x1, waiting for transfers between devices: none -> 5.95 us  [local(): parts = lax.all_to_all(parts, 'band', 0, 0, axis_index_groups=groups)]
    ppermute x6, waiting for transfers between devices: 15 us -> 11.8 us  [the longest x3 11.8 us: swap_far(): lax.ppermute(x, 'dom', [p for i in range(1, n - 1, 2) for p in ((i, i + 1...]
    pallas_call x7 -> x8, Pallas kernels: 16.7 us -> 17.2 us  [call(): pl.pallas_call(kernel, out_shape=[jax.ShapeDtypeStruct(s, jnp.float32) fo...]
  transfers between devices with their start and end apart: 8 -> 9, of which waited for: 4 -> 5; matrix products, arithmetic and copies ran while one was open for 0% -> 0% of each run, Pallas kernels for 5% -> 8%
where the time goes in v4:
time: 82.5 us; the launch traced here: 82 us
  starting transfers between devices  38 us (46%)
  waiting for transfers between devices  25.9 us (31%)
  Pallas kernels  17.2 us (21%)
    pallas_call x8, Pallas kernels, call(): pl.pallas_call(kernel, out_shape=[jax.ShapeDtypeStruct(s, jnp.float32) fo...  17.2 us
    ppermute x3, waiting for transfers between devices, swap_far(): lax.ppermute(x, 'dom', [p for i in range(1, n - 1, 2) for p in ((i, i + 1...  11.8 us
    all_to_all x1, starting transfers between devices, local(): parts = lax.all_to_all(parts, 'band', 0, 0, axis_index_groups=groups)  10 us
    ppermute x3, starting transfers between devices, swap_near(): lax.ppermute(x, 'dom', [p for i in range(0, n - 1, 2) for p in ((i, i + 1...  8.74 us
    ppermute x3, starting transfers between devices, swap_far(): lax.ppermute(x, 'dom', [p for i in range(1, n - 1, 2) for p in ((i, i + 1...  8.4 us
    all_to_all x1, waiting for transfers between devices, local(): lax.all_to_all(spread(half, mine, other), 'band', 0, 0, axis_index_groups...  8.11 us
    ppermute x1, starting transfers between devices, local(): lax.ppermute(mine, 'band', [(i, (i + half) % bands) for i in range(bands)])  7.45 us
    all_to_all x1, waiting for transfers between devices, local(): parts = lax.all_to_all(parts, 'band', 0, 0, axis_index_groups=groups)  5.95 us
  transfers between devices with their start and end apart: 9, of which 5 were waited for; matrix products, arithmetic and copies ran while one was open for 0% of the time, Pallas kernels for 8%

profile of v4, /device:TPU:7, one launch (start us, length us, event | category | flops | bytes accessed | tf_op | source)
XLA Modules:
  0.0 82.0 jit_solution(10917603264943237199)
XLA Ops:
  0.6 1.8 %shard_map.68 = f32[8,36,128]{2,1,0:T(8,128)} custom-call(f32[4]{0:T(128)} %refs_0_.1, f32[4,6,48,128]{3,2,1,0:T(8,128)} %orb.4), custom_call_target="tpu_custom_call" | custom-call | flops 2000000000 | bytes 2000000 | tf_op jit(solution)/shard_map/pallas_call | solution.py:35
  2.5 10.0 %all-to-all-start = ((f32[8,36,128]{2,1,0:T(8,128)}), f32[8,36,128]{2,1,0:T(8,128)S(1)}, u32[]{:S(2)}, u32[]{:S(2)}) async-start(f32[8,36,128]{2,1,0:T(8,128)} %shard_map.68), calls=%async_computation | async-start | bytes 327680 | tf_op jit(solution)/shard_map/all_to_all | solution.py:568
  12.5 2.2 %shard_map.69 = f32[7,6,48,128]{3,2,1,0:T(8,128)} custom-call(f32[4,6,48,128]{3,2,1,0:T(8,128)} %orb.4, f32[6,48,128]{2,1,0:T(8,128)} %field.2, f32[6,48,128]{2,1,0:T(8,128)} %diel.2, f32[6,48,128]{2,1,0:T(8,128)} %core.2), custom_call_target="tpu_custom_call" | custom-call | flops 20000000000 | bytes 20000000 | tf_op jit(solution)/shard_map/pallas_call | solution.py:35
  14.7 5.9 %all-to-all-done = f32[8,36,128]{2,1,0:T(8,128)S(1)} async-done(((f32[8,36,128]{2,1,0:T(8,128)}), f32[8,36,128]{2,1,0:T(8,128)S(1)}, u32[]{:S(2)}, u32[]{:S(2)}) %all-to-all-start) | async-done | bytes 147488 | tf_op jit(solution)/shard_map/all_to_all | solution.py:568
  20.7 7.5 %collective-permute-start.2 = (f32[36,128]{1,0:T(8,128)S(1)}, f32[36,128]{1,0:T(8,128)S(1)}, u32[]{:S(2)}, u32[]{:S(2)}) collective-permute-start(f32[36,128]{1,0:T(8,128)S(1)} %reduce_sum.9.mine), channel_id=1, source_target_pairs={{0,256},{32,288},{64,320},{96,352},{128,384},{160,416},{192,448},{... | collective-permute-start | bytes 55304 | tf_op jit(solution)/shard_map/ppermute | solution.py:571
  28.1 4.8 %collective-permute-start.1 = (f32[7,6,48,128]{3,2,1,0:T(8,128)}, f32[7,6,48,128]{3,2,1,0:T(8,128)S(1)}, u32[]{:S(2)}, u32[]{:S(2)}) collective-permute-start(f32[7,6,48,128]{3,2,1,0:T(8,128)} %shard_map.69), channel_id=1, source_target_pairs={{0,1},{1,0},{2,3},{3,2},{4,5},{5,4},{6,7},{7,6},{8,9},{9,8},{10,11... | collective-permute-start | bytes 3096584 | tf_op jit(solution)/shard_map/ppermute | solution.py:553
  32.9 2.1 %collective-permute-start = (f32[7,6,48,128]{3,2,1,0:T(8,128)}, f32[7,6,48,128]{3,2,1,0:T(8,128)S(1)}, u32[]{:S(2)}, u32[]{:S(2)}) collective-permute-start(f32[7,6,48,128]{3,2,1,0:T(8,128)} %shard_map.69), channel_id=1, source_target_pairs={{1,2},{2,1},{3,4},{4,3},{5,6},{6,5},{7,8},{8,7},{9,10},{10,9},{11,... | collective-permute-start | bytes 3096584 | tf_op jit(solution)/shard_map/ppermute | solution.py:548
  35.0 0.0 collective-permute-done.2.other
  35.1 0.7 shard_map.70
  35.7 3.4 %all-to-all-start.1 = ((f32[8,36,128]{2,1,0:T(8,128)}), f32[8,36,128]{2,1,0:T(8,128)S(1)}, u32[]{:S(2)}, u32[]{:S(2)}) async-start(f32[8,36,128]{2,1,0:T(8,128)} %shard_map.70), calls=%async_computation.1 | async-start | bytes 327680 | tf_op jit(solution)/shard_map/all_to_all | solution.py:573
  39.1 0.1 pad_add_fusion.refs_0_.sides.turn_in
  39.2 8.1 %all-to-all-done.1.refs_1_ = f32[8,36,128]{2,1,0:T(8,128)S(1)} async-done(((f32[8,36,128]{2,1,0:T(8,128)}), f32[8,36,128]{2,1,0:T(8,128)S(1)}, u32[]{:S(2)}, u32[]{:S(2)}) %all-to-all-start.1) | async-done | bytes 147488 | tf_op jit(solution)/shard_map/all_to_all | solution.py:573
  47.3 0.0 collective-permute-done.1.refs_2_.near
  47.3 3.8 %collective-permute-done.refs_3_.far = f32[7,6,48,128]{3,2,1,0:T(8,128)S(1)} collective-permute-done((f32[7,6,48,128]{3,2,1,0:T(8,128)}, f32[7,6,48,128]{3,2,1,0:T(8,128)S(1)}, u32[]{:S(2)}, u32[]{:S(2)}) %collective-permute-start) | collective-permute-done | bytes 1032224 | tf_op jit(solution)/shard_map/ppermute | solution.py:548
  51.2 0.6 shard_map.71
  51.8 2.8 %collective-permute-start.3 = (f32[384,128]{1,0:T(8,128)S(1)}, f32[384,128]{1,0:T(8,128)S(1)}, u32[]{:S(2)}, u32[]{:S(2)}) collective-permute-start(f32[384,128]{1,0:T(8,128)S(1)} %get-tuple-element.32), channel_id=1, source_target_pairs={{1,2},{2,1},{3,4},{4,3},{5,6},{6,5},{7,8},{8,7},{9,10},{10,9},{11,... | collective-permute-start | bytes 589832 | tf_op jit(solution)/shard_map/ppermute | solution.py:548
  54.6 0.0 copy-start.1
  54.6 2.1 %collective-permute-start.4 = (f32[384,128]{1,0:T(8,128)S(1)}, f32[384,128]{1,0:T(8,128)S(1)}, u32[]{:S(2)}, u32[]{:S(2)}) collective-permute-start(f32[384,128]{1,0:T(8,128)S(1)} %get-tuple-element.31), channel_id=1, source_target_pairs={{0,1},{1,0},{2,3},{3,2},{4,5},{5,4},{6,7},{7,6},{8,9},{9,8},{10,11... | collective-permute-start | bytes 589832 | tf_op jit(solution)/shard_map/ppermute | solution.py:553
  56.7 0.0 copy-done
  56.7 0.0 copy-done.2
  56.7 0.0 copy-done.3
  56.7 2.7 %shard_map.72 = (f32[7,16,6,8,128]{4,3,2,1,0:T(8,128)S(1)}, f32[18,6,8,128]{3,2,1,0:T(8,128)S(1)}, f32[4,12,6,8,128]{4,3,2,1,0:T(8,128)S(1)}) custom-call(s32[2]{0:T(128)S(1)} %pad_add_fusion.refs_0_.sides.turn_in, f32[4,6,48,128]{3,2,1,0:T(8,128)S(1)} %copy-done, f32[6,48,128]{2,1,0:T(8,128)S(1)} %copy-done.3, f32[6,48,128]{2,1,0:T(8,128)S(1)} %copy-done.2, ...), custom_call_target="tpu_custom_call" | custom-call | flops 2000000000 | bytes 2000000 | tf_op jit(solution)/shard_map/pallas_call | solution.py:35
  59.5 1.4 %collective-permute-done.3 = f32[384,128]{1,0:T(8,128)S(1)} collective-permute-done((f32[384,128]{1,0:T(8,128)S(1)}, f32[384,128]{1,0:T(8,128)S(1)}, u32[]{:S(2)}, u32[]{:S(2)}) %collective-permute-start.3) | collective-permute-done | bytes 196640 | tf_op jit(solution)/shard_map/ppermute | solution.py:548
  60.9 0.0 collective-permute-done.4
  60.9 0.0 copy-done.1
  60.9 4.9 %shard_map.73 = (f32[6,48,128]{2,1,0:T(8,128)}, f32[12,6,8,128]{3,2,1,0:T(8,128)S(1)}, f32[4,12,6,8,128]{4,3,2,1,0:T(8,128)S(1)}, f32[4,6,6,8,128]{4,3,2,1,0:T(8,128)S(1)}) custom-call(s32[2]{0:T(128)S(1)} %pad_add_fusion.refs_0_.sides.turn_in, f32[4,6,48,128]{3,2,1,0:T(8,128)S(1)} %copy-done, f32[6,48,128]{2,1,0:T(8,128)S(1)} %copy-done.1, ...), custom_call_target="tpu_custom_call" | custom-call | flops 2000000000 | bytes 2000000 | tf_op jit(solution)/shard_map/pallas_call | solution.py:35
  65.7 3.4 %collective-permute-start.6 = (f32[4,6,6,8,128]{4,3,2,1,0:T(8,128)S(1)}, f32[4,6,6,8,128]{4,3,2,1,0:T(8,128)S(1)}, u32[]{:S(2)}, u32[]{:S(2)}) collective-permute-start(f32[4,6,6,8,128]{4,3,2,1,0:T(8,128)S(1)} %get-tuple-element.38.y2), channel_id=1, source_target_pairs={{1,2},{2,1},{3,4},{4,3},{5,6},{6,5},{7,8},{8,7},{9,10},{10,9},{11,... | collective-permute-start | bytes 1769480 | tf_op jit(solution)/shard_map/ppermute | solution.py:548
  69.2 1.9 %collective-permute-start.5 = (f32[4,6,6,8,128]{4,3,2,1,0:T(8,128)S(1)}, f32[4,6,6,8,128]{4,3,2,1,0:T(8,128)S(1)}, u32[]{:S(2)}, u32[]{:S(2)}) collective-permute-start(f32[4,6,6,8,128]{4,3,2,1,0:T(8,128)S(1)} %get-tuple-element.38.y2), channel_id=1, source_target_pairs={{0,1},{1,0},{2,3},{3,2},{4,5},{5,4},{6,7},{7,6},{8,9},{9,8},{10,11... | collective-permute-start | bytes 1769480 | tf_op jit(solution)/shard_map/ppermute | solution.py:553
  71.1 1.3 %shard_map.74.partial = f32[4,6,6,8,128]{4,3,2,1,0:T(8,128)S(1)} custom-call(f32[4,12,6,8,128]{4,3,2,1,0:T(8,128)S(1)} %get-tuple-element.37.y1, f32[4,6,6,8,128]{4,3,2,1,0:T(8,128)S(1)} %get-tuple-element.38.y2, f32[12,6,8,128]{3,2,1,0:T(8,128)S(1)} %get-tuple-element.39.diag, s32[2]{0:T(128)S(1)} %pad_add_fusion.refs_0_.sides.turn_in), custom_call_target="tpu_custom_call" | custom-call | flops 2000000000 | bytes 2000000 | tf_op jit(solution)/shard_map/pallas_call | solution.py:35
  72.4 6.6 %collective-permute-done.6.far = f32[4,6,6,8,128]{4,3,2,1,0:T(8,128)S(1)} collective-permute-done((f32[4,6,6,8,128]{4,3,2,1,0:T(8,128)S(1)}, f32[4,6,6,8,128]{4,3,2,1,0:T(8,128)S(1)}, u32[]{:S(2)}, u32[]{:S(2)}) %collective-permute-start.6) | collective-permute-done | bytes 589856 | tf_op jit(solution)/shard_map/ppermute | solution.py:548
  79.0 0.0 collective-permute-done.5.near
  79.0 3.0 %shard_map.75 = f32[4,6,48,128]{3,2,1,0:T(8,128)} custom-call(s32[2]{0:T(128)S(1)} %pad_add_fusion.refs_0_.sides.turn_in, f32[4,12,6,8,128]{4,3,2,1,0:T(8,128)S(1)} %get-tuple-element.37.y1, f32[4,6,6,8,128]{4,3,2,1,0:T(8,128)S(1)} %get-tuple-element.38.y2, f32[4,6,6,8,128]{4,3,2,1,0:T(8,128)S(1)} %collective-permute-done.5.near, ...), custom_call_target="tpu_custom_call" | custom-call | flops 2000000000 | bytes 2000000 | tf_op jit(solution)/shard_map/pallas_call | solution.py:35
  (4 shorter events, 0.0 us)
Async XLA Ops:
  2.5 18.2 %all-to-all-start = ((f32[8,36,128]{2,1,0:T(8,128)}), f32[8,36,128]{2,1,0:T(8,128)S(1)}, u32[]{:S(2)}, u32[]{:S(2)}) async-start(f32[8,36,128]{2,1,0:T(8,128)} %shard_map.68), calls=%async_computation | async-start | bytes 327680 | tf_op jit(solution)/shard_map/all_to_all | solution.py:568
  20.7 14.4 %collective-permute-start.2 = (f32[36,128]{1,0:T(8,128)S(1)}, f32[36,128]{1,0:T(8,128)S(1)}, u32[]{:S(2)}, u32[]{:S(2)}) collective-permute-start(f32[36,128]{1,0:T(8,128)S(1)} %reduce_sum.9.mine), channel_id=1, source_target_pairs={{0,256},{32,288},{64,320},{96,352},{128,384},{160,416},{192,448},{... | collective-permute-start | bytes 55304 | tf_op jit(solution)/shard_map/ppermute | solution.py:571
  28.1 19.2 %collective-permute-start.1 = (f32[7,6,48,128]{3,2,1,0:T(8,128)}, f32[7,6,48,128]{3,2,1,0:T(8,128)S(1)}, u32[]{:S(2)}, u32[]{:S(2)}) collective-permute-start(f32[7,6,48,128]{3,2,1,0:T(8,128)} %shard_map.69), channel_id=1, source_target_pairs={{0,1},{1,0},{2,3},{3,2},{4,5},{5,4},{6,7},{7,6},{8,9},{9,8},{10,11... | collective-permute-start | bytes 3096584 | tf_op jit(solution)/shard_map/ppermute | solution.py:553
  32.9 18.3 %collective-permute-start = (f32[7,6,48,128]{3,2,1,0:T(8,128)}, f32[7,6,48,128]{3,2,1,0:T(8,128)S(1)}, u32[]{:S(2)}, u32[]{:S(2)}) collective-permute-start(f32[7,6,48,128]{3,2,1,0:T(8,128)} %shard_map.69), channel_id=1, source_target_pairs={{1,2},{2,1},{3,4},{4,3},{5,6},{6,5},{7,8},{8,7},{9,10},{10,9},{11,... | collective-permute-start | bytes 3096584 | tf_op jit(solution)/shard_map/ppermute | solution.py:548
  35.7 11.6 %all-to-all-start.1 = ((f32[8,36,128]{2,1,0:T(8,128)}), f32[8,36,128]{2,1,0:T(8,128)S(1)}, u32[]{:S(2)}, u32[]{:S(2)}) async-start(f32[8,36,128]{2,1,0:T(8,128)} %shard_map.70), calls=%async_computation.1 | async-start | bytes 327680 | tf_op jit(solution)/shard_map/all_to_all | solution.py:573
  39.2 17.5 %copy-start = (f32[4,6,48,128]{3,2,1,0:T(8,128)S(1)}, f32[4,6,48,128]{3,2,1,0:T(8,128)}, u32[]{:S(2)}) copy-start(f32[4,6,48,128]{3,2,1,0:T(8,128)} %orb.4) | copy-start | bytes 1769476
  39.2 17.5 %copy-start.2 = (f32[6,48,128]{2,1,0:T(8,128)S(1)}, f32[6,48,128]{2,1,0:T(8,128)}, u32[]{:S(2)}) copy-start(f32[6,48,128]{2,1,0:T(8,128)} %field.2) | copy-start | bytes 442372
  39.2 17.5 %copy-start.3 = (f32[6,48,128]{2,1,0:T(8,128)S(1)}, f32[6,48,128]{2,1,0:T(8,128)}, u32[]{:S(2)}) copy-start(f32[6,48,128]{2,1,0:T(8,128)} %diel.2) | copy-start | bytes 442372
  51.8 9.1 %collective-permute-start.3 = (f32[384,128]{1,0:T(8,128)S(1)}, f32[384,128]{1,0:T(8,128)S(1)}, u32[]{:S(2)}, u32[]{:S(2)}) collective-permute-start(f32[384,128]{1,0:T(8,128)S(1)} %get-tuple-element.32), channel_id=1, source_target_pairs={{1,2},{2,1},{3,4},{4,3},{5,6},{6,5},{7,8},{8,7},{9,10},{10,9},{11,... | collective-permute-start | bytes 589832 | tf_op jit(solution)/shard_map/ppermute | solution.py:548
  54.6 6.3 %copy-start.1 = (f32[6,48,128]{2,1,0:T(8,128)S(1)}, f32[6,48,128]{2,1,0:T(8,128)}, u32[]{:S(2)}) copy-start(f32[6,48,128]{2,1,0:T(8,128)} %core.2) | copy-start | bytes 442372
  54.6 6.2 %collective-permute-start.4 = (f32[384,128]{1,0:T(8,128)S(1)}, f32[384,128]{1,0:T(8,128)S(1)}, u32[]{:S(2)}, u32[]{:S(2)}) collective-permute-start(f32[384,128]{1,0:T(8,128)S(1)} %get-tuple-element.31), channel_id=1, source_target_pairs={{0,1},{1,0},{2,3},{3,2},{4,5},{5,4},{6,7},{7,6},{8,9},{9,8},{10,11... | collective-permute-start | bytes 589832 | tf_op jit(solution)/shard_map/ppermute | solution.py:553
  65.7 13.3 %collective-permute-start.6 = (f32[4,6,6,8,128]{4,3,2,1,0:T(8,128)S(1)}, f32[4,6,6,8,128]{4,3,2,1,0:T(8,128)S(1)}, u32[]{:S(2)}, u32[]{:S(2)}) collective-permute-start(f32[4,6,6,8,128]{4,3,2,1,0:T(8,128)S(1)} %get-tuple-element.38.y2), channel_id=1, source_target_pairs={{1,2},{2,1},{3,4},{4,3},{5,6},{6,5},{7,8},{8,7},{9,10},{10,9},{11,... | collective-permute-start | bytes 1769480 | tf_op jit(solution)/shard_map/ppermute | solution.py:548
  69.2 9.9 %collective-permute-start.5 = (f32[4,6,6,8,128]{4,3,2,1,0:T(8,128)S(1)}, f32[4,6,6,8,128]{4,3,2,1,0:T(8,128)S(1)}, u32[]{:S(2)}, u32[]{:S(2)}) collective-permute-start(f32[4,6,6,8,128]{4,3,2,1,0:T(8,128)S(1)} %get-tuple-element.38.y2), channel_id=1, source_target_pairs={{0,1},{1,0},{2,3},{3,2},{4,5},{5,4},{6,7},{7,6},{8,9},{9,8},{10,11... | collective-permute-start | bytes 1769480 | tf_op jit(solution)/shard_map/ppermute | solution.py:553

commit v5 on v4

--- a/solution.py
+++ b/solution.py
@@ -44,13 +44,19 @@
     )(*args)
 
 
-def density_kernel(chunks, occ_in, orb, parts, occ, u, dens, sems):
+def density_kernel(chunks, occ_in, orb, parts, occ, u, dens, held, sems):
     size = ROWS // chunks
-    loads = [pltpu.make_async_copy(occ_in, occ, sems.at[0]), pltpu.make_async_copy(orb, u, sems.at[1])]
-    for c in loads:
-        c.start()
-    for c in loads:
-        c.wait()
+    load_occ = pltpu.make_async_copy(occ_in, occ, sems.at[0])
+    load_occ.start()
+    half = BX // 2
+    loads, saves = [], []
+    for h in range(2):
+        planes = pl.ds(h * half, half)
+        loads.append(pltpu.make_async_copy(orb.at[:, planes], u.at[:, planes], sems.at[1 + h]))
+        loads[h].start()
+        some = pl.ds(h * chunks // 2, chunks // 2)
+        saves.append(pltpu.make_async_copy(held.at[some], parts.at[some], sems.at[3 + h]))
+    load_occ.wait()
 
     def plane(p, _):
         total = occ[0] * u[0, p] * u[0, p]
@@ -59,9 +65,14 @@
         dens[pl.ds(pl.multiple_of(p * NY, NY), NY), :] = total
         return 0
 
-    lax.fori_loop(0, BX, plane, 0, unroll=2)
-    for c in range(chunks):
-        parts[c] = dens[pl.ds(c * size, size), :]
+    for h in range(2):
+        loads[h].wait()
+        lax.fori_loop(h * half, (h + 1) * half, plane, 0, unroll=True)
+        for c in range(h * chunks // 2, (h + 1) * chunks // 2):
+            held[c] = dens[pl.ds(c * size, size), :]
+        saves[h].start()
+    for c in saves:
+        c.wait()
 
 
 def density(chunks, occ, orb):
@@ -72,12 +83,13 @@
         kernel,
         [(chunks, ROWS // chunks, NZ)],
         [HBM, HBM],
-        [VM],
+        [HBM],
         [
             pltpu.SMEM((NB,), jnp.float32),
             pltpu.VMEM((NB, BX, NY, NZ), jnp.float32),
             pltpu.VMEM((ROWS, NZ), jnp.float32),
-            pltpu.SemaphoreType.DMA((2,)),
+            pltpu.VMEM((chunks, ROWS // chunks, NZ), jnp.float32),
+            pltpu.SemaphoreType.DMA((5,)),
         ],
         (occ, orb),
         vmem=VMEM_ALL,
@@ -273,7 +285,7 @@
                 wts[k, i, j] = got[j][k]
         return 0
 
-    lax.fori_loop(0, 3 * BX - 2, weigh, 0, unroll=2)
+    lax.fori_loop(0, 3 * BX - 2, weigh, 0, unroll=4)
 
     def laplace(o, _):
         get = extended((far, orb, near), o, at)
@@ -325,13 +337,13 @@
             put_plain(y2, [2.0 * a * b + (c - d) for a, b, c, d in zip(q, mid, part, old)], i, here)
         return 0
 
-    lax.fori_loop(0, BX, step_two, 0)
+    lax.fori_loop(0, BX, step_two, 0, unroll=2)
 
 
 def first_kernel(
     sides, orb, core, far, near, mine, rho_far, rho_near, wts, fs, rest,
     potential, diag, y1, y2,
-    fa, fb, src, xc, zp,
+    fa, fb, src, xc, zp, pot, sem,
 ):
     has_far = sides[0] > 0
     turn = sides[1]
@@ -345,7 +357,7 @@
                 src[i, j] = wts[6, i, j] * v
             return 0
 
-        lax.fori_loop(lo, hi, body, 0)
+        lax.fori_loop(lo, hi, body, 0, unroll=True)
 
     sources(rho_far, 1, BX, -1)
     sources(mine, 0, BX, BX - 1)
@@ -362,7 +374,7 @@
                 xc[p + base, j] = SLATER * root
             return 0
 
-        lax.fori_loop(0, count, body, 0)
+        lax.fori_loop(0, count, body, 0, unroll=3)
 
     exchange(rho_far, far.at[NB + 2], BX - 3, 3, 0)
     exchange(mine, core, 0, BX, 3)
@@ -399,7 +411,7 @@
             put_plain(dst, new, e)
             return 0
 
-        lax.fori_loop(margin, 3 * BX - margin, body, 0, unroll=4)
+        lax.fori_loop(margin, 3 * BX - margin, body, 0, unroll=8)
 
     sweep(fs, fb, 1)
     sweep(fb, fa, 1)
@@ -415,14 +427,17 @@
         put_plain(diag, [(v - CENTER) * (1.0 / HALF) + 3.0 * COEFF_ZERO * SCALE for v in new], j)
         return 0
 
-    lax.fori_loop(0, 2 * BX, last_sweep, 0, unroll=4)
+    lax.fori_loop(0, 2 * BX, last_sweep, 0, unroll=6)
 
     def give(p, _):
-        put_strips(potential, plain(fa, p + BX), turned(turn, p))
+        put_strips(pot, plain(fa, p + BX), turned(turn, p))
         return 0
 
     lax.fori_loop(0, BX, give, 0, unroll=2)
+    save = pltpu.make_async_copy(pot, potential, sem.at[0])
+    save.start()
     two_steps(sides, orb, far, near, diag, rest, y1, y2, zp, m)
+    save.wait()
 
 
 def first(sides, orb, core, far, near, mine, rho_far, rho_near, wts, fs, rest):
@@ -431,13 +446,15 @@
         first_kernel,
         [(BX, NY, NZ), (2 * BX, *VEC), (NB, 2 * BX, *VEC), (NB, BX, *VEC)],
         [SM] + [VM] * 10,
-        [VM] * 4,
+        [HBM] + [VM] * 3,
         [
             pltpu.VMEM((3 * BX, *VEC), f),
             pltpu.VMEM((3 * BX, *VEC), f),
             pltpu.VMEM((3 * BX - 2, *VEC), f),
             pltpu.VMEM((2 * BX, *VEC), f),
             pltpu.VMEM((NB, BX, *VEC), f),
+            pltpu.VMEM((BX, NY, NZ), f),
+            pltpu.SemaphoreType.DMA((1,)),
         ],
         (sides, orb, core, far, near, mine, rho_far, rho_near, wts, fs, rest),
     )
@@ -573,7 +590,7 @@
     got = lax.all_to_all(spread(half, mine, other), "band", 0, 0, axis_index_groups=groups)
     to_near, to_far = join(half, sides, got, far, near)
     rho_far, rho_near = swap_far(to_far), swap_near(to_near)
-    (far, near), to_near = lax.optimization_barrier(((far, near), to_near))
+    (near, far), to_near = lax.optimization_barrier(((near, far), to_near))
     wts, fs, rest = prepare(sides, orbitals, dielectric, start_field, far, near)
     cells = (-1, NY, NZ)
     potential, diag, y1, y2 = first(

time: 82.5 us -> 79.4 us (0.962); the launches traced: 82 us -> 78 us
  waiting for transfers between devices: 25.9 us -> 20.2 us
  starting transfers between devices: 38 us -> 41 us
  Pallas kernels: 17.2 us -> 15.8 us
    ppermute x3, waiting for transfers between devices: 11.8 us -> 5.55 us  [swap_far(): lax.ppermute(x, 'dom', [p for i in range(1, n - 1, 2) for p in ((i, i + 1...]
    ppermute x3, starting transfers between devices: 8.4 us -> 14.3 us  [swap_far(): lax.ppermute(x, 'dom', [p for i in range(1, n - 1, 2) for p in ((i, i + 1...]
    ppermute x3, starting transfers between devices: 8.74 us -> 5.89 us  [swap_near(): lax.ppermute(x, 'dom', [p for i in range(0, n - 1, 2) for p in ((i, i + 1...]
    pallas_call x8, Pallas kernels: 17.2 us -> 15.8 us  [call(): pl.pallas_call(kernel, out_shape=[jax.ShapeDtypeStruct(s, jnp.float32) fo...]
  transfers between devices with their start and end apart: 9 -> 9, of which waited for: 5 -> 3; matrix products, arithmetic and copies ran while one was open for 0% -> 0% of each run, Pallas kernels for 8% -> 9%
where the time goes in v5:
time: 79.4 us; the launch traced here: 78 us
  starting transfers between devices  41 us (52%)
  waiting for transfers between devices  20.2 us (25%)
  Pallas kernels  15.8 us (20%)
  between operations  0.83 us (1%)
    pallas_call x8, Pallas kernels, call(): pl.pallas_call(kernel, out_shape=[jax.ShapeDtypeStruct(s, jnp.float32) fo...  15.8 us
    ppermute x3, starting transfers between devices, swap_far(): lax.ppermute(x, 'dom', [p for i in range(1, n - 1, 2) for p in ((i, i + 1...  14.3 us
    all_to_all x1, starting transfers between devices, local(): parts = lax.all_to_all(parts, 'band', 0, 0, axis_index_groups=groups)  10 us
    all_to_all x1, waiting for transfers between devices, local(): lax.all_to_all(spread(half, mine, other), 'band', 0, 0, axis_index_groups...  8.73 us
    ppermute x1, starting transfers between devices, local(): lax.ppermute(mine, 'band', [(i, (i + half) % bands) for i in range(bands)])  7.45 us
    all_to_all x1, waiting for transfers between devices, local(): parts = lax.all_to_all(parts, 'band', 0, 0, axis_index_groups=groups)  5.95 us
    ppermute x3, starting transfers between devices, swap_near(): lax.ppermute(x, 'dom', [p for i in range(0, n - 1, 2) for p in ((i, i + 1...  5.89 us
    ppermute x3, waiting for transfers between devices, swap_far(): lax.ppermute(x, 'dom', [p for i in range(1, n - 1, 2) for p in ((i, i + 1...  5.55 us
  transfers between devices with their start and end apart: 9, of which 3 were waited for; matrix products, arithmetic and copies ran while one was open for 0% of the time, Pallas kernels for 9%

profile of v5, /device:TPU:7, one launch (start us, length us, event | category | flops | bytes accessed | tf_op | source)
XLA Modules:
  0.0 78.0 jit_solution(13175732319191038762)
XLA Ops:
  0.6 1.8 %shard_map.68 = f32[8,36,128]{2,1,0:T(8,128)} custom-call(f32[4]{0:T(128)} %refs_0_.1, f32[4,6,48,128]{3,2,1,0:T(8,128)} %orb.4), custom_call_target="tpu_custom_call" | custom-call | flops 2000000000 | bytes 2000000 | tf_op jit(solution)/shard_map/pallas_call | solution.py:35
  2.4 10.0 %all-to-all-start = ((f32[8,36,128]{2,1,0:T(8,128)}), f32[8,36,128]{2,1,0:T(8,128)S(1)}, u32[]{:S(2)}, u32[]{:S(2)}) async-start(f32[8,36,128]{2,1,0:T(8,128)} %shard_map.68), calls=%async_computation | async-start | bytes 327680 | tf_op jit(solution)/shard_map/all_to_all | solution.py:585
  12.5 2.2 %shard_map.69 = f32[7,6,48,128]{3,2,1,0:T(8,128)} custom-call(f32[4,6,48,128]{3,2,1,0:T(8,128)} %orb.4, f32[6,48,128]{2,1,0:T(8,128)} %field.2, f32[6,48,128]{2,1,0:T(8,128)} %diel.2, f32[6,48,128]{2,1,0:T(8,128)} %core.2), custom_call_target="tpu_custom_call" | custom-call | flops 20000000000 | bytes 20000000 | tf_op jit(solution)/shard_map/pallas_call | solution.py:35
  14.7 5.9 %all-to-all-done = f32[8,36,128]{2,1,0:T(8,128)S(1)} async-done(((f32[8,36,128]{2,1,0:T(8,128)}), f32[8,36,128]{2,1,0:T(8,128)S(1)}, u32[]{:S(2)}, u32[]{:S(2)}) %all-to-all-start) | async-done | bytes 147488 | tf_op jit(solution)/shard_map/all_to_all | solution.py:585
  20.6 7.5 %collective-permute-start.2 = (f32[36,128]{1,0:T(8,128)S(1)}, f32[36,128]{1,0:T(8,128)S(1)}, u32[]{:S(2)}, u32[]{:S(2)}) collective-permute-start(f32[36,128]{1,0:T(8,128)S(1)} %reduce_sum.9.mine), channel_id=1, source_target_pairs={{0,256},{32,288},{64,320},{96,352},{128,384},{160,416},{192,448},{... | collective-permute-start | bytes 55304 | tf_op jit(solution)/shard_map/ppermute | solution.py:588
  28.1 5.0 %collective-permute-start.1 = (f32[7,6,48,128]{3,2,1,0:T(8,128)}, f32[7,6,48,128]{3,2,1,0:T(8,128)S(1)}, u32[]{:S(2)}, u32[]{:S(2)}) collective-permute-start(f32[7,6,48,128]{3,2,1,0:T(8,128)} %shard_map.69), channel_id=1, source_target_pairs={{1,2},{2,1},{3,4},{4,3},{5,6},{6,5},{7,8},{8,7},{9,10},{10,9},{11,... | collective-permute-start | bytes 3096584 | tf_op jit(solution)/shard_map/ppermute | solution.py:565
  33.1 1.9 %collective-permute-start = (f32[7,6,48,128]{3,2,1,0:T(8,128)}, f32[7,6,48,128]{3,2,1,0:T(8,128)S(1)}, u32[]{:S(2)}, u32[]{:S(2)}) collective-permute-start(f32[7,6,48,128]{3,2,1,0:T(8,128)} %shard_map.69), channel_id=1, source_target_pairs={{0,1},{1,0},{2,3},{3,2},{4,5},{5,4},{6,7},{7,6},{8,9},{9,8},{10,11... | collective-permute-start | bytes 3096584 | tf_op jit(solution)/shard_map/ppermute | solution.py:570
  35.0 0.0 collective-permute-done.2.other
  35.0 0.7 shard_map.70
  35.7 3.4 %all-to-all-start.1 = ((f32[8,36,128]{2,1,0:T(8,128)}), f32[8,36,128]{2,1,0:T(8,128)S(1)}, u32[]{:S(2)}, u32[]{:S(2)}) async-start(f32[8,36,128]{2,1,0:T(8,128)} %shard_map.70), calls=%async_computation.1 | async-start | bytes 327680 | tf_op jit(solution)/shard_map/all_to_all | solution.py:590
  39.1 0.1 pad_add_fusion.refs_0_.sides.turn_in
  39.2 8.7 %all-to-all-done.1.refs_1_ = f32[8,36,128]{2,1,0:T(8,128)S(1)} async-done(((f32[8,36,128]{2,1,0:T(8,128)}), f32[8,36,128]{2,1,0:T(8,128)S(1)}, u32[]{:S(2)}, u32[]{:S(2)}) %all-to-all-start.1) | async-done | bytes 147488 | tf_op jit(solution)/shard_map/all_to_all | solution.py:590
  47.9 0.0 collective-permute-done.1.refs_3_.far
  47.9 0.0 collective-permute-done.refs_2_.near
  47.9 0.6 shard_map.71
  48.5 4.8 %collective-permute-start.3 = (f32[384,128]{1,0:T(8,128)S(1)}, f32[384,128]{1,0:T(8,128)S(1)}, u32[]{:S(2)}, u32[]{:S(2)}) collective-permute-start(f32[384,128]{1,0:T(8,128)S(1)} %get-tuple-element.32), channel_id=1, source_target_pairs={{1,2},{2,1},{3,4},{4,3},{5,6},{6,5},{7,8},{8,7},{9,10},{10,9},{11,... | collective-permute-start | bytes 589832 | tf_op jit(solution)/shard_map/ppermute | solution.py:565
  53.3 0.0 copy-start.1
  53.3 2.1 %collective-permute-start.4 = (f32[384,128]{1,0:T(8,128)S(1)}, f32[384,128]{1,0:T(8,128)S(1)}, u32[]{:S(2)}, u32[]{:S(2)}) collective-permute-start(f32[384,128]{1,0:T(8,128)S(1)} %get-tuple-element.31), channel_id=1, source_target_pairs={{0,1},{1,0},{2,3},{3,2},{4,5},{5,4},{6,7},{7,6},{8,9},{9,8},{10,11... | collective-permute-start | bytes 589832 | tf_op jit(solution)/shard_map/ppermute | solution.py:570
  55.4 0.0 copy-done
  55.4 0.0 copy-done.2
  55.4 0.0 copy-done.3
  55.4 2.4 %shard_map.72 = (f32[7,16,6,8,128]{4,3,2,1,0:T(8,128)S(1)}, f32[18,6,8,128]{3,2,1,0:T(8,128)S(1)}, f32[4,12,6,8,128]{4,3,2,1,0:T(8,128)S(1)}) custom-call(s32[2]{0:T(128)S(1)} %pad_add_fusion.refs_0_.sides.turn_in, f32[4,6,48,128]{3,2,1,0:T(8,128)S(1)} %copy-done, f32[6,48,128]{2,1,0:T(8,128)S(1)} %copy-done.3, f32[6,48,128]{2,1,0:T(8,128)S(1)} %copy-done.2, ...), custom_call_target="tpu_custom_call" | custom-call | flops 2000000000 | bytes 2000000 | tf_op jit(solution)/shard_map/pallas_call | solution.py:35
  57.8 0.0 collective-permute-done.3
  57.9 0.0 collective-permute-done.4
  57.9 0.0 copy-done.1
  57.9 3.9 %shard_map.73 = (f32[6,48,128]{2,1,0:T(8,128)}, f32[12,6,8,128]{3,2,1,0:T(8,128)S(1)}, f32[4,12,6,8,128]{4,3,2,1,0:T(8,128)S(1)}, f32[4,6,6,8,128]{4,3,2,1,0:T(8,128)S(1)}) custom-call(s32[2]{0:T(128)S(1)} %pad_add_fusion.refs_0_.sides.turn_in, f32[4,6,48,128]{3,2,1,0:T(8,128)S(1)} %copy-done, f32[6,48,128]{2,1,0:T(8,128)S(1)} %copy-done.1, ...), custom_call_target="tpu_custom_call" | custom-call | flops 2000000000 | bytes 2000000 | tf_op jit(solution)/shard_map/pallas_call | solution.py:35
  61.7 4.5 %collective-permute-start.6 = (f32[4,6,6,8,128]{4,3,2,1,0:T(8,128)S(1)}, f32[4,6,6,8,128]{4,3,2,1,0:T(8,128)S(1)}, u32[]{:S(2)}, u32[]{:S(2)}) collective-permute-start(f32[4,6,6,8,128]{4,3,2,1,0:T(8,128)S(1)} %get-tuple-element.38.y2), channel_id=1, source_target_pairs={{1,2},{2,1},{3,4},{4,3},{5,6},{6,5},{7,8},{8,7},{9,10},{10,9},{11,... | collective-permute-start | bytes 1769480 | tf_op jit(solution)/shard_map/ppermute | solution.py:565
  66.3 1.9 %collective-permute-start.5 = (f32[4,6,6,8,128]{4,3,2,1,0:T(8,128)S(1)}, f32[4,6,6,8,128]{4,3,2,1,0:T(8,128)S(1)}, u32[]{:S(2)}, u32[]{:S(2)}) collective-permute-start(f32[4,6,6,8,128]{4,3,2,1,0:T(8,128)S(1)} %get-tuple-element.38.y2), channel_id=1, source_target_pairs={{0,1},{1,0},{2,3},{3,2},{4,5},{5,4},{6,7},{7,6},{8,9},{9,8},{10,11... | collective-permute-start | bytes 1769480 | tf_op jit(solution)/shard_map/ppermute | solution.py:570
  68.2 1.3 %shard_map.74.partial = f32[4,6,6,8,128]{4,3,2,1,0:T(8,128)S(1)} custom-call(f32[4,12,6,8,128]{4,3,2,1,0:T(8,128)S(1)} %get-tuple-element.37.y1, f32[4,6,6,8,128]{4,3,2,1,0:T(8,128)S(1)} %get-tuple-element.38.y2, f32[12,6,8,128]{3,2,1,0:T(8,128)S(1)} %get-tuple-element.39.diag, s32[2]{0:T(128)S(1)} %pad_add_fusion.refs_0_.sides.turn_in), custom_call_target="tpu_custom_call" | custom-call | flops 2000000000 | bytes 2000000 | tf_op jit(solution)/shard_map/pallas_call | solution.py:35
  69.5 5.5 %collective-permute-done.6.far = f32[4,6,6,8,128]{4,3,2,1,0:T(8,128)S(1)} collective-permute-done((f32[4,6,6,8,128]{4,3,2,1,0:T(8,128)S(1)}, f32[4,6,6,8,128]{4,3,2,1,0:T(8,128)S(1)}, u32[]{:S(2)}, u32[]{:S(2)}) %collective-permute-start.6) | collective-permute-done | bytes 589856 | tf_op jit(solution)/shard_map/ppermute | solution.py:565
  75.0 0.0 collective-permute-done.5.near
  75.0 3.0 %shard_map.75 = f32[4,6,48,128]{3,2,1,0:T(8,128)} custom-call(s32[2]{0:T(128)S(1)} %pad_add_fusion.refs_0_.sides.turn_in, f32[4,12,6,8,128]{4,3,2,1,0:T(8,128)S(1)} %get-tuple-element.37.y1, f32[4,6,6,8,128]{4,3,2,1,0:T(8,128)S(1)} %get-tuple-element.38.y2, f32[4,6,6,8,128]{4,3,2,1,0:T(8,128)S(1)} %collective-permute-done.5.near, ...), custom_call_target="tpu_custom_call" | custom-call | flops 2000000000 | bytes 2000000 | tf_op jit(solution)/shard_map/pallas_call | solution.py:35
  (4 shorter events, 0.0 us)
Async XLA Ops:
  2.4 18.2 %all-to-all-start = ((f32[8,36,128]{2,1,0:T(8,128)}), f32[8,36,128]{2,1,0:T(8,128)S(1)}, u32[]{:S(2)}, u32[]{:S(2)}) async-start(f32[8,36,128]{2,1,0:T(8,128)} %shard_map.68), calls=%async_computation | async-start | bytes 327680 | tf_op jit(solution)/shard_map/all_to_all | solution.py:585
  20.6 14.4 %collective-permute-start.2 = (f32[36,128]{1,0:T(8,128)S(1)}, f32[36,128]{1,0:T(8,128)S(1)}, u32[]{:S(2)}, u32[]{:S(2)}) collective-permute-start(f32[36,128]{1,0:T(8,128)S(1)} %reduce_sum.9.mine), channel_id=1, source_target_pairs={{0,256},{32,288},{64,320},{96,352},{128,384},{160,416},{192,448},{... | collective-permute-start | bytes 55304 | tf_op jit(solution)/shard_map/ppermute | solution.py:588
  28.1 19.8 %collective-permute-start.1 = (f32[7,6,48,128]{3,2,1,0:T(8,128)}, f32[7,6,48,128]{3,2,1,0:T(8,128)S(1)}, u32[]{:S(2)}, u32[]{:S(2)}) collective-permute-start(f32[7,6,48,128]{3,2,1,0:T(8,128)} %shard_map.69), channel_id=1, source_target_pairs={{1,2},{2,1},{3,4},{4,3},{5,6},{6,5},{7,8},{8,7},{9,10},{10,9},{11,... | collective-permute-start | bytes 3096584 | tf_op jit(solution)/shard_map/ppermute | solution.py:565
  33.1 14.8 %collective-permute-start = (f32[7,6,48,128]{3,2,1,0:T(8,128)}, f32[7,6,48,128]{3,2,1,0:T(8,128)S(1)}, u32[]{:S(2)}, u32[]{:S(2)}) collective-permute-start(f32[7,6,48,128]{3,2,1,0:T(8,128)} %shard_map.69), channel_id=1, source_target_pairs={{0,1},{1,0},{2,3},{3,2},{4,5},{5,4},{6,7},{7,6},{8,9},{9,8},{10,11... | collective-permute-start | bytes 3096584 | tf_op jit(solution)/shard_map/ppermute | solution.py:570
  35.7 12.2 %all-to-all-start.1 = ((f32[8,36,128]{2,1,0:T(8,128)}), f32[8,36,128]{2,1,0:T(8,128)S(1)}, u32[]{:S(2)}, u32[]{:S(2)}) async-start(f32[8,36,128]{2,1,0:T(8,128)} %shard_map.70), calls=%async_computation.1 | async-start | bytes 327680 | tf_op jit(solution)/shard_map/all_to_all | solution.py:590
  39.2 16.2 %copy-start = (f32[4,6,48,128]{3,2,1,0:T(8,128)S(1)}, f32[4,6,48,128]{3,2,1,0:T(8,128)}, u32[]{:S(2)}) copy-start(f32[4,6,48,128]{3,2,1,0:T(8,128)} %orb.4) | copy-start | bytes 1769476
  39.2 16.2 %copy-start.2 = (f32[6,48,128]{2,1,0:T(8,128)S(1)}, f32[6,48,128]{2,1,0:T(8,128)}, u32[]{:S(2)}) copy-start(f32[6,48,128]{2,1,0:T(8,128)} %field.2) | copy-start | bytes 442372
  39.2 16.2 %copy-start.3 = (f32[6,48,128]{2,1,0:T(8,128)S(1)}, f32[6,48,128]{2,1,0:T(8,128)}, u32[]{:S(2)}) copy-start(f32[6,48,128]{2,1,0:T(8,128)} %diel.2) | copy-start | bytes 442372
  48.5 9.4 %collective-permute-start.3 = (f32[384,128]{1,0:T(8,128)S(1)}, f32[384,128]{1,0:T(8,128)S(1)}, u32[]{:S(2)}, u32[]{:S(2)}) collective-permute-start(f32[384,128]{1,0:T(8,128)S(1)} %get-tuple-element.32), channel_id=1, source_target_pairs={{1,2},{2,1},{3,4},{4,3},{5,6},{6,5},{7,8},{8,7},{9,10},{10,9},{11,... | collective-permute-start | bytes 589832 | tf_op jit(solution)/shard_map/ppermute | solution.py:565
  53.3 4.6 %copy-start.1 = (f32[6,48,128]{2,1,0:T(8,128)S(1)}, f32[6,48,128]{2,1,0:T(8,128)}, u32[]{:S(2)}) copy-start(f32[6,48,128]{2,1,0:T(8,128)} %core.2) | copy-start | bytes 442372
  53.3 4.6 %collective-permute-start.4 = (f32[384,128]{1,0:T(8,128)S(1)}, f32[384,128]{1,0:T(8,128)S(1)}, u32[]{:S(2)}, u32[]{:S(2)}) collective-permute-start(f32[384,128]{1,0:T(8,128)S(1)} %get-tuple-element.31), channel_id=1, source_target_pairs={{0,1},{1,0},{2,3},{3,2},{4,5},{5,4},{6,7},{7,6},{8,9},{9,8},{10,11... | collective-permute-start | bytes 589832 | tf_op jit(solution)/shard_map/ppermute | solution.py:570
  61.7 13.3 %collective-permute-start.6 = (f32[4,6,6,8,128]{4,3,2,1,0:T(8,128)S(1)}, f32[4,6,6,8,128]{4,3,2,1,0:T(8,128)S(1)}, u32[]{:S(2)}, u32[]{:S(2)}) collective-permute-start(f32[4,6,6,8,128]{4,3,2,1,0:T(8,128)S(1)} %get-tuple-element.38.y2), channel_id=1, source_target_pairs={{1,2},{2,1},{3,4},{4,3},{5,6},{6,5},{7,8},{8,7},{9,10},{10,9},{11,... | collective-permute-start | bytes 1769480 | tf_op jit(solution)/shard_map/ppermute | solution.py:565
  66.3 8.8 %collective-permute-start.5 = (f32[4,6,6,8,128]{4,3,2,1,0:T(8,128)S(1)}, f32[4,6,6,8,128]{4,3,2,1,0:T(8,128)S(1)}, u32[]{:S(2)}, u32[]{:S(2)}) collective-permute-start(f32[4,6,6,8,128]{4,3,2,1,0:T(8,128)S(1)} %get-tuple-element.38.y2), channel_id=1, source_target_pairs={{0,1},{1,0},{2,3},{3,2},{4,5},{5,4},{6,7},{7,6},{8,9},{9,8},{10,11... | collective-permute-start | bytes 1769480 | tf_op jit(solution)/shard_map/ppermute | solution.py:570

commit v6 on v5

--- a/solution.py
+++ b/solution.py
@@ -580,7 +580,9 @@
     sides = jnp.stack([has_far.astype(jnp.int32), turn.astype(jnp.int32)])
 
     parts = density(half, occupation, orbitals)
-    held, parts = lax.optimization_barrier(((orbitals, start_field, dielectric, core_density), parts))
+    held, parts, sides = lax.optimization_barrier(
+        ((orbitals, start_field, dielectric, core_density), parts, sides)
+    )
     packed = pack(*held)
     parts = lax.all_to_all(parts, "band", 0, 0, axis_index_groups=groups)
     mine = jnp.sum(parts, axis=0)

time: 79.4 us -> 77.9 us (0.981)
  blocking collectives: 0 us -> 11.3 us
  waiting for transfers between devices: 20.2 us -> 11.5 us
  starting transfers between devices: 41 us -> 37.8 us
  Pallas kernels: 15.8 us -> 15 us
    all_to_all x0 -> x1, blocking collectives: none -> 11.3 us  [local(): lax.all_to_all(spread(half, mine, other), 'band', 0, 0, axis_index_groups...]
    all_to_all x1 -> x0, waiting for transfers between devices: 8.73 us -> none  [local(): lax.all_to_all(spread(half, mine, other), 'band', 0, 0, axis_index_groups...]
    all_to_all x1 -> x0, starting transfers between devices: 3.38 us -> none  [local(): lax.all_to_all(spread(half, mine, other), 'band', 0, 0, axis_index_groups...]
  transfers between devices with their start and end apart: 9 -> 8, of which waited for: 3 -> 2; matrix products, arithmetic and copies ran while one was open for 0% -> 0% of each run, Pallas kernels for 9% -> 8%
where the time goes in v6:
time: 77.9 us; the launch traced here: 76.6 us
  starting transfers between devices  37.8 us (49%)
  Pallas kernels  15 us (19%)
  waiting for transfers between devices  11.5 us (15%)
  blocking collectives  11.3 us (15%)
  between operations  0.84 us (1%)
    pallas_call x8, Pallas kernels, call(): pl.pallas_call(kernel, out_shape=[jax.ShapeDtypeStruct(s, jnp.float32) fo...  15 us
    ppermute x3, starting transfers between devices, swap_far(): lax.ppermute(x, 'dom', [p for i in range(1, n - 1, 2) for p in ((i, i + 1...  14.4 us
    all_to_all x1, blocking collectives, local(): lax.all_to_all(spread(half, mine, other), 'band', 0, 0, axis_index_groups...  11.3 us
    all_to_all x1, starting transfers between devices, local(): parts = lax.all_to_all(parts, 'band', 0, 0, axis_index_groups=groups)  10 us
    ppermute x1, starting transfers between devices, local(): lax.ppermute(mine, 'band', [(i, (i + half) % bands) for i in range(bands)])  7.45 us
    all_to_all x1, waiting for transfers between devices, local(): parts = lax.all_to_all(parts, 'band', 0, 0, axis_index_groups=groups)  5.95 us
    ppermute x3, starting transfers between devices, swap_near(): lax.ppermute(x, 'dom', [p for i in range(0, n - 1, 2) for p in ((i, i + 1...  5.89 us
    ppermute x3, waiting for transfers between devices, swap_far(): lax.ppermute(x, 'dom', [p for i in range(1, n - 1, 2) for p in ((i, i + 1...  5.57 us
  transfers between devices with their start and end apart: 8, of which 2 were waited for; matrix products, arithmetic and copies ran while one was open for 0% of the time, Pallas kernels for 8%

profile of v6, /device:TPU:7, one launch (start us, length us, event | category | flops | bytes accessed | tf_op | source)
XLA Modules:
  0.0 76.6 jit_solution(17734494979321865096)
XLA Ops:
  0.6 0.1 pad_add_fusion.refs_0_.sides.turn_in
  0.7 1.8 %shard_map.68 = f32[8,36,128]{2,1,0:T(8,128)} custom-call(f32[4]{0:T(128)} %refs_0_.1, f32[4,6,48,128]{3,2,1,0:T(8,128)} %orb.4), custom_call_target="tpu_custom_call" | custom-call | flops 2000000000 | bytes 2000000 | tf_op jit(solution)/shard_map/pallas_call | solution.py:35
  2.5 10.0 %all-to-all-start = ((f32[8,36,128]{2,1,0:T(8,128)}), f32[8,36,128]{2,1,0:T(8,128)S(1)}, u32[]{:S(2)}, u32[]{:S(2)}) async-start(f32[8,36,128]{2,1,0:T(8,128)} %shard_map.68), calls=%async_computation | async-start | bytes 327680 | tf_op jit(solution)/shard_map/all_to_all | solution.py:587
  12.5 2.2 %shard_map.69 = f32[7,6,48,128]{3,2,1,0:T(8,128)} custom-call(f32[4,6,48,128]{3,2,1,0:T(8,128)} %orb.4, f32[6,48,128]{2,1,0:T(8,128)} %field.2, f32[6,48,128]{2,1,0:T(8,128)} %diel.2, f32[6,48,128]{2,1,0:T(8,128)} %core.2), custom_call_target="tpu_custom_call" | custom-call | flops 20000000000 | bytes 20000000 | tf_op jit(solution)/shard_map/pallas_call | solution.py:35
  14.7 6.0 %all-to-all-done = f32[8,36,128]{2,1,0:T(8,128)S(1)} async-done(((f32[8,36,128]{2,1,0:T(8,128)}), f32[8,36,128]{2,1,0:T(8,128)S(1)}, u32[]{:S(2)}, u32[]{:S(2)}) %all-to-all-start) | async-done | bytes 147488 | tf_op jit(solution)/shard_map/all_to_all | solution.py:587
  20.7 7.5 %collective-permute-start.2 = (f32[36,128]{1,0:T(8,128)S(1)}, f32[36,128]{1,0:T(8,128)S(1)}, u32[]{:S(2)}, u32[]{:S(2)}) collective-permute-start(f32[36,128]{1,0:T(8,128)S(1)} %reduce_sum.9.mine), channel_id=1, source_target_pairs={{0,256},{32,288},{64,320},{96,352},{128,384},{160,416},{192,448},{... | collective-permute-start | bytes 55304 | tf_op jit(solution)/shard_map/ppermute | solution.py:590
  28.2 5.0 %collective-permute-start.1 = (f32[7,6,48,128]{3,2,1,0:T(8,128)}, f32[7,6,48,128]{3,2,1,0:T(8,128)S(1)}, u32[]{:S(2)}, u32[]{:S(2)}) collective-permute-start(f32[7,6,48,128]{3,2,1,0:T(8,128)} %shard_map.69), channel_id=1, source_target_pairs={{1,2},{2,1},{3,4},{4,3},{5,6},{6,5},{7,8},{8,7},{9,10},{10,9},{11,... | collective-permute-start | bytes 3096584 | tf_op jit(solution)/shard_map/ppermute | solution.py:565
  33.1 1.9 %collective-permute-start = (f32[7,6,48,128]{3,2,1,0:T(8,128)}, f32[7,6,48,128]{3,2,1,0:T(8,128)S(1)}, u32[]{:S(2)}, u32[]{:S(2)}) collective-permute-start(f32[7,6,48,128]{3,2,1,0:T(8,128)} %shard_map.69), channel_id=1, source_target_pairs={{0,1},{1,0},{2,3},{3,2},{4,5},{5,4},{6,7},{7,6},{8,9},{9,8},{10,11... | collective-permute-start | bytes 3096584 | tf_op jit(solution)/shard_map/ppermute | solution.py:570
  35.1 0.0 collective-permute-done.2.other
  35.1 11.3 %all_to_all.10.refs_1_ = f32[8,36,128]{2,1,0:T(8,128)S(1)} all-to-all(f32[8,36,128]{2,1,0:T(8,128)S(1)} %shard_map.70), channel_id=1, replica_groups={{0,32,64,96,128,160,192,224},{256,288,320,352,384,416,448,480},{1,33,65..., dimensions={0} | all-to-all | bytes 294912 | tf_op jit(solution)/shard_map/all_to_all | solution.py:592
  46.4 0.0 copy-start
  46.4 0.0 copy-start.2
  46.4 0.0 collective-permute-done.1.refs_3_.far
  46.4 0.0 collective-permute-done.refs_2_.near
  46.5 0.6 shard_map.71
  47.0 4.9 %collective-permute-start.3 = (f32[384,128]{1,0:T(8,128)S(1)}, f32[384,128]{1,0:T(8,128)S(1)}, u32[]{:S(2)}, u32[]{:S(2)}) collective-permute-start(f32[384,128]{1,0:T(8,128)S(1)} %get-tuple-element.34), channel_id=1, source_target_pairs={{1,2},{2,1},{3,4},{4,3},{5,6},{6,5},{7,8},{8,7},{9,10},{10,9},{11,... | collective-permute-start | bytes 589832 | tf_op jit(solution)/shard_map/ppermute | solution.py:565
  52.0 0.0 copy-start.1
  52.0 2.1 %collective-permute-start.4 = (f32[384,128]{1,0:T(8,128)S(1)}, f32[384,128]{1,0:T(8,128)S(1)}, u32[]{:S(2)}, u32[]{:S(2)}) collective-permute-start(f32[384,128]{1,0:T(8,128)S(1)} %get-tuple-element.33), channel_id=1, source_target_pairs={{0,1},{1,0},{2,3},{3,2},{4,5},{5,4},{6,7},{7,6},{8,9},{9,8},{10,11... | collective-permute-start | bytes 589832 | tf_op jit(solution)/shard_map/ppermute | solution.py:570
  54.1 0.0 copy-done
  54.1 0.0 copy-done.2
  54.1 0.0 copy-done.3
  54.1 2.4 %shard_map.72 = (f32[7,16,6,8,128]{4,3,2,1,0:T(8,128)S(1)}, f32[18,6,8,128]{3,2,1,0:T(8,128)S(1)}, f32[4,12,6,8,128]{4,3,2,1,0:T(8,128)S(1)}) custom-call(s32[2]{0:T(128)S(1)} %pad_add_fusion.refs_0_.sides.turn_in, f32[4,6,48,128]{3,2,1,0:T(8,128)S(1)} %copy-done, f32[6,48,128]{2,1,0:T(8,128)S(1)} %copy-done.3, f32[6,48,128]{2,1,0:T(8,128)S(1)} %copy-done.2, ...), custom_call_target="tpu_custom_call" | custom-call | flops 2000000000 | bytes 2000000 | tf_op jit(solution)/shard_map/pallas_call | solution.py:35
  56.5 0.0 collective-permute-done.3
  56.6 0.0 collective-permute-done.4
  56.6 0.0 copy-done.1
  56.6 3.8 %shard_map.73 = (f32[6,48,128]{2,1,0:T(8,128)}, f32[12,6,8,128]{3,2,1,0:T(8,128)S(1)}, f32[4,12,6,8,128]{4,3,2,1,0:T(8,128)S(1)}, f32[4,6,6,8,128]{4,3,2,1,0:T(8,128)S(1)}) custom-call(s32[2]{0:T(128)S(1)} %pad_add_fusion.refs_0_.sides.turn_in, f32[4,6,48,128]{3,2,1,0:T(8,128)S(1)} %copy-done, f32[6,48,128]{2,1,0:T(8,128)S(1)} %copy-done.1, ...), custom_call_target="tpu_custom_call" | custom-call | flops 2000000000 | bytes 2000000 | tf_op jit(solution)/shard_map/pallas_call | solution.py:35
  60.3 4.5 %collective-permute-start.6 = (f32[4,6,6,8,128]{4,3,2,1,0:T(8,128)S(1)}, f32[4,6,6,8,128]{4,3,2,1,0:T(8,128)S(1)}, u32[]{:S(2)}, u32[]{:S(2)}) collective-permute-start(f32[4,6,6,8,128]{4,3,2,1,0:T(8,128)S(1)} %get-tuple-element.40.y2), channel_id=1, source_target_pairs={{1,2},{2,1},{3,4},{4,3},{5,6},{6,5},{7,8},{8,7},{9,10},{10,9},{11,... | collective-permute-start | bytes 1769480 | tf_op jit(solution)/shard_map/ppermute | solution.py:565
  64.8 1.9 %collective-permute-start.5 = (f32[4,6,6,8,128]{4,3,2,1,0:T(8,128)S(1)}, f32[4,6,6,8,128]{4,3,2,1,0:T(8,128)S(1)}, u32[]{:S(2)}, u32[]{:S(2)}) collective-permute-start(f32[4,6,6,8,128]{4,3,2,1,0:T(8,128)S(1)} %get-tuple-element.40.y2), channel_id=1, source_target_pairs={{0,1},{1,0},{2,3},{3,2},{4,5},{5,4},{6,7},{7,6},{8,9},{9,8},{10,11... | collective-permute-start | bytes 1769480 | tf_op jit(solution)/shard_map/ppermute | solution.py:570
  66.8 1.3 %shard_map.74.partial = f32[4,6,6,8,128]{4,3,2,1,0:T(8,128)S(1)} custom-call(f32[4,12,6,8,128]{4,3,2,1,0:T(8,128)S(1)} %get-tuple-element.39.y1, f32[4,6,6,8,128]{4,3,2,1,0:T(8,128)S(1)} %get-tuple-element.40.y2, f32[12,6,8,128]{3,2,1,0:T(8,128)S(1)} %get-tuple-element.41.diag, s32[2]{0:T(128)S(1)} %pad_add_fusion.refs_0_.sides.turn_in), custom_call_target="tpu_custom_call" | custom-call | flops 2000000000 | bytes 2000000 | tf_op jit(solution)/shard_map/pallas_call | solution.py:35
  68.1 5.6 %collective-permute-done.6.far = f32[4,6,6,8,128]{4,3,2,1,0:T(8,128)S(1)} collective-permute-done((f32[4,6,6,8,128]{4,3,2,1,0:T(8,128)S(1)}, f32[4,6,6,8,128]{4,3,2,1,0:T(8,128)S(1)}, u32[]{:S(2)}, u32[]{:S(2)}) %collective-permute-start.6) | collective-permute-done | bytes 589856 | tf_op jit(solution)/shard_map/ppermute | solution.py:565
  73.7 0.0 collective-permute-done.5.near
  73.7 3.0 %shard_map.75 = f32[4,6,48,128]{3,2,1,0:T(8,128)} custom-call(s32[2]{0:T(128)S(1)} %pad_add_fusion.refs_0_.sides.turn_in, f32[4,12,6,8,128]{4,3,2,1,0:T(8,128)S(1)} %get-tuple-element.39.y1, f32[4,6,6,8,128]{4,3,2,1,0:T(8,128)S(1)} %get-tuple-element.40.y2, f32[4,6,6,8,128]{4,3,2,1,0:T(8,128)S(1)} %collective-permute-done.5.near, ...), custom_call_target="tpu_custom_call" | custom-call | flops 2000000000 | bytes 2000000 | tf_op jit(solution)/shard_map/pallas_call | solution.py:35
  (3 shorter events, 0.0 us)
Async XLA Ops:
  2.5 18.2 %all-to-all-start = ((f32[8,36,128]{2,1,0:T(8,128)}), f32[8,36,128]{2,1,0:T(8,128)S(1)}, u32[]{:S(2)}, u32[]{:S(2)}) async-start(f32[8,36,128]{2,1,0:T(8,128)} %shard_map.68), calls=%async_computation | async-start | bytes 327680 | tf_op jit(solution)/shard_map/all_to_all | solution.py:587
  20.7 14.4 %collective-permute-start.2 = (f32[36,128]{1,0:T(8,128)S(1)}, f32[36,128]{1,0:T(8,128)S(1)}, u32[]{:S(2)}, u32[]{:S(2)}) collective-permute-start(f32[36,128]{1,0:T(8,128)S(1)} %reduce_sum.9.mine), channel_id=1, source_target_pairs={{0,256},{32,288},{64,320},{96,352},{128,384},{160,416},{192,448},{... | collective-permute-start | bytes 55304 | tf_op jit(solution)/shard_map/ppermute | solution.py:590
  28.2 18.3 %collective-permute-start.1 = (f32[7,6,48,128]{3,2,1,0:T(8,128)}, f32[7,6,48,128]{3,2,1,0:T(8,128)S(1)}, u32[]{:S(2)}, u32[]{:S(2)}) collective-permute-start(f32[7,6,48,128]{3,2,1,0:T(8,128)} %shard_map.69), channel_id=1, source_target_pairs={{1,2},{2,1},{3,4},{4,3},{5,6},{6,5},{7,8},{8,7},{9,10},{10,9},{11,... | collective-permute-start | bytes 3096584 | tf_op jit(solution)/shard_map/ppermute | solution.py:565
  33.1 13.3 %collective-permute-start = (f32[7,6,48,128]{3,2,1,0:T(8,128)}, f32[7,6,48,128]{3,2,1,0:T(8,128)S(1)}, u32[]{:S(2)}, u32[]{:S(2)}) collective-permute-start(f32[7,6,48,128]{3,2,1,0:T(8,128)} %shard_map.69), channel_id=1, source_target_pairs={{0,1},{1,0},{2,3},{3,2},{4,5},{5,4},{6,7},{7,6},{8,9},{9,8},{10,11... | collective-permute-start | bytes 3096584 | tf_op jit(solution)/shard_map/ppermute | solution.py:570
  46.4 7.6 %copy-start = (f32[4,6,48,128]{3,2,1,0:T(8,128)S(1)}, f32[4,6,48,128]{3,2,1,0:T(8,128)}, u32[]{:S(2)}) copy-start(f32[4,6,48,128]{3,2,1,0:T(8,128)} %orb.4) | copy-start | bytes 1769476
  46.4 7.6 %copy-start.2 = (f32[6,48,128]{2,1,0:T(8,128)S(1)}, f32[6,48,128]{2,1,0:T(8,128)}, u32[]{:S(2)}) copy-start(f32[6,48,128]{2,1,0:T(8,128)} %field.2) | copy-start | bytes 442372
  46.4 7.6 %copy-start.3 = (f32[6,48,128]{2,1,0:T(8,128)S(1)}, f32[6,48,128]{2,1,0:T(8,128)}, u32[]{:S(2)}) copy-start(f32[6,48,128]{2,1,0:T(8,128)} %diel.2) | copy-start | bytes 442372
  47.0 9.5 %collective-permute-start.3 = (f32[384,128]{1,0:T(8,128)S(1)}, f32[384,128]{1,0:T(8,128)S(1)}, u32[]{:S(2)}, u32[]{:S(2)}) collective-permute-start(f32[384,128]{1,0:T(8,128)S(1)} %get-tuple-element.34), channel_id=1, source_target_pairs={{1,2},{2,1},{3,4},{4,3},{5,6},{6,5},{7,8},{8,7},{9,10},{10,9},{11,... | collective-permute-start | bytes 589832 | tf_op jit(solution)/shard_map/ppermute | solution.py:565
  52.0 4.6 %copy-start.1 = (f32[6,48,128]{2,1,0:T(8,128)S(1)}, f32[6,48,128]{2,1,0:T(8,128)}, u32[]{:S(2)}) copy-start(f32[6,48,128]{2,1,0:T(8,128)} %core.2) | copy-start | bytes 442372
  52.0 4.6 %collective-permute-start.4 = (f32[384,128]{1,0:T(8,128)S(1)}, f32[384,128]{1,0:T(8,128)S(1)}, u32[]{:S(2)}, u32[]{:S(2)}) collective-permute-start(f32[384,128]{1,0:T(8,128)S(1)} %get-tuple-element.33), channel_id=1, source_target_pairs={{0,1},{1,0},{2,3},{3,2},{4,5},{5,4},{6,7},{7,6},{8,9},{9,8},{10,11... | collective-permute-start | bytes 589832 | tf_op jit(solution)/shard_map/ppermute | solution.py:570
  60.3 13.3 %collective-permute-start.6 = (f32[4,6,6,8,128]{4,3,2,1,0:T(8,128)S(1)}, f32[4,6,6,8,128]{4,3,2,1,0:T(8,128)S(1)}, u32[]{:S(2)}, u32[]{:S(2)}) collective-permute-start(f32[4,6,6,8,128]{4,3,2,1,0:T(8,128)S(1)} %get-tuple-element.40.y2), channel_id=1, source_target_pairs={{1,2},{2,1},{3,4},{4,3},{5,6},{6,5},{7,8},{8,7},{9,10},{10,9},{11,... | collective-permute-start | bytes 1769480 | tf_op jit(solution)/shard_map/ppermute | solution.py:565
  64.8 8.8 %collective-permute-start.5 = (f32[4,6,6,8,128]{4,3,2,1,0:T(8,128)S(1)}, f32[4,6,6,8,128]{4,3,2,1,0:T(8,128)S(1)}, u32[]{:S(2)}, u32[]{:S(2)}) collective-permute-start(f32[4,6,6,8,128]{4,3,2,1,0:T(8,128)S(1)} %get-tuple-element.40.y2), channel_id=1, source_target_pairs={{0,1},{1,0},{2,3},{3,2},{4,5},{5,4},{6,7},{7,6},{8,9},{9,8},{10,11... | collective-permute-start | bytes 1769480 | tf_op jit(solution)/shard_map/ppermute | solution.py:570
